TPU v7x, 32 devices: a whole 2x2x4 slice. The times are simulated.
32 devices in a mesh: dp: 8 (over z, y), blk: 4 (over x, core).
Axes of the slice: x: 2, y: 2, z: 4, core: 2. Of those that a mesh axis runs over, the one named last changes fastest.
Arguments:
- tokens: bfloat16 [2, 16, 256, 512], P(None, 'dp', 'blk'), may hold values from -6 to 6
- mask_flags: int32 [2, 16, 256], P(None, 'dp', 'blk'), may hold values 0 or 1
- buckets: int32 [2, 8], P(None, 'dp'), may hold values from 0 to 2
- cotangent: bfloat16 [2, 16, 256, 512], P(None, 'dp', 'blk'), may hold values from -6 to 6
- mask_token: bfloat16 [512], replicated, may hold values from -5 to 5
- norm1_gain: bfloat16 [512], replicated, may hold values from 0.5 to 1.5
- norm1_bias: bfloat16 [512], replicated, may hold values from -1.5 to 1.5
- w_qkv: bfloat16 [512, 1536], replicated, may hold values from -0.25 to 0.25
- b_query: bfloat16 [512], replicated, may hold values from -1.5 to 1.5
- b_value: bfloat16 [512], replicated, may hold values from -1.5 to 1.5
- w_out: bfloat16 [512, 512], replicated, may hold values from -1 to 1
- b_out: bfloat16 [512], replicated, may hold values from -1.5 to 1.5
- norm2_gain: bfloat16 [512], replicated, may hold values from 0.5 to 1.5
- norm2_bias: bfloat16 [512], replicated, may hold values from -1.5 to 1.5
- w_up: bfloat16 [512, 2048], replicated, may hold values from -0.25 to 0.25
- b_up: bfloat16 [2048], replicated, may hold values from -1.5 to 1.5
- w_down: bfloat16 [2048, 512], replicated, may hold values from -0.125 to 0.125
- b_down: bfloat16 [512], replicated, may hold values from -1.5 to 1.5
Outputs:
- block_out: bfloat16 [2, 16, 256, 512], P(None, 'dp', 'blk')
- token_grad: float32 [2, 16, 256, 512], P(None, 'dp', 'blk')
- grad_mask_token: float32 [512], replicated
- grad_norm1_gain: float32 [512], replicated
- grad_norm1_bias: float32 [512], replicated
- grad_w_qkv: float32 [512, 1536], replicated
- grad_b_query: float32 [512], replicated
- grad_b_value: float32 [512], replicated
- grad_w_out: float32 [512, 512], replicated
- grad_b_out: float32 [512], replicated
- grad_norm2_gain: float32 [512], replicated
- grad_norm2_bias: float32 [512], replicated
- grad_w_up: float32 [512, 2048], replicated
- grad_b_up: float32 [2048], replicated
- grad_w_down: float32 [2048, 512], replicated
- grad_b_down: float32 [512], replicated
Inputs may be any that keep to these rules, and one draw needn't show every extreme that they name: `buckets`: all images that one index of dp holds in one micro-batch share this bucket: 0, 1, 2 stand for 100, 196, 256 patches; every image's patches are split evenly over the 4 devices of blk, each device's share in the first rows of its 64 slots, the rest padding.
All inputs are finite; a program needn't handle non-finite values. No bound on the sum of `mask_flags` on one device may be relied on, other than what follows from the above.
Results may differ from a plain program's by a relative error of at most 0.02.
Values may be sent and summed in bfloat16 or wider, within the bound.
No kernel may reach another device: no remote copies, remote signals or barrier semaphores. Data moves between devices by JAX's collectives and lax.ppermute only.
A program may use at most 128 MiB of HBM per device.

v0:
```python
import jax
import jax.numpy as jnp
from jax import lax
from jax.sharding import PartitionSpec as P

HEADS = 16


def layer_norm(inputs, norm_gain, norm_shift):
    centre = jnp.mean(inputs, axis=-1, keepdims=True)
    centred = inputs - centre
    spread = jnp.mean(centred * centred, axis=-1, keepdims=True)
    return centred * lax.rsqrt(spread + 1e-06) * norm_gain + norm_shift


def gelu_exact(inputs):
    return jax.nn.gelu(inputs, approximate=False)


def row_quota(bucket):
    return jnp.where(bucket == 0, 25, jnp.where(bucket == 1, 49, 64)).astype(jnp.int32)


def rows_dot(lhs_rows, rhs_rows):
    return jnp.einsum("rk,rn->kn", lhs_rows, rhs_rows, preferred_element_type=jnp.float32)


def back_dot(grad_rows, weight):
    return jnp.einsum("rn,kn->rk", grad_rows, weight, preferred_element_type=jnp.float32)


def shards(
    tokens,
    mask_flags,
    buckets,
    cotangent,
    mask_token,
    norm1_gain,
    norm1_bias,
    w_qkv,
    b_query,
    b_value,
    w_out,
    b_out,
    norm2_gain,
    norm2_bias,
    w_up,
    b_up,
    w_down,
    b_down,
):
    micro_count, images, share, width = tokens.shape
    head_size = width // HEADS
    scale_factor = head_size ** (-0.5)
    mask_vec = mask_token.astype(jnp.float32)
    gain_one = norm1_gain.astype(jnp.float32)
    shift_one = norm1_bias.astype(jnp.float32)
    gain_two = norm2_gain.astype(jnp.float32)
    shift_two = norm2_bias.astype(jnp.float32)
    bias_after = b_out.astype(jnp.float32)
    bias_expand = b_up.astype(jnp.float32)
    bias_reduce = b_down.astype(jnp.float32)
    qkv_bias = jnp.concatenate(
        [b_query.astype(jnp.float32), jnp.zeros((width,), jnp.float32), b_value.astype(jnp.float32)]
    )
    batches = []
    outputs = []
    token_grads = []
    row_count = images * share
    for which in range(micro_count):
        limit = row_quota(buckets[which, 0])
        row_live = jnp.arange(share, dtype=jnp.int32) < limit
        live_rows = jnp.broadcast_to(row_live[None, :], (images, share)).reshape(row_count)
        flag_rows = (mask_flags[which] == 1).reshape(row_count)
        tok_rows = tokens[which].astype(jnp.float32).reshape(row_count, width)
        flat_rows = jnp.where(flag_rows[:, None], mask_vec[None, :], tok_rows)
        grad_out = cotangent[which].astype(jnp.float32).reshape(row_count, width) * live_rows[
            :, None
        ].astype(jnp.float32)
        layer_row_count = images * share
        normed_f, norm_one_back = jax.vjp(layer_norm, flat_rows, gain_one, shift_one)
        normed_one = normed_f.astype(jnp.bfloat16)
        projected = (
            jnp.dot(normed_one, w_qkv, preferred_element_type=jnp.float32) + qkv_bias
        ).astype(jnp.bfloat16)
        queries = projected[:, :width].reshape(images, share, HEADS, head_size)
        key_rows = projected[:, width : 2 * width].reshape(images, share, width)
        value_rows = projected[:, 2 * width :].reshape(images, share, width)

        def scores_for(key_piece):
            key_count = key_piece.shape[1]
            key_heads = key_piece.reshape(images, key_count, HEADS, head_size)
            raw_scores = (
                jnp.einsum(
                    "iqhd,ikhd->ihqk", queries, key_heads, preferred_element_type=jnp.float32
                )
                * scale_factor
            )
            key_live = jnp.arange(key_count, dtype=jnp.int32) % share < limit
            return (raw_scores, key_live)

        run_max = jnp.full((images, HEADS, share), -1e30, jnp.float32)
        fold_key_piece = lax.all_gather(key_rows, "blk", axis=1, tiled=True)
        value_piece = lax.all_gather(value_rows, "blk", axis=1, tiled=True)
        fold_raw_scores, fold_key_live = scores_for(fold_key_piece)
        masked = jnp.where(fold_key_live[None, None, None, :], fold_raw_scores, -1e30)
        new_max = jnp.maximum(run_max, jnp.max(masked, axis=-1))
        weights = jnp.where(
            fold_key_live[None, None, None, :], jnp.exp(masked - new_max[..., None]), 0.0
        )
        fold_key_count = value_piece.shape[1]
        value_heads = value_piece.reshape(images, fold_key_count, HEADS, head_size)
        run_total = jnp.sum(weights, axis=-1)
        run_acc = jnp.einsum(
            "ihqk,ikhd->ihqd",
            weights.astype(jnp.bfloat16),
            value_heads,
            preferred_element_type=jnp.float32,
        )
        run_max, run_total, run_acc = (new_max, run_total, run_acc)
        attended_heads = run_acc / run_total[..., None]
        log_total = run_max + jnp.log(run_total)
        attended = (
            attended_heads.transpose(0, 2, 1, 3)
            .reshape(layer_row_count, width)
            .astype(jnp.bfloat16)
        )
        attn_out = jnp.dot(attended, w_out, preferred_element_type=jnp.float32) + bias_after
        middle = flat_rows + attn_out
        normed_two_f, norm_two_back = jax.vjp(layer_norm, middle, gain_two, shift_two)
        normed_two = normed_two_f.astype(jnp.bfloat16)
        hidden = jnp.dot(normed_two, w_up, preferred_element_type=jnp.float32) + bias_expand
        activated_f, gelu_back = jax.vjp(gelu_exact, hidden)
        activated = activated_f.astype(jnp.bfloat16)
        branch = jnp.dot(activated, w_down, preferred_element_type=jnp.float32) + bias_reduce
        out_rows = (middle + branch).astype(jnp.bfloat16)
        grad_branch = grad_out.astype(jnp.bfloat16)
        grad_reduce = rows_dot(activated, grad_branch)
        grad_bias_reduce = jnp.sum(grad_branch.astype(jnp.float32), axis=0)
        grad_activated = back_dot(grad_branch, w_down)
        (grad_hidden_f,) = gelu_back(grad_activated)
        grad_hidden = grad_hidden_f.astype(jnp.bfloat16)
        grad_expand = rows_dot(normed_two, grad_hidden)
        grad_bias_expand = jnp.sum(grad_hidden.astype(jnp.float32), axis=0)
        grad_middle_part, grad_gain_two, grad_shift_two = norm_two_back(back_dot(grad_hidden, w_up))
        grad_middle = grad_out + grad_middle_part
        grad_attn = grad_middle.astype(jnp.bfloat16)
        grad_after = rows_dot(attended, grad_attn)
        grad_bias_after = jnp.sum(grad_attn.astype(jnp.float32), axis=0)
        grad_attended = (
            back_dot(grad_attn, w_out).astype(jnp.bfloat16).reshape(images, share, HEADS, head_size)
        )
        key_all = lax.all_gather(key_rows, "blk", axis=1, tiled=True)
        value_all = lax.all_gather(value_rows, "blk", axis=1, tiled=True)
        total_keys = key_all.shape[1]
        raw_scores, key_live = scores_for(key_all)
        weights = jnp.where(
            key_live[None, None, None, :], jnp.exp(raw_scores - log_total[..., None]), 0.0
        )
        weights_low = weights.astype(jnp.bfloat16)
        delta = jnp.einsum("iqhd,ihqd->ihq", grad_attended.astype(jnp.float32), attended_heads)
        grad_value = jnp.einsum(
            "ihqk,iqhd->ikhd", weights_low, grad_attended, preferred_element_type=jnp.float32
        ).reshape(images, total_keys, width)
        value_heads = value_all.reshape(images, total_keys, HEADS, head_size)
        key_heads = key_all.reshape(images, total_keys, HEADS, head_size)
        grad_weights = jnp.einsum(
            "iqhd,ikhd->ihqk", grad_attended, value_heads, preferred_element_type=jnp.float32
        )
        grad_scores = (weights * (grad_weights - delta[..., None])).astype(jnp.bfloat16)
        grad_query = (
            jnp.einsum(
                "ihqk,ikhd->iqhd", grad_scores, key_heads, preferred_element_type=jnp.float32
            )
            * scale_factor
        )
        grad_key = (
            jnp.einsum(
                "ihqk,iqhd->ikhd", grad_scores, queries, preferred_element_type=jnp.float32
            ).reshape(images, total_keys, width)
            * scale_factor
        )
        own_key = lax.psum_scatter(
            grad_key.astype(jnp.bfloat16), "blk", scatter_dimension=1, tiled=True
        ).astype(jnp.float32)
        own_value = lax.psum_scatter(
            grad_value.astype(jnp.bfloat16), "blk", scatter_dimension=1, tiled=True
        ).astype(jnp.float32)
        grad_projected = jnp.concatenate(
            [
                grad_query.reshape(layer_row_count, width),
                own_key.reshape(layer_row_count, width),
                own_value.reshape(layer_row_count, width),
            ],
            axis=1,
        ).astype(jnp.bfloat16)
        grad_proj = rows_dot(normed_one, grad_projected)
        grad_proj_f = grad_projected.astype(jnp.float32)
        grad_bias_query = jnp.sum(grad_proj_f[:, :width], axis=0)
        grad_bias_value = jnp.sum(grad_proj_f[:, 2 * width :], axis=0)
        grad_rows_part, grad_gain_one, grad_shift_one = norm_one_back(
            back_dot(grad_projected, w_qkv)
        )
        grad_rows = grad_middle + grad_rows_part
        grads = (
            grad_gain_one,
            grad_shift_one,
            grad_proj,
            grad_bias_query,
            grad_bias_value,
            grad_after,
            grad_bias_after,
            grad_gain_two,
            grad_shift_two,
            grad_expand,
            grad_bias_expand,
            grad_reduce,
            grad_bias_reduce,
        )
        out_rows, grad_rows, grads = (out_rows, grad_rows, grads)
        outputs.append(out_rows.reshape(images, share, width))
        grad_mask = jnp.sum(jnp.where(flag_rows[:, None], grad_rows, 0.0), axis=0)
        token_grads.append(
            jnp.where(flag_rows[:, None], 0.0, grad_rows).reshape(images, share, width)
        )
        batches.append((grad_mask,) + grads)
    block_out = jnp.stack(outputs)
    token_grad = jnp.stack(token_grads)
    local_sums = ()
    for position, batch_grads in enumerate(batches):
        if position == 0:
            local_sums = batch_grads
        else:
            local_sums = tuple((earlier + later for earlier, later in zip(local_sums, batch_grads)))
    (
        acc_mask,
        acc_gain_one,
        acc_shift_one,
        acc_proj,
        acc_bias_query,
        acc_bias_value,
        acc_after,
        acc_bias_after,
        acc_gain_two,
        acc_shift_two,
        acc_expand,
        acc_bias_expand,
        acc_reduce,
        acc_bias_reduce,
    ) = local_sums
    final_sums = lax.psum(
        (
            acc_mask,
            acc_gain_one,
            acc_shift_one,
            acc_proj,
            acc_bias_query,
            acc_bias_value,
            acc_after,
            acc_bias_after,
            acc_gain_two,
            acc_shift_two,
            acc_expand,
            acc_bias_expand,
            acc_reduce,
            acc_bias_reduce,
        ),
        ("dp", "blk"),
    )
    image_total = float(micro_count * images * lax.axis_size("dp"))
    return (block_out, token_grad) + tuple((item / image_total for item in final_sums))


def solution(mesh):
    placed = (
        P(None, "dp", "blk", None),
        P(None, "dp", "blk"),
        P(None, "dp"),
        P(None, "dp", "blk", None),
        P(),
        P(),
        P(),
        P(),
        P(),
        P(),
        P(),
        P(),
        P(),
        P(),
        P(),
        P(),
        P(),
        P(),
    )
    return jax.shard_map(
        shards,
        mesh=mesh,
        in_specs=placed,
        out_specs=(
            P(None, "dp", "blk", None),
            P(None, "dp", "blk", None),
            P(),
            P(),
            P(),
            P(),
            P(),
            P(),
            P(),
            P(),
            P(),
            P(),
            P(),
            P(),
            P(),
            P(),
        ),
        check_vma=False,
    )
```

profile of v0, /device:TPU:1, one launch (start us, length us, event | category | flops | bytes accessed | tf_op | source)
XLA Modules:
  0.0 463.1 jit_solution(151145795815784572)
XLA Ops:
  33.3 8.5 %all_gather.19 = bf16[2,256,512]{2,1,0:T(8,128)(2,1)S(1)} all-gather(bf16[2,64,512]{2,1,0:T(8,128)(2,1)S(1)} %bitcast.181), channel_id=1, replica_groups=mesh['dp'=8,'blk'=4] {'blk'}, dimensions={1}, use_global_device_ids=true | all-gather | bytes 655360 | tf_op jit(solution)/shard_map/all_gather | solution.py:104
  42.8 7.3 %all_gather.17 = bf16[2,256,512]{2,1,0:T(8,128)(2,1)S(1)} all-gather(bf16[2,64,512]{2,1,0:T(8,128)(2,1)S(1)} %bitcast.179), channel_id=1, replica_groups=mesh['dp'=8,'blk'=4] {'blk'}, dimensions={1}, use_global_device_ids=true | all-gather | bytes 655360 | tf_op jit(solution)/shard_map/all_gather | solution.py:104
  51.1 7.3 %all_gather.18 = bf16[2,256,512]{2,1,0:T(8,128)(2,1)S(1)} all-gather(bf16[2,64,512]{2,1,0:T(8,128)(2,1)S(1)} %bitcast.180), channel_id=1, replica_groups=mesh['dp'=8,'blk'=4] {'blk'}, dimensions={1}, use_global_device_ids=true | all-gather | bytes 655360 | tf_op jit(solution)/shard_map/all_gather | solution.py:103
  59.4 7.5 %all_gather.16 = bf16[2,256,512]{2,1,0:T(8,128)(2,1)S(1)} all-gather(bf16[2,64,512]{2,1,0:T(8,128)(2,1)} %bitcast.178), channel_id=1, replica_groups=mesh['dp'=8,'blk'=4] {'blk'}, dimensions={1}, use_global_device_ids=true | all-gather | bytes 655360 | tf_op jit(solution)/shard_map/all_gather | solution.py:103
  77.6 4.6 convert_reduce_fusion.1
  91.7 4.4 convert_reduce_fusion
  105.1 2.9 convolution_convert_fusion.1
  112.5 2.8 multiply_convert_fusion.1
  123.3 2.9 convolution_convert_fusion
  131.0 2.8 multiply_convert_fusion
  139.7 2.2 fusion.96
  142.0 2.8 fusion.81
  150.1 2.7 convolution_add_fusion.7
  152.8 2.7 fusion.97
  158.7 5.3 %convolution_add_fusion.1 = f32[2048,512]{1,0:T(8,128)} fusion(f32[2048,512]{1,0:T(8,128)} %fusion.97, bf16[128,2048]{1,0:T(8,128)(2,1)} %multiply_convert_fusion.2, bf16[128,512]{1,0:T(8,128)(2,1)} %get-tuple-element.91), kind=kOutput, calls=%fused_computation.1 | convolution fusion | flops 269484032 | bytes 9043968 | tf_op jit(solution)/shard_map/rk,rn->kn/dot_general | solution.py:25
  164.1 2.8 convolution_add_fusion.2
  170.2 10.6 %reduce-scatter.11.cloned.1.call-done = bf16[2,64,512]{2,1,0:T(8,128)(2,1)} async-done(((bf16[2,256,512]{2,1,0:T(8,128)(2,1)}), bf16[2,64,512]{2,1,0:T(8,128)(2,1)}) %reduce-scatter.11.cloned.1.call-update) | async-done | bytes 131088 | tf_op jit(solution)/shard_map/reduce_scatter | solution.py:186
  182.5 22.5 %reduce-scatter.9.cloned.1.call-done = bf16[2,64,512]{2,1,0:T(8,128)(2,1)} async-done(((bf16[2,256,512]{2,1,0:T(8,128)(2,1)}), bf16[2,64,512]{2,1,0:T(8,128)(2,1)}) %reduce-scatter.9.cloned.1.call-update) | async-done | bytes 131088 | tf_op jit(solution)/shard_map/reduce_scatter | solution.py:183
  208.4 2.3 convolution_add_fusion
  216.8 41.4 %all-reduce = (f32[512]{0:T(512)S(1)}, f32[512]{0:T(512)S(1)}, f32[512]{0:T(512)S(1)}, f32[512]{0:T(512)S(1)}, f32[512]{0:T(512)S(1)}, /*index=5*/f32[512]{0:T(5...) all-reduce(f32[512]{0:T(512)S(1)} %add.302, ...), channel_id=1, replica_groups=mesh['dp'=8,'blk'=4] {'dp','blk'}, use_global_device_ids=true, to_apply=%region_26.27 | all-reduce | flops 6656 | bytes 53248 | tf_op jit(solution)/shard_map/psum | solution.py:251
  265.1 180.3 %all-reduce.4.cloned.1.call-done = (f32[512,1536]{1,0:T(8,128)}, f32[512,512]{1,0:T(8,128)}, f32[512,2048]{1,0:T(8,128)}, f32[2048,512]{1,0:T(8,128)}) async-done(((f32[512,1536]{1,0:T(8,128)}, f32[512,512]{1,0:T(8,128)}, f32[512,2048]{1,0:T(8,128)}, f32[2048,512]{1,0:T(8,128)}), (f32[512,1536]{1,0:T(8,128)}, f32[512,512]{1,0:T(8,128)}, f32[512,2048]{1,0:T(8,128)}, ...) | async-done | bytes 12582928 | tf_op jit(solution)/shard_map/psum | solution.py:251
  445.4 4.0 broadcast_multiply_fusion.2
  450.4 2.5 broadcast_multiply_fusion.1
  454.1 2.5 broadcast_multiply_fusion
  (408 shorter events, 109.5 us)
Async XLA Ops:
  7.2 70.4 %copy-start = (bf16[2048,512]{1,0:T(8,128)(2,1)S(1)}, bf16[2048,512]{1,0:T(8,128)(2,1)}, u32[]{:S(2)}) copy-start(bf16[2048,512]{1,0:T(8,128)(2,1)} %param.34) | copy-start | bytes 6291460
  7.2 159.7 %reduce-scatter.7.cloned.1.call-start = ((), (), s32[]{:S(2)}) async-start(), calls=%async_computation.5 | async-start | bytes 655360 | tf_op jit(solution)/shard_map/reduce_scatter | solution.py:186
  12.4 9.2 %copy-start.112 = (f32[64]{0:T(128)}, f32[64]{0:T(128)S(1)}, u32[]{:S(2)}) copy-start(f32[64]{0:T(128)S(1)} %get-tuple-element.117) | copy-start | bytes 772
  12.4 12.6 %copy-start.114 = (f32[64]{0:T(128)}, f32[64]{0:T(128)S(1)}, u32[]{:S(2)}) copy-start(f32[64]{0:T(128)S(1)} %get-tuple-element.118) | copy-start | bytes 772
  13.2 16.9 %copy-start.83 = (pred[128]{0:T(512)(128)(4,1)}, pred[128]{0:T(512)(128)(4,1)S(1)}, u32[]{:S(2)}) copy-start(pred[128]{0:T(512)(128)(4,1)S(1)} %eq.50) | copy-start | bytes 388
  13.2 16.8 %copy-start.81 = (pred[128]{0:T(512)(128)(4,1)}, pred[128]{0:T(512)(128)(4,1)S(1)}, u32[]{:S(2)}) copy-start(pred[128]{0:T(512)(128)(4,1)S(1)} %eq.55) | copy-start | bytes 388
  13.9 16.2 %copy-start.64 = (f32[512]{0:T(512)}, f32[512]{0:T(512)S(1)}, u32[]{:S(2)}) copy-start(f32[512]{0:T(512)S(1)} %convert_element_type.260) | copy-start | bytes 6148
  15.1 15.0 %copy-start.98 = (f32[128]{0:T(128)}, f32[128]{0:T(128)S(1)}, u32[]{:S(2)}) copy-start(f32[128]{0:T(128)S(1)} %div.164) | copy-start | bytes 1540
  16.4 13.7 %copy-start.100 = (f32[128]{0:T(128)}, f32[128]{0:T(128)S(1)}, u32[]{:S(2)}) copy-start(f32[128]{0:T(128)S(1)} %div.172) | copy-start | bytes 1540
  19.4 10.7 %copy-start.102 = (f32[128]{0:T(128)}, f32[128]{0:T(128)S(1)}, u32[]{:S(2)}) copy-start(f32[128]{0:T(128)S(1)} %rsqrt.40) | copy-start | bytes 1540
  19.5 10.6 %copy-start.104 = (f32[128]{0:T(128)}, f32[128]{0:T(128)S(1)}, u32[]{:S(2)}) copy-start(f32[128]{0:T(128)S(1)} %rsqrt.42) | copy-start | bytes 1540
  20.2 55.2 %copy-start.61 = (f32[512]{0:T(512)}, f32[512]{0:T(512)S(1)}, u32[]{:S(2)}) copy-start(f32[512]{0:T(512)S(1)} %convert_element_type.274) | copy-start | bytes 6148
  20.9 54.5 %copy-start.67 = (f32[512]{0:T(512)}, f32[512]{0:T(512)S(1)}, u32[]{:S(2)}) copy-start(f32[512]{0:T(512)S(1)} %convert_element_type.275) | copy-start | bytes 6148
  21.6 8.5 %copy-start.69 = (f32[512]{0:T(512)}, f32[512]{0:T(512)S(1)}, u32[]{:S(2)}) copy-start(f32[512]{0:T(512)S(1)} %convert_element_type.264) | copy-start | bytes 6148
  25.6 49.8 %copy-start.66 = (f32[2048]{0:T(1024)}, f32[2048]{0:T(1024)S(1)}, u32[]{:S(2)}) copy-start(f32[2048]{0:T(1024)S(1)} %convert_element_type.277) | copy-start | bytes 24580
  30.4 36.7 %copy-start.26 = (bf16[2,64,16,32]{1,0,3,2:T(2,128)(2,1)}, bf16[2,64,16,32]{1,0,3,2:T(2,128)(2,1)S(1)}, u32[]{:S(2)}) copy-start(bf16[2,64,16,32]{1,0,3,2:T(2,128)(2,1)S(1)} %reshape.456) | copy-start | bytes 393220
  71.9 5.7 %copy-start.37 = (bf16[128,512]{0,1:T(8,128)(2,1)}, bf16[128,512]{0,1:T(8,128)(2,1)S(1)}, u32[]{:S(2)}) copy-start(bf16[128,512]{0,1:T(8,128)(2,1)S(1)} %convert_element_type.272) | copy-start | bytes 393220
  89.3 8.4 %copy-start.75 = (f32[128]{0:T(128)}, f32[128]{0:T(128)S(1)}, u32[]{:S(2)}) copy-start(f32[128]{0:T(128)S(1)} %broadcast_multiply_fusion.16) | copy-start | bytes 1540
  89.5 8.2 %copy-start.88 = (f32[128]{0:T(128)}, f32[128]{0:T(128)S(1)}, u32[]{:S(2)}) copy-start(f32[128]{0:T(128)S(1)} %fusion.65) | copy-start | bytes 1540
  110.1 58.4 %reduce-scatter.5.cloned.1.call-start = ((), (), s32[]{:S(2)}) async-start(), calls=%async_computation.4 | async-start | bytes 655360 | tf_op jit(solution)/shard_map/reduce_scatter | solution.py:183
  119.5 61.4 %reduce-scatter.11.cloned.1.call-start = ((), (), s32[]{:S(2)}) async-start(), calls=%async_computation.7 | async-start | bytes 655360 | tf_op jit(solution)/shard_map/reduce_scatter | solution.py:186
  122.5 5.8 %copy-start.50 = (bf16[2,64,16,32]{1,0,3,2:T(2,128)(2,1)}, bf16[2,64,16,32]{1,0,3,2:T(2,128)(2,1)S(1)}, u32[]{:S(2)}) copy-start(bf16[2,64,16,32]{1,0,3,2:T(2,128)(2,1)S(1)} %reshape.470) | copy-start | bytes 393220
  128.4 76.6 %reduce-scatter.9.cloned.1.call-start = ((), (), s32[]{:S(2)}) async-start(), calls=%async_computation.6 | async-start | bytes 655360 | tf_op jit(solution)/shard_map/reduce_scatter | solution.py:183
  138.0 307.4 %all-reduce.4.cloned.1.call-start = ((), (), s32[]{:S(2)}) async-start(), calls=%async_computation.8 | async-start | bytes 25165824 | tf_op jit(solution)/shard_map/psum | solution.py:251
  (104 other events, 240.2 us)
Sparse Core Ops, SparseCore 0:
  110.3 21.9 reduce-scatter.6
  134.9 21.6 reduce-scatter.4
  159.1 21.6 reduce-scatter.10
  183.3 21.6 reduce-scatter.8
  212.4 232.8 all-reduce.3
where the time goes:
time: 466 us; the launch traced here: 463 us
  waiting for transfers between devices  214 us (46%)
  blocking collectives  72 us (15%)
  matrix products  70.8 us (15%)
  other arithmetic  45.2 us (10%)
  local copies, waits for them, and re-layouts  43.2 us (9%)
  between operations  18 us (4%)
    psum x1, waiting for transfers between devices, shards(): lax.psum((acc_mask, acc_gain_one, acc_shift_one, acc_proj, acc_bias_query...  180 us
    psum x1, blocking collectives, shards(): lax.psum((acc_mask, acc_gain_one, acc_shift_one, acc_proj, acc_bias_query...  41.4 us
    dot_general x8, matrix products, rows_dot(): jnp.einsum('rk,rn->kn', lhs_rows, rhs_rows, preferred_element_type=jnp.fl...  22.6 us
    reduce_scatter x2, waiting for transfers between devices, shards(): lax.psum_scatter(grad_key.astype(jnp.bfloat16), 'blk', scatter_dimension=...  22.5 us
    dot_general x8, matrix products, back_dot(): jnp.einsum('rn,kn->rk', grad_rows, weight, preferred_element_type=jnp.flo...  16.2 us
    div x14, other arithmetic, shards(): item / image_total  15.8 us
    all_gather x2, blocking collectives, shards(): value_piece = lax.all_gather(value_rows, 'blk', axis=1, tiled=True)  15.8 us
    all_gather x2, blocking collectives, shards(): fold_key_piece = lax.all_gather(key_rows, 'blk', axis=1, tiled=True)  14.8 us
  transfers between devices with their start and end apart: 5, of which 3 were waited for; matrix products, arithmetic and copies ran while one was open for 15% of the time, Pallas kernels for 0%

commit v1 on v0

v1 whole, which is shorter than its diff:
```python
import functools

import jax
import jax.numpy as jnp
from jax import lax
from jax.experimental import pallas as pl
from jax.experimental.pallas import tpu as pltpu
from jax.sharding import PartitionSpec as P

HEADS = 16
LANES = 128
EPS = 1e-06
LOG2E = 1.4426950408889634
BF16 = jnp.bfloat16
F32 = jnp.float32
VMEM_LIMIT = 44 * 1024 * 1024


def dot(a, b):
    return jnp.dot(a, b, preferred_element_type=F32)


def dot_nt(a, b):
    return lax.dot_general(a, b, (((1,), (1,)), ((), ())), preferred_element_type=F32)


def dot_tn(a, b):
    return lax.dot_general(a, b, (((0,), (0,)), ((), ())), preferred_element_type=F32)


def norm_stats(rows):
    centre = jnp.mean(rows, axis=-1, keepdims=True)
    centred = rows - centre
    spread = jnp.mean(centred * centred, axis=-1, keepdims=True)
    rstd = lax.rsqrt(spread + EPS)
    return centred * rstd, rstd


def norm_back(grad_normed, xhat, rstd, gain):
    grad_xhat = grad_normed * gain
    first = jnp.mean(grad_xhat, axis=-1, keepdims=True)
    second = jnp.mean(grad_xhat * xhat, axis=-1, keepdims=True)
    return rstd * (grad_xhat - first - xhat * second)


class Pieces:
    def __init__(self, rows, cols, chips):
        self.rows = rows
        self.half = cols // 2
        self.row_blocks = min(chips, rows // 16)
        self.lane_blocks = chips // self.row_blocks
        self.height = rows // self.row_blocks
        self.width = self.half // self.lane_blocks
        self.tall = self.height * self.width // LANES


def relative(core, x, y, z, ax, ay, az, depth):
    px, py = ax ^ x, ay ^ y
    return jnp.where(core == 0, px * 2 + py, py * 2 + px) * depth + (az ^ z)


def chip_of(index, depth):
    return index // (2 * depth), (index // depth) % 2, index % depth


def absolute(core, x, y, z, index, depth):
    first, second, az = chip_of(index, depth)
    ax = jnp.where(core == 0, first ^ x, second ^ x)
    ay = jnp.where(core == 0, second ^ y, first ^ y)
    return (ax * 2 + ay) * depth + (az ^ z)


def store_pieces(out_ref, core, place, depth, pieces, base, value, row_start):
    x, y, z = place
    for first in range(0, value.shape[0], pieces.height):
        row_block = (row_start + first) // pieces.height
        for lane_block in range(pieces.lane_blocks):
            index = row_block * pieces.lane_blocks + lane_block
            rel = relative(core, x, y, z, *chip_of(index, depth), depth)
            for j in range(pieces.width // LANES):
                at = base + j * pieces.height
                lane = lane_block * pieces.width + j * LANES
                out_ref[rel, at : at + pieces.height, :] = value[
                    first : first + pieces.height, lane : lane + LANES
                ].astype(BF16)


def weight_grad(keep_ref, send_ref, core, place, depth, pieces, base, lhs, rhs_ref):
    stripe = max(pieces.height, min(512, pieces.rows))
    for out_ref, owner in ((send_ref, core ^ 1), (keep_ref, core)):
        rhs = rhs_ref[:, pl.ds(pl.multiple_of(owner * pieces.half, LANES), pieces.half)]
        for start in range(0, pieces.rows, stripe):
            value = dot_tn(lhs[:, start : start + stripe], rhs)
            store_pieces(out_ref, owner, place, depth, pieces, base, value, start)


def place_of(meta):
    return meta[0], (meta[1], meta[2], meta[3])


def fill_kernel(meta, tokens, flags, mask_token, *outs):
    blk = meta[5]
    count, share, _ = tokens.shape
    eye = lax.broadcasted_iota(jnp.int32, (share, share), 0) == lax.broadcasted_iota(
        jnp.int32, (share, share), 1
    )
    for k in range(count):
        at = blk ^ k
        flag = flags[pl.ds(at, 1), 0, :]
        column = jnp.sum(jnp.where(eye, flag, 0), axis=1, keepdims=True)
        outs[k][...] = jnp.where(
            column == 1, mask_token[...].astype(F32), tokens[at].astype(F32)
        ).astype(BF16)


def cotangent_kernel(meta, cotangent, flags, *outs):
    blk = meta[5]
    count, share, _ = cotangent.shape
    for k in range(count):
        at = blk ^ k
        outs[k][:share, :] = cotangent[at]
        outs[k][share:, :] = jnp.zeros((16, outs[k].shape[1]), BF16)
        row = lax.broadcasted_iota(jnp.int32, (16, share), 0) == 0
        flag = (flags[pl.ds(at, 1), 0, :] == 1).astype(F32)
        outs[k][share:, :share] = jnp.where(row, flag, 0.0).astype(BF16)


def forward_kernel(
    depth,
    down,
    count,
    share,
    meta,
    *refs,
):
    refs = list(refs)
    xs = [refs.pop(0) for _ in range(count)]
    cs = [refs.pop(0) for _ in range(count)]
    (
        gain1, bias1, w_qkv, b_query, b_value, w_out, b_out, gain2, bias2, w_up, b_up,
        qkv_ref, p_ref, rinv_ref, o_ref, x2_ref, n2_ref, h_ref, gp_ref, g_ref, keep_ref, send_ref,
    ) = refs
    core, place = place_of(meta)
    quota = meta[4]
    width = xs[0].shape[1]
    head = width // HEADS
    rows = count * share
    live_rows = lax.broadcasted_iota(jnp.int32, (share, 1), 0) < quota
    for k in range(count):
        g_ref[k * share : (k + 1) * share, :] = jnp.where(
            live_rows, cs[k][:share, :].astype(F32), 0.0
        ).astype(BF16)
    x = jnp.concatenate([ref[...] for ref in xs], axis=0).astype(F32)
    xhat, _ = norm_stats(x)
    n1 = (xhat * gain1[...].astype(F32) + bias1[...].astype(F32)).astype(BF16)
    for part in range(3):
        cols = slice(part * width, (part + 1) * width)
        value = dot(n1, w_qkv[:, cols])
        if part == 0:
            value = value + b_query[...].astype(F32)
        if part == 2:
            value = value + b_value[...].astype(F32)
        qkv_ref[:, cols] = value.astype(BF16)
    key = lax.broadcasted_iota(jnp.int32, (1, rows), 1)
    mask_row = jnp.where(key % share < quota, 0.0, -1e30).astype(F32)
    lane_head = lax.broadcasted_iota(jnp.int32, (1, LANES), 1) // head
    scale = head ** (-0.5) * LOG2E
    per = LANES // head
    ones = jnp.ones((rows, LANES), BF16)
    for group in range(width // LANES):
        at = group * LANES
        q = qkv_ref[:, at : at + LANES]
        keys = qkv_ref[:, width + at : width + at + LANES]
        values = jnp.concatenate(
            [qkv_ref[:, 2 * width + at : 2 * width + at + LANES], ones], axis=1
        )
        acc = jnp.zeros((rows, LANES), F32)
        racc = jnp.zeros((rows, LANES), F32)
        for i in range(per):
            here = lane_head == i
            qm = q * here.astype(F32).astype(BF16)
            s = dot_nt(qm, keys) * scale + mask_row
            top = jnp.max(s, axis=1, keepdims=True)
            p = jnp.exp2(s - top).astype(BF16)
            p_ref[group * per + i] = p
            both = dot(p, values)
            rinv = 1.0 / both[:, LANES:]
            acc = jnp.where(here, both[:, :LANES] * rinv, acc)
            racc = jnp.where(here, rinv, racc)
        o_ref[:, at : at + LANES] = acc.astype(BF16)
        rinv_ref[:, at : at + LANES] = racc
    x2 = x + (dot(o_ref[...], w_out[...]) + b_out[...].astype(F32))
    x2_ref[...] = x2
    xhat2, _ = norm_stats(x2)
    n2 = (xhat2 * gain2[...].astype(F32) + bias2[...].astype(F32)).astype(BF16)
    n2_ref[...] = n2
    hidden = w_up.shape[1]
    step = 512
    for start in range(0, hidden, step):
        cols = slice(start, start + step)
        u = dot(n2, w_up[:, cols]) + b_up[:, cols].astype(F32)
        cdf = 0.5 + 0.5 * lax.erf(u * (0.5**0.5))
        pdf = jnp.exp(-0.5 * u * u) * 0.3989422804014327
        h_ref[:, cols] = (u * cdf).astype(BF16)
        gp_ref[:, cols] = (cdf + u * pdf).astype(BF16)
    weight_grad(keep_ref, send_ref, core, place, depth, down, 0, h_ref, g_ref)


def middle_kernel(
    depth,
    up,
    after,
    meta,
    g_ref, gp_ref, h_ref, n2_ref, o_ref, x2_ref, gain2, w_up, w_down, b_down,
    keep_ref, send_ref, dx2_ref, dx2r_ref, out_ref, small_ref, du_ref,
):
    core, place = place_of(meta)
    g = g_ref[...]
    hidden = w_up.shape[1]
    width = g.shape[1]
    step = 512
    small_ref[...] = jnp.zeros(small_ref.shape, F32)
    dn2 = jnp.zeros((g.shape[0], width), F32)
    for start in range(0, hidden, step):
        cols = slice(start, start + step)
        dh = dot_nt(g, w_down[cols, :])
        du = (dh * gp_ref[:, cols].astype(F32)).astype(BF16)
        du_ref[:, cols] = du
        small_ref[0:1, cols] = jnp.sum(du.astype(F32), axis=0, keepdims=True)
        dn2 = dn2 + dot_nt(du, w_up[:, cols])
    x2 = x2_ref[...]
    xhat, rstd = norm_stats(x2)
    gf = g.astype(F32)
    dx2 = gf + norm_back(dn2, xhat, rstd, gain2[...].astype(F32))
    dx2_ref[...] = dx2
    dx2r = dx2.astype(BF16)
    dx2r_ref[...] = dx2r
    small_ref[1:2, 0:width] = jnp.sum(dx2r.astype(F32), axis=0, keepdims=True)
    small_ref[1:2, width : 2 * width] = jnp.sum(dn2 * xhat, axis=0, keepdims=True)
    small_ref[1:2, 2 * width : 3 * width] = jnp.sum(dn2, axis=0, keepdims=True)
    small_ref[1:2, 3 * width : 4 * width] = jnp.sum(gf, axis=0, keepdims=True)
    weight_grad(keep_ref, send_ref, core, place, depth, up, 0, n2_ref, du_ref)
    weight_grad(keep_ref, send_ref, core, place, depth, after, up.tall, o_ref, dx2r_ref)
    out_ref[...] = (x2 + (dot(h_ref[...], w_down[...]) + b_down[...].astype(F32))).astype(BF16)


def backward_kernel(
    depth,
    proj,
    count,
    share,
    meta,
    *refs,
):
    refs = list(refs)
    xs = [refs.pop(0) for _ in range(count)]
    cs = [refs.pop(0) for _ in range(count)]
    qkv_ref, p_ref, rinv_ref, o_ref, dx2_ref, dx2r_ref, block_ref, sub_ref, gain1, bias1, w_qkv, w_out = refs[:12]
    refs = refs[12:]
    results = [refs.pop(0) for _ in range(count)]
    keep_ref, send_ref, dqkv_ref, small = refs
    core, place = place_of(meta)
    rows = count * share
    width = xs[0].shape[1]
    head = width // HEADS
    per = LANES // head
    d_o = dot_nt(dx2r_ref[...], w_out[...]).astype(BF16).astype(F32)
    d_scaled = d_o * rinv_ref[...]
    product = (d_scaled * o_ref[...].astype(F32)).astype(BF16)
    d_scaled = d_scaled.astype(BF16)
    lane_head = lax.broadcasted_iota(jnp.int32, (1, LANES), 1) // head
    minus = jnp.full((rows, LANES), -1.0, BF16)
    scale = head ** (-0.5)
    for group in range(width // LANES):
        at = group * LANES
        q = qkv_ref[:, at : at + LANES]
        keys = qkv_ref[:, width + at : width + at + LANES]
        values = jnp.concatenate(
            [qkv_ref[:, 2 * width + at : 2 * width + at + LANES], minus], axis=1
        )
        ds_o = d_scaled[:, at : at + LANES]
        pr_o = product[:, at : at + LANES]
        dq = jnp.zeros((rows, LANES), F32)
        dk = jnp.zeros((rows, LANES), F32)
        dv = jnp.zeros((rows, LANES), F32)
        for i in range(per):
            here = lane_head == i
            mask = here.astype(F32).astype(BF16)
            lhs = jnp.concatenate([ds_o * mask, pr_o * mask], axis=1)
            p = p_ref[group * per + i]
            ds = (p.astype(F32) * dot_nt(lhs, values)).astype(BF16)
            dq = jnp.where(here, dot(ds, keys), dq)
            dk = jnp.where(here, dot_tn(ds, q), dk)
            dv = jnp.where(here, dot_tn(p, ds_o), dv)
        dqkv_ref[:, at : at + LANES] = (dq * scale).astype(BF16)
        dqkv_ref[:, width + at : width + at + LANES] = (dk * scale).astype(BF16)
        dqkv_ref[:, 2 * width + at : 2 * width + at + LANES] = dv.astype(BF16)
    x = jnp.concatenate([ref[...] for ref in xs], axis=0).astype(F32)
    xhat, rstd = norm_stats(x)
    gain = gain1[...].astype(F32)
    n1 = (xhat * gain + bias1[...].astype(F32)).astype(BF16)
    weight_grad(keep_ref, send_ref, core, place, depth, proj, 0, n1, dqkv_ref)
    dn1 = dot_nt(dqkv_ref[...], w_qkv[...])
    dx = (dx2_ref[...] + norm_back(dn1, xhat, rstd, gain)).astype(BF16)
    d_mask = jnp.zeros((16, width), F32)
    for k in range(count):
        part = dx[k * share : (k + 1) * share, :]
        d_mask = d_mask + dot(cs[k][share : share + 16, :share], part)
        results[k][:share, :] = block_ref[k * share : (k + 1) * share, :]
        results[k][share:, :] = part
    blocks = small.shape[0]
    small[...] = jnp.zeros(small.shape, F32)
    wide = [
        d_mask[0:1, :],
        jnp.sum(dn1 * xhat, axis=0, keepdims=True),
        jnp.sum(dn1, axis=0, keepdims=True),
        jnp.sum(dqkv_ref[:, :width].astype(F32), axis=0, keepdims=True),
        jnp.sum(dqkv_ref[:, 2 * width :].astype(F32), axis=0, keepdims=True),
        sub_ref[1:2, :],
        sub_ref[0:1, :],
    ]
    lines = [v[:, j : j + LANES] for v in wide for j in range(0, v.shape[1], LANES)]
    each = -(-len(lines) // blocks)
    for i, line in enumerate(lines):
        small[i // each, i % each : i % each + 1, :] = line
    chips = blocks // 2
    x0, y0, z0 = place
    for out_ref, owner in ((send_ref, core ^ 1), (keep_ref, core)):
        for index in range(chips):
            rel = relative(owner, x0, y0, z0, *chip_of(index, depth), depth)
            out_ref[rel, proj.tall : proj.tall + 16, :] = small[owner * chips + index].astype(BF16)


def load_pieces(refs, rel):
    for ref in refs:
        if rel < ref.shape[0]:
            return ref, rel
        rel -= ref.shape[0]


def gather_kernel(depth, layout, scale, small_at, sizes, meta, *refs):
    own, other = refs[:3], refs[3:6]
    outs = refs[6 : 6 + len(layout)]
    rest = refs[6 + len(layout) :]
    core, (x, y, z) = place_of(meta)
    chips = sum(ref.shape[0] for ref in own)
    for held, owner in ((own, core), (other, core ^ 1)):
        for rel in range(chips):
            ref, at_block = load_pieces(held, rel)
            index = absolute(owner, x, y, z, rel, depth)
            for out, (pieces, base) in zip(outs, layout):
                row = pl.multiple_of((index // pieces.lane_blocks) * pieces.height, 8)
                lane = owner * pieces.half + (index % pieces.lane_blocks) * pieces.width
                for j in range(pieces.width // LANES):
                    at = base + j * pieces.height
                    block = ref[at_block, at : at + pieces.height, :]
                    out[
                        pl.ds(row, pieces.height),
                        pl.ds(pl.multiple_of(lane + j * LANES, LANES), LANES),
                    ] = block.astype(F32) * scale
            if rest:
                small = rest[-1]
                small[owner * chips + index] = (
                    ref[at_block, small_at : small_at + 16, :].astype(F32) * scale
                )
    if rest:
        small = rest[-1]
        lines = sum(sizes) // LANES
        each = -(-lines // (2 * chips))
        line = 0
        for out, size in zip(rest[:-1], sizes):
            for j in range(size // LANES):
                out[:, j * LANES : (j + 1) * LANES] = small[
                    line // each, line % each : line % each + 1, :
                ]
                line += 1


def finish_kernel(meta, flags, *refs):
    count = len(refs) - 2
    block_out, token_grad = refs[-2:]
    share = block_out.shape[1]
    blk = meta[5]
    eye = lax.broadcasted_iota(jnp.int32, (share, share), 0) == lax.broadcasted_iota(
        jnp.int32, (share, share), 1
    )
    for k in range(count):
        at = blk ^ k
        block_out[at] = refs[k][:share, :]
        flag = flags[pl.ds(at, 1), 0, :]
        column = jnp.sum(jnp.where(eye, flag, 0), axis=1, keepdims=True)
        token_grad[at] = jnp.where(column == 1, 0.0, refs[k][share:, :].astype(F32))


SCALARS = pl.BlockSpec(memory_space=pltpu.SMEM)
WHOLE = pl.BlockSpec(memory_space=pltpu.VMEM)


def call(kernel, outs, *args, scratch=(), flops=0, name=None):
    size = sum(a.size * a.dtype.itemsize for a in args) + sum(
        o.size * o.dtype.itemsize for o in outs
    )
    return pl.pallas_call(
        kernel,
        out_shape=tuple(outs),
        in_specs=[SCALARS] + [WHOLE] * (len(args) - 1),
        out_specs=tuple([WHOLE] * len(outs)),
        scratch_shapes=list(scratch),
        compiler_params=pltpu.CompilerParams(vmem_limit_bytes=VMEM_LIMIT),
        cost_estimate=pl.CostEstimate(flops=flops, bytes_accessed=size, transcendentals=0),
        name=name,
    )(*args)


def shape(dims, kind=BF16):
    return jax.ShapeDtypeStruct(tuple(dims), kind)


def add(*parts):
    total = parts[0].astype(F32)
    for part in parts[1:]:
        total = total + part.astype(F32)
    return total.astype(BF16)


def shards(
    dp_size,
    blk_size,
    tokens,
    mask_flags,
    buckets,
    cotangent,
    mask_token,
    norm1_gain,
    norm1_bias,
    w_qkv,
    b_query,
    b_value,
    w_out,
    b_out,
    norm2_gain,
    norm2_bias,
    w_up,
    b_up,
    w_down,
    b_down,
):
    micro_count, images, share, width = tokens.shape
    hidden = w_up.shape[1]
    count = micro_count * images
    rows = count * share
    depth = dp_size // 2
    chips = 4 * depth
    total_images = float(micro_count * images * dp_size)

    dp = lax.axis_index("dp")
    blk = lax.axis_index("blk")
    bucket = buckets[blk // images, 0]
    quota = jnp.where(bucket == 0, 25, jnp.where(bucket == 1, 49, 64))
    meta = jnp.stack([blk % 2, blk // 2, dp % 2, dp // 2, quota, blk]).astype(jnp.int32)

    def pairs(change):
        out = []
        for d in range(dp_size):
            for b in range(blk_size):
                nz, ny, nx, nc = change(d // 2, d % 2, b // 2, b % 2)
                out.append((d * blk_size + b, (nz * 2 + ny) * blk_size + nx * 2 + nc))
        return out

    def send(value, change):
        return lax.ppermute(value, ("dp", "blk"), pairs(change))

    def core_pair(z, y, x, c):
        return z, y, x, c ^ 1

    def first_pair(z, y, x, c):
        return (z, y, x ^ 1, c) if c == 0 else (z, y ^ 1, x, c)

    def second_pair(z, y, x, c):
        return (z, y ^ 1, x, c) if c == 0 else (z, y, x ^ 1, c)

    def depth_pair(k):
        return lambda z, y, x, c: (z ^ k, y, x, c)

    def image_pair(k):
        return lambda z, y, x, c: (z, y, x ^ (k >> 1), c ^ (k & 1))

    def reduce_blocks(keep, sent):
        got = send(sent, core_pair)
        h = chips // 2
        away = add(keep[h:], got[h:])
        stay = add(keep[:h], got[:h])
        got = send(away, first_pair)
        h = chips // 4
        away = add(stay[h:], got[h:])
        stay = add(stay[:h], got[:h])
        got = send(away, second_pair)
        held = add(stay, got)
        return add(held[0], *[send(held[k], depth_pair(k)) for k in range(1, depth)])

    def gather_blocks(block):
        first = jnp.stack([block] + [send(block, depth_pair(k)) for k in range(1, depth)])
        second = send(first, second_pair)
        third = send(jnp.concatenate([first, second]), first_pair)
        mine = (first, second, third)
        return mine + tuple(send(a, core_pair) for a in mine)

    def wide(v):
        return v.reshape(1, -1)

    flags = mask_flags.reshape(count, 1, share)
    xs = call(
        fill_kernel,
        [shape((share, width))] * count,
        meta,
        tokens.reshape(count, share, width),
        flags,
        wide(mask_token),
        name="fill",
    )
    xs = [xs[0]] + [send(xs[k], image_pair(k)) for k in range(1, count)]
    cs = call(
        cotangent_kernel,
        [shape((share + 16, width))] * count,
        meta,
        cotangent.reshape(count, share, width),
        flags,
        name="cotangents",
    )
    cs = [cs[0]] + [send(cs[k], image_pair(k)) for k in range(1, count)]

    down = Pieces(hidden, width, chips)
    up = Pieces(width, hidden, chips)
    after = Pieces(width, width, chips)
    proj = Pieces(width, 3 * width, chips)

    qkv, p, rinv, o, x2, n2, h, gp, g, keep1, send1 = call(
        functools.partial(forward_kernel, depth, down, count, share),
        [
            shape((rows, 3 * width)),
            shape((HEADS, rows, rows)),
            shape((rows, width), F32),
            shape((rows, width)),
            shape((rows, width), F32),
            shape((rows, width)),
            shape((rows, hidden)),
            shape((rows, hidden)),
            shape((rows, width)),
            shape((chips, down.tall, LANES)),
            shape((chips, down.tall, LANES)),
        ],
        meta,
        *xs,
        *cs,
        wide(norm1_gain),
        wide(norm1_bias),
        w_qkv,
        wide(b_query),
        wide(b_value),
        w_out,
        wide(b_out),
        wide(norm2_gain),
        wide(norm2_bias),
        w_up,
        wide(b_up),
        flops=2 * rows * width * (3 * width + width + 2 * hidden),
        name="forward",
    )
    keep2, send2, dx2, dx2r, block, sub = call(
        functools.partial(middle_kernel, depth, up, after),
        [
            shape((chips, up.tall + after.tall, LANES)),
            shape((chips, up.tall + after.tall, LANES)),
            shape((rows, width), F32),
            shape((rows, width)),
            shape((rows, width)),
            shape((8, hidden), F32),
        ],
        meta,
        g,
        gp,
        h,
        n2,
        o,
        x2,
        wide(norm2_gain),
        w_up,
        w_down,
        wide(b_down),
        scratch=[pltpu.VMEM((rows, hidden), BF16)],
        flops=2 * rows * width * (4 * hidden + width),
        name="middle",
    )
    *results, keep3, send3 = call(
        functools.partial(backward_kernel, depth, proj, count, share),
        [shape((2 * share, width))] * count + [shape((chips, proj.tall + 16, LANES))] * 2,
        meta,
        *xs,
        *cs,
        qkv,
        p,
        rinv,
        o,
        dx2,
        dx2r,
        block,
        sub,
        wide(norm1_gain),
        wide(norm1_bias),
        w_qkv,
        w_out,
        scratch=[
            pltpu.VMEM((rows, 3 * width), BF16),
            pltpu.VMEM((2 * chips, 16, LANES), F32),
        ],
        flops=2 * rows * width * (7 * width),
        name="backward",
    )

    done1 = gather_blocks(reduce_blocks(keep1, send1))
    done2 = gather_blocks(reduce_blocks(keep2, send2))
    done3 = gather_blocks(reduce_blocks(keep3, send3))

    def whole(done, layout, small_at=0, sizes=(), name=None):
        outs = [shape((p.rows, 2 * p.half), F32) for p, _ in layout]
        scratch = []
        if sizes:
            outs += [shape((1, n), F32) for n in sizes]
            scratch = [pltpu.VMEM((2 * chips, 16, LANES), F32)]
        return call(
            functools.partial(
                gather_kernel, depth, layout, 1.0 / total_images, small_at, sizes
            ),
            outs,
            meta,
            *done,
            scratch=scratch,
            name=name,
        )

    (grad_down,) = whole(done1, [(down, 0)], name="gather_down")
    grad_up, grad_out = whole(done2, [(up, 0), (after, up.tall)], name="gather_up")
    sizes = (width,) * 9 + (hidden,)
    grad_proj, *small = whole(done3, [(proj, 0)], proj.tall, sizes, name="gather_proj")
    mask_g, gain1_g, bias1_g, query_g, value_g, after_g, gain2_g, bias2_g, reduce_g, expand_g = [
        v.reshape(-1) for v in small
    ]

    results = [results[0]] + [send(results[k], image_pair(k)) for k in range(1, count)]
    block_out, token_grad = call(
        finish_kernel,
        [shape((count, share, width)), shape((count, share, width), F32)],
        meta,
        flags,
        *results,
        name="finish",
    )
    return (
        block_out.reshape(tokens.shape),
        token_grad.reshape(tokens.shape),
        mask_g,
        gain1_g,
        bias1_g,
        grad_proj,
        query_g,
        value_g,
        grad_out,
        after_g,
        gain2_g,
        bias2_g,
        grad_up,
        expand_g,
        grad_down,
        reduce_g,
    )


def solution(mesh):
    rows = P(None, "dp", "blk", None)
    placed = (rows, P(None, "dp", "blk"), P(None, "dp"), rows) + (P(),) * 14
    return jax.shard_map(
        functools.partial(shards, mesh.shape["dp"], mesh.shape["blk"]),
        mesh=mesh,
        in_specs=placed,
        out_specs=(rows, rows) + (P(),) * 14,
        check_vma=False,
    )
```

time: 466 us -> 170 us (0.36)
  waiting for transfers between devices: 214 us -> 43.8 us
  starting transfers between devices: 0.43 us -> 75.6 us
  blocking collectives: 72 us -> 0 us
  matrix products: 70.8 us -> 0 us
  other arithmetic: 45.2 us -> 2.86 us
  Pallas kernels: 0 us -> 31.5 us
  local copies, waits for them, and re-layouts: 43.2 us -> 13.2 us
  between operations: 18 us -> 2.31 us
    psum x1 -> x0, waiting for transfers between devices: 180 us -> none  [shards(): lax.psum((acc_mask, acc_gain_one, acc_shift_one, acc_proj, acc_bias_query...]
    ppermute x0 -> x51, starting transfers between devices: none -> 75.6 us  [send(): return lax.ppermute(value, ('dp', 'blk'), pairs(change))]
    dot_general x36 -> x0, matrix products: 70.8 us -> none  [the longest x8 22.6 us: rows_dot(): jnp.einsum('rk,rn->kn', lhs_rows, rhs_rows, preferred_element_type=jnp.fl...]
    ppermute x0 -> x51, waiting for transfers between devices: none -> 43.8 us  [send(): return lax.ppermute(value, ('dp', 'blk'), pairs(change))]
    psum x1 -> x0, blocking collectives: 41.4 us -> none  [shards(): lax.psum((acc_mask, acc_gain_one, acc_shift_one, acc_proj, acc_bias_query...]
    reduce_scatter x4 -> x0, waiting for transfers between devices: 33.1 us -> none  [the longest x2 22.5 us: shards(): lax.psum_scatter(grad_key.astype(jnp.bfloat16), 'blk', scatter_dimension=...]
    pallas_call x0 -> x9, Pallas kernels: none -> 31.5 us  [call(): pl.pallas_call(kernel, out_shape=tuple(outs), in_specs=[SCALARS] + [WHOLE...]
    all_gather x4 -> x0, blocking collectives: 30.5 us -> none  [the longest x2 15.8 us: shards(): value_piece = lax.all_gather(value_rows, 'blk', axis=1, tiled=True)]
  transfers between devices with their start and end apart: 5 -> 51, of which waited for: 3 -> 18; matrix products, arithmetic and copies ran while one was open for 15% -> 5% of each run, Pallas kernels for 0% -> 5%
where the time goes in v1:
time: 170 us; the launch traced here: 169 us
  starting transfers between devices  75.6 us (44%)
  waiting for transfers between devices  43.8 us (26%)
  Pallas kernels  31.5 us (19%)
  local copies, waits for them, and re-layouts  13.2 us (8%)
  other arithmetic  2.86 us (2%)
  between operations  2.31 us (1%)
    ppermute x51, starting transfers between devices, send(): return lax.ppermute(value, ('dp', 'blk'), pairs(change))  75.6 us
    ppermute x51, waiting for transfers between devices, send(): return lax.ppermute(value, ('dp', 'blk'), pairs(change))  43.8 us
    pallas_call x9, Pallas kernels, call(): pl.pallas_call(kernel, out_shape=tuple(outs), in_specs=[SCALARS] + [WHOLE...  31.5 us
    reshape x10, local copies, waits for them, and re-layouts, wide(): return v.reshape(1, -1)  6.83 us
    unnamed x31, local copies, waits for them, and re-layouts  6.14 us
  transfers between devices with their start and end apart: 51, of which 18 were waited for; matrix products, arithmetic and copies ran while one was open for 5% of the time, Pallas kernels for 5%

profile of v1, /device:TPU:1, one launch (start us, length us, event | category | flops | bytes accessed | tf_op | source)
XLA Modules:
  0.0 169.3 jit_solution(3490631639110299770)
XLA Ops:
  8.5 2.3 %collective-permute-start.4 = (bf16[80,512]{1,0:T(8,128)(2,1)S(1)}, bf16[80,512]{1,0:T(8,128)(2,1)S(1)}, u32[]{:S(2)}, u32[]{:S(2)}) collective-permute-start(bf16[80,512]{1,0:T(8,128)(2,1)S(1)} %get-tuple-element.68), channel_id=1, source_target_pairs={{0,2},{1,3},{2,0},{3,1},{4,6},{5,7},{6,4},{7,5},{8,10},{9,11},{10,... | collective-permute-start | bytes 245768 | tf_op jit(solution)/shard_map/ppermute | solution.py:471
  21.8 7.5 %forward.1 = (bf16[256,1536]{1,0:T(8,128)(2,1)S(1)}, bf16[16,256,256]{2,1,0:T(8,128)(2,1)}, f32[256,512]{1,0:T(8,128)S(1)}, bf16[256,512]{1,0:T(8,128)(2,1)S(1)}...) custom-call(s32[6]{0:T(128)S(1)} %stack.72.meta, ...), custom_call_target="tpu_custom_call" | custom-call | flops 1610612736 | bytes 13708312 | tf_op jit(solution)/shard_map/forward/pallas_call | solution.py:403
  30.3 4.8 %middle.1 = (bf16[16,320,128]{2,1,0:T(8,128)(2,1)S(1)}, bf16[16,320,128]{2,1,0:T(8,128)(2,1)S(1)}, f32[256,512]{1,0:T(8,128)S(1)}, bf16[256,512]{1,0:T(8,128)(2,...) custom-call(s32[6]{0:T(128)S(1)} %stack.72.meta, bf16[256,512]{1,0:T(8,128)(2,1)S(1)} %get-tuple-element.74.g_ref, ...), custom_call_target="tpu_custom_call" | custom-call | flops 2281701376 | bytes 11339800 | tf_op jit(solution)/shard_map/middle/pallas_call | solution.py:403
  35.2 7.3 %backward.1 = (bf16[128,512]{1,0:T(8,128)(2,1)S(1)}, bf16[128,512]{1,0:T(8,128)(2,1)S(1)}, bf16[128,512]{1,0:T(8,128)(2,1)S(1)}, bf16[128,512]{1,0:T(8,128)(2,1)...) custom-call(s32[6]{0:T(128)S(1)} %stack.72.meta, ...), custom_call_target="tpu_custom_call" | custom-call | flops 939524096 | bytes 9701400 | tf_op jit(solution)/shard_map/backward/pallas_call | solution.py:403
  47.1 5.4 %collective-permute-done.10 = bf16[8,208,128]{2,1,0:T(8,128)(2,1)S(1)} collective-permute-done((bf16[8,208,128]{2,1,0:T(8,128)(2,1)S(1)}, bf16[8,208,128]{2,1,0:T(8,128)(2,1)S(1)}, u32[]{:S(2)}, u32[]{:S(2)}) %collective-permute-start.10) | collective-permute-done | bytes 426016 | tf_op jit(solution)/shard_map/ppermute | solution.py:471
  55.5 2.2 %collective-permute-done.11 = bf16[4,208,128]{2,1,0:T(8,128)(2,1)S(1)} collective-permute-done((bf16[4,208,128]{2,1,0:T(8,128)(2,1)S(1)}, bf16[4,208,128]{2,1,0:T(8,128)(2,1)S(1)}, u32[]{:S(2)}, u32[]{:S(2)}) %collective-permute-start.11) | collective-permute-done | bytes 213024 | tf_op jit(solution)/shard_map/ppermute | solution.py:471
  57.8 3.4 %collective-permute-start.14 = (bf16[208,128]{1,0:T(8,128)(2,1)S(1)}, bf16[208,128]{1,0:T(8,128)(2,1)S(1)}, u32[]{:S(2)}, u32[]{:S(2)}) collective-permute-start(bf16[208,128]{1,0:T(8,128)(2,1)S(1)} %get-tuple-element.127), channel_id=1, source_target_pairs={{0,24},{1,25},{2,26},{3,27},{4,28},{5,29},{6,30},{7,31},{8,16},{9,... | collective-permute-start | bytes 159752 | tf_op jit(solution)/shard_map/ppermute | solution.py:471
  73.0 4.2 %collective-permute-done.39 = bf16[4,256,128]{2,1,0:T(8,128)(2,1)S(1)} collective-permute-done((bf16[4,256,128]{2,1,0:T(8,128)(2,1)S(1)}, bf16[4,256,128]{2,1,0:T(8,128)(2,1)S(1)}, u32[]{:S(2)}, u32[]{:S(2)}) %collective-permute-start.39) | collective-permute-done | bytes 262176 | tf_op jit(solution)/shard_map/ppermute | solution.py:471
  89.6 2.1 %collective-permute-done.44 = bf16[256,128]{1,0:T(8,128)(2,1)S(1)} collective-permute-done((bf16[256,128]{1,0:T(8,128)(2,1)S(1)}, bf16[256,128]{1,0:T(8,128)(2,1)S(1)}, u32[]{:S(2)}, u32[]{:S(2)}) %collective-permute-start.44) | collective-permute-done | bytes 65568 | tf_op jit(solution)/shard_map/ppermute | solution.py:471
  94.7 2.2 %collective-permute-start.26 = (bf16[320,128]{1,0:T(8,128)(2,1)S(1)}, bf16[320,128]{1,0:T(8,128)(2,1)S(1)}, u32[]{:S(2)}, u32[]{:S(2)}) collective-permute-start(bf16[320,128]{1,0:T(8,128)(2,1)S(1)} %get-tuple-element.120), channel_id=1, source_target_pairs={{0,8},{1,9},{2,10},{3,11},{4,12},{5,13},{6,14},{7,15},{8,0},{9,1},... | collective-permute-start | bytes 245768 | tf_op jit(solution)/shard_map/ppermute | solution.py:471
  96.9 2.0 %collective-permute-done.28 = bf16[320,128]{1,0:T(8,128)(2,1)S(1)} collective-permute-done((bf16[320,128]{1,0:T(8,128)(2,1)S(1)}, bf16[320,128]{1,0:T(8,128)(2,1)S(1)}, u32[]{:S(2)}, u32[]{:S(2)}) %collective-permute-start.28) | collective-permute-done | bytes 81952 | tf_op jit(solution)/shard_map/ppermute | solution.py:471
  98.9 2.4 %collective-permute-done.27 = bf16[320,128]{1,0:T(8,128)(2,1)S(1)} collective-permute-done((bf16[320,128]{1,0:T(8,128)(2,1)S(1)}, bf16[320,128]{1,0:T(8,128)(2,1)S(1)}, u32[]{:S(2)}, u32[]{:S(2)}) %collective-permute-start.27) | collective-permute-done | bytes 81952 | tf_op jit(solution)/shard_map/ppermute | solution.py:471
  101.4 2.1 %collective-permute-start.31 = (bf16[320,128]{1,0:T(8,128)(2,1)S(1)}, bf16[320,128]{1,0:T(8,128)(2,1)S(1)}, u32[]{:S(2)}, u32[]{:S(2)}) collective-permute-start(bf16[320,128]{1,0:T(8,128)(2,1)S(1)} %get-tuple-element.111), channel_id=1, source_target_pairs={{0,24},{1,25},{2,26},{3,27},{4,28},{5,29},{6,30},{7,31},{8,16},{9,... | collective-permute-start | bytes 245768 | tf_op jit(solution)/shard_map/ppermute | solution.py:471
  106.6 2.9 %collective-permute-done.30 = bf16[320,128]{1,0:T(8,128)(2,1)S(1)} collective-permute-done((bf16[320,128]{1,0:T(8,128)(2,1)S(1)}, bf16[320,128]{1,0:T(8,128)(2,1)S(1)}, u32[]{:S(2)}, u32[]{:S(2)}) %collective-permute-start.30) | collective-permute-done | bytes 81952 | tf_op jit(solution)/shard_map/ppermute | solution.py:471
  109.6 2.7 %collective-permute-start.32 = (bf16[4,320,128]{2,1,0:T(8,128)(2,1)S(1)}, bf16[4,320,128]{2,1,0:T(8,128)(2,1)S(1)}, u32[]{:S(2)}, u32[]{:S(2)}) collective-permute-start(bf16[4,320,128]{2,1,0:T(8,128)(2,1)S(1)} %pad_maximum_fusion.refs_0_), channel_id=1, source_target_pairs={{0,4},{1,3},{2,6},{3,1},{4,0},{5,7},{6,2},{7,5},{8,12},{9,11},{10,... | collective-permute-start | bytes 983048 | tf_op jit(solution)/shard_map/ppermute | solution.py:471
  112.3 4.4 %collective-permute-done.32.refs_1_ = bf16[4,320,128]{2,1,0:T(8,128)(2,1)S(1)} collective-permute-done((bf16[4,320,128]{2,1,0:T(8,128)(2,1)S(1)}, bf16[4,320,128]{2,1,0:T(8,128)(2,1)S(1)}, u32[]{:S(2)}, u32[]{:S(2)}) %collective-permute-start.32) | collective-permute-done | bytes 327712 | tf_op jit(solution)/shard_map/ppermute | solution.py:471
  116.8 2.9 %collective-permute-start.33 = (bf16[8,320,128]{2,1,0:T(8,128)(2,1)S(1)}, bf16[8,320,128]{2,1,0:T(8,128)(2,1)S(1)}, u32[]{:S(2)}, u32[]{:S(2)}) collective-permute-start(bf16[8,320,128]{2,1,0:T(8,128)(2,1)S(1)} %constant_dynamic-update-slice_fusion.5), channel_id=1, source_target_pairs={{0,2},{1,5},{2,0},{3,7},{4,6},{5,1},{6,4},{7,3},{8,10},{9,13},{10,... | collective-permute-start | bytes 1966088 | tf_op jit(solution)/shard_map/ppermute | solution.py:471
  119.8 13.9 %collective-permute-start.6 = (bf16[128,512]{1,0:T(8,128)(2,1)S(1)}, bf16[128,512]{1,0:T(8,128)(2,1)S(1)}, u32[]{:S(2)}, u32[]{:S(2)}) collective-permute-start(bf16[128,512]{1,0:T(8,128)(2,1)S(1)} %get-tuple-element.84), channel_id=1, source_target_pairs={{0,1},{1,0},{2,3},{3,2},{4,5},{5,4},{6,7},{7,6},{8,9},{9,8},{10,11... | collective-permute-start | bytes 393224 | tf_op jit(solution)/shard_map/ppermute | solution.py:471
  135.2 4.1 %collective-permute-done.7.refs_2_ = bf16[128,512]{1,0:T(8,128)(2,1)S(1)} collective-permute-done((bf16[128,512]{1,0:T(8,128)(2,1)S(1)}, bf16[128,512]{1,0:T(8,128)(2,1)S(1)}, u32[]{:S(2)}, u32[]{:S(2)}) %collective-permute-start.7) | collective-permute-done | bytes 131104 | tf_op jit(solution)/shard_map/ppermute | solution.py:471
  139.3 12.3 %collective-permute-start.8 = (bf16[128,512]{1,0:T(8,128)(2,1)S(1)}, bf16[128,512]{1,0:T(8,128)(2,1)S(1)}, u32[]{:S(2)}, u32[]{:S(2)}) collective-permute-start(bf16[128,512]{1,0:T(8,128)(2,1)S(1)} %get-tuple-element.86), channel_id=1, source_target_pairs={{0,3},{1,2},{2,1},{3,0},{4,7},{5,6},{6,5},{7,4},{8,11},{9,10},{10,... | collective-permute-start | bytes 393224 | tf_op jit(solution)/shard_map/ppermute | solution.py:471
  152.1 3.8 %collective-permute-done.8.refs_3_ = bf16[128,512]{1,0:T(8,128)(2,1)S(1)} collective-permute-done((bf16[128,512]{1,0:T(8,128)(2,1)S(1)}, bf16[128,512]{1,0:T(8,128)(2,1)S(1)}, u32[]{:S(2)}, u32[]{:S(2)}) %collective-permute-start.8) | collective-permute-done | bytes 131104 | tf_op jit(solution)/shard_map/ppermute | solution.py:471
  160.2 2.6 %gather_proj.1 = (f32[512,1536]{1,0:T(8,128)}, f32[1,512]{1,0:T(1,128)}, f32[1,512]{1,0:T(1,128)}, f32[1,512]{1,0:T(1,128)}, f32[1,512]{1,0:T(1,128)}, /*index=5...) custom-call(s32[6]{0:T(128)S(1)} %stack.72.meta, ...), custom_call_target="tpu_custom_call" | custom-call | bytes 4876312 | tf_op jit(solution)/shard_map/gather_proj/pallas_call | solution.py:403
  162.8 3.0 %gather_down.1 = f32[2048,512]{1,0:T(8,128)} custom-call(s32[6]{0:T(128)S(1)} %stack.72.meta, bf16[4,256,128]{2,1,0:T(8,128)(2,1)S(1)} %pad_maximum_fusion.1.refs_0_, bf16[4,256,128]{2,1,0:T(8,128)(2,1)S(1)} %collective-permute-done.46.refs_1_, bf16[8,256,128]{2,1,0:T(8,128)(2,1)S(1)} %collective-permute-done.47.refs_2_, ...), custom_call_target="tpu_custom_call" | custom-call | bytes 6291480 | tf_op jit(solution)/shard_map/gather_down/pallas_call | solution.py:403
  165.8 3.5 %gather_up.1 = (f32[512,2048]{1,0:T(8,128)}, f32[512,512]{1,0:T(8,128)}) custom-call(s32[6]{0:T(128)S(1)} %stack.72.meta, bf16[4,320,128]{2,1,0:T(8,128)(2,1)S(1)} %pad_maximum_fusion.refs_0_, bf16[4,320,128]{2,1,0:T(8,128)(2,1)S(1)} %collective-permute-done.32.refs_1_, bf16[8,320,128]{2,1,0:T(8,128)(2,1)S(1)} %collective-permute-done.33.refs_2_, ...), custom_call_target="tpu_custom_call" | custom-call | bytes 7864344 | tf_op jit(solution)/shard_map/gather_up/pallas_call | solution.py:403
  (151 shorter events, 62.9 us)
Async XLA Ops:
  8.0 11.3 %collective-permute-start.3 = (bf16[80,512]{1,0:T(8,128)(2,1)S(1)}, bf16[80,512]{1,0:T(8,128)(2,1)S(1)}, u32[]{:S(2)}, u32[]{:S(2)}) collective-permute-start(bf16[80,512]{1,0:T(8,128)(2,1)S(1)} %get-tuple-element.67), channel_id=1, source_target_pairs={{0,1},{1,0},{2,3},{3,2},{4,5},{5,4},{6,7},{7,6},{8,9},{9,8},{10,11... | collective-permute-start | bytes 245768 | tf_op jit(solution)/shard_map/ppermute | solution.py:471
  8.5 10.8 %collective-permute-start.4 = (bf16[80,512]{1,0:T(8,128)(2,1)S(1)}, bf16[80,512]{1,0:T(8,128)(2,1)S(1)}, u32[]{:S(2)}, u32[]{:S(2)}) collective-permute-start(bf16[80,512]{1,0:T(8,128)(2,1)S(1)} %get-tuple-element.68), channel_id=1, source_target_pairs={{0,2},{1,3},{2,0},{3,1},{4,6},{5,7},{6,4},{7,5},{8,10},{9,11},{10,... | collective-permute-start | bytes 245768 | tf_op jit(solution)/shard_map/ppermute | solution.py:471
  10.8 8.6 %collective-permute-start.5 = (bf16[80,512]{1,0:T(8,128)(2,1)S(1)}, bf16[80,512]{1,0:T(8,128)(2,1)S(1)}, u32[]{:S(2)}, u32[]{:S(2)}) collective-permute-start(bf16[80,512]{1,0:T(8,128)(2,1)S(1)} %get-tuple-element.69), channel_id=1, source_target_pairs={{0,3},{1,2},{2,1},{3,0},{4,7},{5,6},{6,5},{7,4},{8,11},{9,10},{10,... | collective-permute-start | bytes 245768 | tf_op jit(solution)/shard_map/ppermute | solution.py:471
  11.1 8.2 %collective-permute-start.1 = (bf16[64,512]{1,0:T(8,128)(2,1)S(1)}, bf16[64,512]{1,0:T(8,128)(2,1)S(1)}, u32[]{:S(2)}, u32[]{:S(2)}) collective-permute-start(bf16[64,512]{1,0:T(8,128)(2,1)S(1)} %get-tuple-element.64), channel_id=1, source_target_pairs={{0,2},{1,3},{2,0},{3,1},{4,6},{5,7},{6,4},{7,5},{8,10},{9,11},{10,... | collective-permute-start | bytes 196616 | tf_op jit(solution)/shard_map/ppermute | solution.py:471
  42.7 11.2 %collective-permute-start.37 = (bf16[16,256,128]{2,1,0:T(8,128)(2,1)S(1)}, bf16[16,256,128]{2,1,0:T(8,128)(2,1)S(1)}, u32[]{:S(2)}, u32[]{:S(2)}) collective-permute-start(bf16[16,256,128]{2,1,0:T(8,128)(2,1)S(1)} %copy-done.10), channel_id=1, source_target_pairs={{0,1},{1,0},{2,3},{3,2},{4,5},{5,4},{6,7},{7,6},{8,9},{9,8},{10,11... | collective-permute-start | bytes 3145736 | tf_op jit(solution)/shard_map/ppermute | solution.py:471
  45.2 7.3 %collective-permute-start.10 = (bf16[8,208,128]{2,1,0:T(8,128)(2,1)S(1)}, bf16[8,208,128]{2,1,0:T(8,128)(2,1)S(1)}, u32[]{:S(2)}, u32[]{:S(2)}) collective-permute-start(bf16[8,208,128]{2,1,0:T(8,128)(2,1)S(1)} %get-tuple-element.119), channel_id=1, source_target_pairs={{0,2},{1,5},{2,0},{3,7},{4,6},{5,1},{6,4},{7,3},{8,10},{9,13},{10,... | collective-permute-start | bytes 1277960 | tf_op jit(solution)/shard_map/ppermute | solution.py:471
  46.5 15.0 %collective-permute-start.23 = (bf16[16,320,128]{2,1,0:T(8,128)(2,1)S(1)}, bf16[16,320,128]{2,1,0:T(8,128)(2,1)S(1)}, u32[]{:S(2)}, u32[]{:S(2)}) collective-permute-start(bf16[16,320,128]{2,1,0:T(8,128)(2,1)S(1)} %get-tuple-element.98), channel_id=1, source_target_pairs={{0,1},{1,0},{2,3},{3,2},{4,5},{5,4},{6,7},{7,6},{8,9},{9,8},{10,11... | collective-permute-start | bytes 3932168 | tf_op jit(solution)/shard_map/ppermute | solution.py:471
  54.2 14.6 %collective-permute-start.38 = (bf16[8,256,128]{2,1,0:T(8,128)(2,1)S(1)}, bf16[8,256,128]{2,1,0:T(8,128)(2,1)S(1)}, u32[]{:S(2)}, u32[]{:S(2)}) collective-permute-start(bf16[8,256,128]{2,1,0:T(8,128)(2,1)S(1)} %get-tuple-element.117), channel_id=1, source_target_pairs={{0,2},{1,5},{2,0},{3,7},{4,6},{5,1},{6,4},{7,3},{8,10},{9,13},{10,... | collective-permute-start | bytes 1572872 | tf_op jit(solution)/shard_map/ppermute | solution.py:471
  61.9 19.1 %collective-permute-start.24 = (bf16[8,320,128]{2,1,0:T(8,128)(2,1)S(1)}, bf16[8,320,128]{2,1,0:T(8,128)(2,1)S(1)}, u32[]{:S(2)}, u32[]{:S(2)}) collective-permute-start(bf16[8,320,128]{2,1,0:T(8,128)(2,1)S(1)} %get-tuple-element.115), channel_id=1, source_target_pairs={{0,2},{1,5},{2,0},{3,7},{4,6},{5,1},{6,4},{7,3},{8,10},{9,13},{10,... | collective-permute-start | bytes 1966088 | tf_op jit(solution)/shard_map/ppermute | solution.py:471
  68.8 8.5 %collective-permute-start.39 = (bf16[4,256,128]{2,1,0:T(8,128)(2,1)S(1)}, bf16[4,256,128]{2,1,0:T(8,128)(2,1)S(1)}, u32[]{:S(2)}, u32[]{:S(2)}) collective-permute-start(bf16[4,256,128]{2,1,0:T(8,128)(2,1)S(1)} %add_convert_fusion.10), channel_id=1, source_target_pairs={{0,4},{1,3},{2,6},{3,1},{4,0},{5,7},{6,2},{7,5},{8,12},{9,11},{10,... | collective-permute-start | bytes 786440 | tf_op jit(solution)/shard_map/ppermute | solution.py:471
  71.7 15.7 %collective-permute-start.18 = (bf16[4,208,128]{2,1,0:T(8,128)(2,1)S(1)}, bf16[4,208,128]{2,1,0:T(8,128)(2,1)S(1)}, u32[]{:S(2)}, u32[]{:S(2)}) collective-permute-start(bf16[4,208,128]{2,1,0:T(8,128)(2,1)S(1)} %pad_maximum_fusion.2.refs_0_), channel_id=1, source_target_pairs={{0,4},{1,3},{2,6},{3,1},{4,0},{5,7},{6,2},{7,5},{8,12},{9,11},{10,... | collective-permute-start | bytes 638984 | tf_op jit(solution)/shard_map/ppermute | solution.py:471
  81.1 12.0 %collective-permute-start.25 = (bf16[4,320,128]{2,1,0:T(8,128)(2,1)S(1)}, bf16[4,320,128]{2,1,0:T(8,128)(2,1)S(1)}, u32[]{:S(2)}, u32[]{:S(2)}) collective-permute-start(bf16[4,320,128]{2,1,0:T(8,128)(2,1)S(1)} %add_convert_fusion.7), channel_id=1, source_target_pairs={{0,4},{1,3},{2,6},{3,1},{4,0},{5,7},{6,2},{7,5},{8,12},{9,11},{10,... | collective-permute-start | bytes 983048 | tf_op jit(solution)/shard_map/ppermute | solution.py:471
  87.5 64.2 %collective-permute-start.19 = (bf16[8,208,128]{2,1,0:T(8,128)(2,1)S(1)}, bf16[8,208,128]{2,1,0:T(8,128)(2,1)S(1)}, u32[]{:S(2)}, u32[]{:S(2)}) collective-permute-start(bf16[8,208,128]{2,1,0:T(8,128)(2,1)S(1)} %constant_dynamic-update-slice_fusion), channel_id=1, source_target_pairs={{0,2},{1,5},{2,0},{3,7},{4,6},{5,1},{6,4},{7,3},{8,10},{9,13},{10,... | collective-permute-start | bytes 1277960 | tf_op jit(solution)/shard_map/ppermute | solution.py:471
  91.7 28.0 %collective-permute-start.46 = (bf16[4,256,128]{2,1,0:T(8,128)(2,1)S(1)}, bf16[4,256,128]{2,1,0:T(8,128)(2,1)S(1)}, u32[]{:S(2)}, u32[]{:S(2)}) collective-permute-start(bf16[4,256,128]{2,1,0:T(8,128)(2,1)S(1)} %pad_maximum_fusion.1.refs_0_), channel_id=1, source_target_pairs={{0,4},{1,3},{2,6},{3,1},{4,0},{5,7},{6,2},{7,5},{8,12},{9,11},{10,... | collective-permute-start | bytes 786440 | tf_op jit(solution)/shard_map/ppermute | solution.py:471
  109.6 7.2 %collective-permute-start.32 = (bf16[4,320,128]{2,1,0:T(8,128)(2,1)S(1)}, bf16[4,320,128]{2,1,0:T(8,128)(2,1)S(1)}, u32[]{:S(2)}, u32[]{:S(2)}) collective-permute-start(bf16[4,320,128]{2,1,0:T(8,128)(2,1)S(1)} %pad_maximum_fusion.refs_0_), channel_id=1, source_target_pairs={{0,4},{1,3},{2,6},{3,1},{4,0},{5,7},{6,2},{7,5},{8,12},{9,11},{10,... | collective-permute-start | bytes 983048 | tf_op jit(solution)/shard_map/ppermute | solution.py:471
  116.8 34.8 %collective-permute-start.33 = (bf16[8,320,128]{2,1,0:T(8,128)(2,1)S(1)}, bf16[8,320,128]{2,1,0:T(8,128)(2,1)S(1)}, u32[]{:S(2)}, u32[]{:S(2)}) collective-permute-start(bf16[8,320,128]{2,1,0:T(8,128)(2,1)S(1)} %constant_dynamic-update-slice_fusion.5), channel_id=1, source_target_pairs={{0,2},{1,5},{2,0},{3,7},{4,6},{5,1},{6,4},{7,3},{8,10},{9,13},{10,... | collective-permute-start | bytes 1966088 | tf_op jit(solution)/shard_map/ppermute | solution.py:471
  119.7 36.7 %collective-permute-start.47 = (bf16[8,256,128]{2,1,0:T(8,128)(2,1)S(1)}, bf16[8,256,128]{2,1,0:T(8,128)(2,1)S(1)}, u32[]{:S(2)}, u32[]{:S(2)}) collective-permute-start(bf16[8,256,128]{2,1,0:T(8,128)(2,1)S(1)} %constant_dynamic-update-slice_fusion.10), channel_id=1, source_target_pairs={{0,2},{1,5},{2,0},{3,7},{4,6},{5,1},{6,4},{7,3},{8,10},{9,13},{10,... | collective-permute-start | bytes 1572872 | tf_op jit(solution)/shard_map/ppermute | solution.py:471
  119.8 15.1 %collective-permute-start.6 = (bf16[128,512]{1,0:T(8,128)(2,1)S(1)}, bf16[128,512]{1,0:T(8,128)(2,1)S(1)}, u32[]{:S(2)}, u32[]{:S(2)}) collective-permute-start(bf16[128,512]{1,0:T(8,128)(2,1)S(1)} %get-tuple-element.84), channel_id=1, source_target_pairs={{0,1},{1,0},{2,3},{3,2},{4,5},{5,4},{6,7},{7,6},{8,9},{9,8},{10,11... | collective-permute-start | bytes 393224 | tf_op jit(solution)/shard_map/ppermute | solution.py:471
  134.9 21.4 %collective-permute-start.20 = (bf16[4,208,128]{2,1,0:T(8,128)(2,1)S(1)}, bf16[4,208,128]{2,1,0:T(8,128)(2,1)S(1)}, u32[]{:S(2)}, u32[]{:S(2)}) collective-permute-start(bf16[4,208,128]{2,1,0:T(8,128)(2,1)S(1)} %pad_maximum_fusion.2.refs_0_), channel_id=1, source_target_pairs={{0,1},{1,0},{2,3},{3,2},{4,5},{5,4},{6,7},{7,6},{8,9},{9,8},{10,11... | collective-permute-start | bytes 638984 | tf_op jit(solution)/shard_map/ppermute | solution.py:471
  139.3 16.7 %collective-permute-start.8 = (bf16[128,512]{1,0:T(8,128)(2,1)S(1)}, bf16[128,512]{1,0:T(8,128)(2,1)S(1)}, u32[]{:S(2)}, u32[]{:S(2)}) collective-permute-start(bf16[128,512]{1,0:T(8,128)(2,1)S(1)} %get-tuple-element.86), channel_id=1, source_target_pairs={{0,3},{1,2},{2,1},{3,0},{4,7},{5,6},{6,5},{7,4},{8,11},{9,10},{10,... | collective-permute-start | bytes 393224 | tf_op jit(solution)/shard_map/ppermute | solution.py:471
  151.6 6.7 %collective-permute-start.22 = (bf16[8,208,128]{2,1,0:T(8,128)(2,1)S(1)}, bf16[8,208,128]{2,1,0:T(8,128)(2,1)S(1)}, u32[]{:S(2)}, u32[]{:S(2)}) collective-permute-start(bf16[8,208,128]{2,1,0:T(8,128)(2,1)S(1)} %collective-permute-done.19.refs_2_), channel_id=1, source_target_pairs={{0,1},{1,0},{2,3},{3,2},{4,5},{5,4},{6,7},{7,6},{8,9},{9,8},{10,11... | collective-permute-start | bytes 1277960 | tf_op jit(solution)/shard_map/ppermute | solution.py:471
  151.6 14.1 %collective-permute-start.36 = (bf16[8,320,128]{2,1,0:T(8,128)(2,1)S(1)}, bf16[8,320,128]{2,1,0:T(8,128)(2,1)S(1)}, u32[]{:S(2)}, u32[]{:S(2)}) collective-permute-start(bf16[8,320,128]{2,1,0:T(8,128)(2,1)S(1)} %collective-permute-done.33.refs_2_), channel_id=1, source_target_pairs={{0,1},{1,0},{2,3},{3,2},{4,5},{5,4},{6,7},{7,6},{8,9},{9,8},{10,11... | collective-permute-start | bytes 1966088 | tf_op jit(solution)/shard_map/ppermute | solution.py:471
  157.8 8.0 %collective-permute-start.34 = (bf16[4,320,128]{2,1,0:T(8,128)(2,1)S(1)}, bf16[4,320,128]{2,1,0:T(8,128)(2,1)S(1)}, u32[]{:S(2)}, u32[]{:S(2)}) collective-permute-start(bf16[4,320,128]{2,1,0:T(8,128)(2,1)S(1)} %pad_maximum_fusion.refs_0_), channel_id=1, source_target_pairs={{0,1},{1,0},{2,3},{3,2},{4,5},{5,4},{6,7},{7,6},{8,9},{9,8},{10,11... | collective-permute-start | bytes 983048 | tf_op jit(solution)/shard_map/ppermute | solution.py:471
  158.2 7.6 %collective-permute-start.35 = (bf16[4,320,128]{2,1,0:T(8,128)(2,1)S(1)}, bf16[4,320,128]{2,1,0:T(8,128)(2,1)S(1)}, u32[]{:S(2)}, u32[]{:S(2)}) collective-permute-start(bf16[4,320,128]{2,1,0:T(8,128)(2,1)S(1)} %collective-permute-done.32.refs_1_), channel_id=1, source_target_pairs={{0,1},{1,0},{2,3},{3,2},{4,5},{5,4},{6,7},{7,6},{8,9},{9,8},{10,11... | collective-permute-start | bytes 983048 | tf_op jit(solution)/shard_map/ppermute | solution.py:471
  (38 other events, 173.7 us)

commit v2 on v1

v2 whole, which is shorter than its diff:
```python
import functools

import jax
import jax.numpy as jnp
from jax import lax
from jax.experimental import pallas as pl
from jax.experimental.pallas import tpu as pltpu
from jax.sharding import PartitionSpec as P

HEADS = 16
LANES = 128
EPS = 1e-06
LOG2E = 1.4426950408889634
BF16 = jnp.bfloat16
F32 = jnp.float32
ORDERS = (('zxy', 'zyx'), ('yxz', 'xyz'), ('xyz', 'yxz'))
TIES = (((0, 1), (3, 0)), ((1, 0), (3, 0)), ((1, 4), (5, 0)))
RESULTS = (3, 0)
WRITTEN = ()
US = {'forward': 15}
VMEM_LIMIT = 24 * 1024 * 1024


def dot(a, b):
    return jnp.dot(a, b, preferred_element_type=F32)


def dot_nt(a, b):
    return lax.dot_general(a, b, (((1,), (1,)), ((), ())), preferred_element_type=F32)


def dot_tn(a, b):
    return lax.dot_general(a, b, (((0,), (0,)), ((), ())), preferred_element_type=F32)


def row(ref):
    return ref[...].astype(F32).reshape(1, -1)


def norm_stats(rows):
    centre = jnp.mean(rows, axis=-1, keepdims=True)
    centred = rows - centre
    spread = jnp.mean(centred * centred, axis=-1, keepdims=True)
    rstd = lax.rsqrt(spread + EPS)
    return centred * rstd, rstd


def norm_back(grad_normed, xhat, rstd, gain):
    grad_xhat = grad_normed * gain
    first = jnp.mean(grad_xhat, axis=-1, keepdims=True)
    second = jnp.mean(grad_xhat * xhat, axis=-1, keepdims=True)
    return rstd * (grad_xhat - first - xhat * second)


class Pieces:
    def __init__(self, rows, cols, chips):
        self.rows = rows
        self.half = cols // 2
        self.row_blocks = min(chips, rows // 16)
        self.lane_blocks = chips // self.row_blocks
        self.height = rows // self.row_blocks
        self.width = self.half // self.lane_blocks
        self.tall = self.height * self.width // LANES


def exchanges(order, depth):
    deep = [("z", 1 << i) for i in reversed(range(depth.bit_length() - 1))]
    bits = {"x": [("x", 1)], "y": [("y", 1)], "z": deep}
    return [sum((bits[axis] for axis in axes), []) for axes in order]


def relative(core, place, chip, depth, order):
    differ = dict(zip("xyz", (a ^ b for a, b in zip(place, chip))))
    found = []
    for bits in exchanges(order, depth):
        at = 0
        for axis, bit in bits:
            at = at * 2 + ((differ[axis] & bit) // bit)
        found.append(at)
    return jnp.where(core == 0, *found)


def chip_of(index, depth):
    return index // (2 * depth), (index // depth) % 2, index % depth


def absolute(core, place, index, depth, order):
    flips = []
    for bits in exchanges(order, depth):
        flip = dict.fromkeys("xyz", 0)
        for i, (axis, bit) in enumerate(reversed(bits)):
            flip[axis] |= bit * ((index >> i) & 1)
        flips.append(flip)
    x, y, z = (
        at ^ jnp.where(core == 0, flips[0][axis], flips[1][axis]) for axis, at in zip("xyz", place)
    )
    return (x * 2 + y) * depth + z % depth


def store_pieces(out_ref, core, place, depth, order, pieces, base, value, row_start):
    for first in range(0, value.shape[0], pieces.height):
        row_block = (row_start + first) // pieces.height
        for lane_block in range(pieces.lane_blocks):
            index = row_block * pieces.lane_blocks + lane_block
            rel = relative(core, place, chip_of(index, depth), depth, order)
            for j in range(pieces.width // LANES):
                at = base + j * pieces.height
                lane = lane_block * pieces.width + j * LANES
                out_ref[rel, at : at + pieces.height, :] = value[
                    first : first + pieces.height, lane : lane + LANES
                ].astype(BF16)


def weight_grad(keep_ref, send_ref, core, place, depth, order, pieces, base, lhs, rhs_ref):
    stripe = max(pieces.height, min(512, pieces.rows))
    for out_ref, owner in ((send_ref, core ^ 1), (keep_ref, core)):
        rhs = rhs_ref[:, pl.ds(pl.multiple_of(owner * pieces.half, LANES), pieces.half)]
        for start in range(0, pieces.rows, stripe):
            value = dot_tn(lhs[:, start : start + stripe], rhs)
            store_pieces(out_ref, owner, place, depth, order, pieces, base, value, start)


def place_of():
    dp, blk = lax.axis_index("dp"), lax.axis_index("blk")
    return blk % 2, (blk // 2, dp % 2, dp // 2), blk


def fetch(sems, *pairs):
    copies = [pltpu.make_async_copy(a, b, sems.at[i]) for i, (a, b) in enumerate(pairs)]
    for copy in copies:
        copy.start()
    return [copy.wait for copy in copies]


def flag_column(flags, at):
    share = flags.shape[2]
    eye = lax.broadcasted_iota(jnp.int32, (share, share), 0) == lax.broadcasted_iota(
        jnp.int32, (share, share), 1
    )
    return jnp.sum(jnp.where(eye, flags[at], 0), axis=1, keepdims=True) == 1


def fill_kernel(count, tokens_hbm, cotangent_hbm, flags_hbm, mask_hbm, *refs):
    outs, cots = refs[:count], refs[count : 2 * count]
    tokens, cotangent, flags, mask_token, sems = refs[2 * count :]
    waits = fetch(
        sems,
        (tokens_hbm, tokens),
        (flags_hbm, flags),
        (mask_hbm, mask_token),
        (cotangent_hbm, cotangent),
    )
    for wait in waits[:3]:
        wait()
    blk = lax.axis_index("blk")
    share = tokens.shape[1]
    for k in range(count):
        at = blk ^ k
        outs[k][...] = jnp.where(
            flag_column(flags, at), row(mask_token), tokens[at].astype(F32)
        ).astype(BF16)
    waits[3]()
    for k in range(count):
        at = blk ^ k
        cots[k][:share, :] = cotangent[at]
        cots[k][share:, :] = jnp.zeros((16, cots[k].shape[1]), BF16)
        first = lax.broadcasted_iota(jnp.int32, (16, share), 0) == 0
        flag = (flags[at] == 1).astype(F32)
        cots[k][share:, :share] = jnp.where(first, flag, 0.0).astype(BF16)


GAIN1, BIAS1, B_QUERY, B_VALUE, B_OUT, GAIN2, BIAS2, B_DOWN, B_UP = range(9)
QUOTA = 15


def prefetch_kernel(images, weight_hbm, buckets_hbm, *refs):
    count = (len(refs) - 4) // 2
    weight, vecs = refs[count : count + 2]
    held, buckets, sems = refs[count + 2 : -2], refs[-2], refs[-1]
    waits = fetch(
        sems, (weight_hbm, weight), (buckets_hbm, buckets), *zip(refs[:count], held)
    )
    for wait in waits[1:]:
        wait()
    width = vecs.shape[1]
    vecs[...] = jnp.zeros(vecs.shape, F32)
    line = 0
    for ref in held:
        for at in range(0, ref.shape[0], width):
            vecs[line : line + 1, :] = row(ref)[:, at : at + width]
            line += 1
    micro = lax.axis_index("blk") // images
    quota = jnp.zeros((1, 1), jnp.int32)
    for m in range(buckets.shape[1]):
        bucket = buckets[:, m : m + 1]
        here = jnp.where(bucket == 0, 25, jnp.where(bucket == 1, 49, 64))
        quota = quota + jnp.where(micro == m, here, 0)
    vecs[QUOTA : QUOTA + 1, :] = jnp.broadcast_to(quota.astype(F32), (1, width))
    waits[0]()


def vector(rows, which):
    return rows[which : which + 1, :]


def forward_kernel(count, share, *refs):
    sources, refs = refs[:3], refs[3:]
    xs, refs = refs[:count], refs[count:]
    vecs, w_qkv = refs[:2]
    targets = refs[2:5]
    qkv_ref, p_ref, rinv_ref, o_ref, x2_ref, n2_ref, h_ref, gp_ref, sems = refs[5:]
    waits = fetch(sems, *zip(sources, targets))
    w_out, w_up, _ = targets
    quota = vecs[QUOTA : QUOTA + 1, 0:1].astype(jnp.int32)
    width = xs[0].shape[1]
    head = width // HEADS
    rows = count * share
    x = jnp.concatenate([ref[...] for ref in xs], axis=0).astype(F32)
    xhat, _ = norm_stats(x)
    n1 = (xhat * vector(vecs, GAIN1) + vector(vecs, BIAS1)).astype(BF16)
    for part in range(3):
        cols = slice(part * width, (part + 1) * width)
        value = dot(n1, w_qkv[:, cols])
        if part == 0:
            value = value + vector(vecs, B_QUERY)
        if part == 2:
            value = value + vector(vecs, B_VALUE)
        qkv_ref[:, cols] = value.astype(BF16)
    key = lax.broadcasted_iota(jnp.int32, (rows, 1), 0)
    dead = jnp.where(key % share < quota, 0.0, -1e30).astype(F32)
    lane_head = lax.broadcasted_iota(jnp.int32, (1, LANES), 1) // head
    scale = head ** (-0.5) * LOG2E
    per = LANES // head
    ones = jnp.ones((rows, LANES), BF16)
    for group in range(width // LANES):
        at = group * LANES
        q = qkv_ref[:, at : at + LANES]
        keys = qkv_ref[:, width + at : width + at + LANES]
        values = jnp.concatenate(
            [qkv_ref[:, 2 * width + at : 2 * width + at + LANES], ones], axis=1
        )
        acc = jnp.zeros((rows, LANES), F32)
        racc = jnp.zeros((rows, LANES), F32)
        for i in range(per):
            here = lane_head == i
            s = dot_nt(keys * here.astype(F32).astype(BF16), q) * scale + dead
            top = jnp.max(s, axis=0, keepdims=True)
            p = jnp.exp2(s - top).astype(BF16)
            p_ref[group * per + i] = p
            both = dot_tn(p, values)
            rinv = 1.0 / both[:, LANES:]
            acc = jnp.where(here, both[:, :LANES] * rinv, acc)
            racc = jnp.where(here, rinv, racc)
        o_ref[:, at : at + LANES] = acc.astype(BF16)
        rinv_ref[:, at : at + LANES] = racc
    waits[0]()
    x2 = x + (dot(o_ref[...], w_out[...]) + vector(vecs, B_OUT))
    x2_ref[...] = x2
    xhat2, _ = norm_stats(x2)
    n2 = (xhat2 * vector(vecs, GAIN2) + vector(vecs, BIAS2)).astype(BF16)
    n2_ref[...] = n2
    hidden = w_up.shape[1]
    step = width
    waits[1]()
    for start in range(0, hidden, step):
        cols = slice(start, start + step)
        u = dot(n2, w_up[:, cols]) + vector(vecs, B_UP + start // step)
        cdf = 0.5 + 0.5 * lax.erf(u * (0.5**0.5))
        pdf = jnp.exp(-0.5 * u * u) * 0.3989422804014327
        h_ref[:, cols] = (u * cdf).astype(BF16)
        gp_ref[:, cols] = (cdf + u * pdf).astype(BF16)
    waits[2]()


def down_kernel(depth, order, down, count, share, *refs):
    cs, (vecs, h_ref, g_ref, keep_ref, send_ref) = refs[:count], refs[count:]
    core, place, _ = place_of()
    quota = vecs[QUOTA : QUOTA + 1, 0:1].astype(jnp.int32)
    live_rows = lax.broadcasted_iota(jnp.int32, (share, 1), 0) < quota
    for k in range(count):
        g_ref[k * share : (k + 1) * share, :] = jnp.where(
            live_rows, cs[k][:share, :].astype(F32), 0.0
        ).astype(BF16)
    weight_grad(keep_ref, send_ref, core, place, depth, order, down, 0, h_ref, g_ref)


def middle_kernel(
    depth,
    order,
    up,
    after,
    g_ref, gp_ref, h_ref, n2_ref, o_ref, x2_ref, vecs, w_up, w_down,
    keep_ref, send_ref, dx2_ref, dx2r_ref, out_ref, small_ref, du_ref,
):
    core, place, _ = place_of()
    g = g_ref[...]
    hidden = w_up.shape[1]
    width = g.shape[1]
    step = 512
    small_ref[...] = jnp.zeros(small_ref.shape, F32)
    dn2 = jnp.zeros((g.shape[0], width), F32)
    for start in range(0, hidden, step):
        cols = slice(start, start + step)
        dh = dot_nt(g, w_down[cols, :])
        du = (dh * gp_ref[:, cols].astype(F32)).astype(BF16)
        du_ref[:, cols] = du
        small_ref[0:1, cols] = jnp.sum(du.astype(F32), axis=0, keepdims=True)
        dn2 = dn2 + dot_nt(du, w_up[:, cols])
    x2 = x2_ref[...]
    xhat, rstd = norm_stats(x2)
    gf = g.astype(F32)
    dx2 = gf + norm_back(dn2, xhat, rstd, vector(vecs, GAIN2))
    dx2_ref[...] = dx2
    dx2r = dx2.astype(BF16)
    dx2r_ref[...] = dx2r
    small_ref[1:2, 0:width] = jnp.sum(dx2r.astype(F32), axis=0, keepdims=True)
    small_ref[1:2, width : 2 * width] = jnp.sum(dn2 * xhat, axis=0, keepdims=True)
    small_ref[1:2, 2 * width : 3 * width] = jnp.sum(dn2, axis=0, keepdims=True)
    small_ref[1:2, 3 * width : 4 * width] = jnp.sum(gf, axis=0, keepdims=True)
    weight_grad(keep_ref, send_ref, core, place, depth, order, up, 0, n2_ref, du_ref)
    weight_grad(keep_ref, send_ref, core, place, depth, order, after, up.tall, o_ref, dx2r_ref)
    out_ref[...] = (x2 + (dot(h_ref[...], w_down[...]) + vector(vecs, B_DOWN))).astype(BF16)


def backward_kernel(
    depth,
    order,
    proj,
    count,
    share,
    *refs,
):
    refs = list(refs)
    xs = [refs.pop(0) for _ in range(count)]
    cs = [refs.pop(0) for _ in range(count)]
    qkv_ref, p_ref, rinv_ref, o_ref, dx2_ref, dx2r_ref, block_ref, sub_ref, vecs, w_qkv, w_out = refs[:11]
    refs = refs[11:]
    results = [refs.pop(0) for _ in range(count)]
    keep_ref, send_ref, dqkv_ref, small = refs
    core, place, _ = place_of()
    rows = count * share
    width = xs[0].shape[1]
    head = width // HEADS
    per = LANES // head
    d_o = dot_nt(dx2r_ref[...], w_out[...]).astype(BF16).astype(F32)
    d_scaled = d_o * rinv_ref[...]
    product = (d_scaled * o_ref[...].astype(F32)).astype(BF16)
    d_scaled = d_scaled.astype(BF16)
    lane_head = lax.broadcasted_iota(jnp.int32, (1, LANES), 1) // head
    minus = jnp.full((rows, LANES), -1.0, BF16)
    scale = head ** (-0.5)
    for group in range(width // LANES):
        at = group * LANES
        q = qkv_ref[:, at : at + LANES]
        keys = qkv_ref[:, width + at : width + at + LANES]
        values = qkv_ref[:, 2 * width + at : 2 * width + at + LANES]
        ds_o = d_scaled[:, at : at + LANES]
        rhs = jnp.concatenate([ds_o, product[:, at : at + LANES]], axis=1)
        dq = jnp.zeros((rows, LANES), F32)
        dk = jnp.zeros((rows, LANES), F32)
        dv = jnp.zeros((rows, LANES), F32)
        for i in range(per):
            here = lane_head == i
            mask = here.astype(F32).astype(BF16)
            lhs = jnp.concatenate([values * mask, minus * mask], axis=1)
            p = p_ref[group * per + i]
            ds = (p.astype(F32) * dot_nt(lhs, rhs)).astype(BF16)
            dq = jnp.where(here, dot_tn(ds, keys), dq)
            dk = jnp.where(here, dot(ds, q), dk)
            dv = jnp.where(here, dot(p, ds_o), dv)
        dqkv_ref[:, at : at + LANES] = (dq * scale).astype(BF16)
        dqkv_ref[:, width + at : width + at + LANES] = (dk * scale).astype(BF16)
        dqkv_ref[:, 2 * width + at : 2 * width + at + LANES] = dv.astype(BF16)
    x = jnp.concatenate([ref[...] for ref in xs], axis=0).astype(F32)
    xhat, rstd = norm_stats(x)
    gain = vector(vecs, GAIN1)
    n1 = (xhat * gain + vector(vecs, BIAS1)).astype(BF16)
    weight_grad(keep_ref, send_ref, core, place, depth, order, proj, 0, n1, dqkv_ref)
    dn1 = dot_nt(dqkv_ref[...], w_qkv[...])
    dx = (dx2_ref[...] + norm_back(dn1, xhat, rstd, gain)).astype(BF16)
    d_mask = jnp.zeros((16, width), F32)
    for k in range(count):
        part = dx[k * share : (k + 1) * share, :]
        d_mask = d_mask + dot(cs[k][share : share + 16, :share], part)
        results[k][:share, :] = block_ref[k * share : (k + 1) * share, :]
        results[k][share:, :] = part
    blocks = small.shape[0]
    small[...] = jnp.zeros(small.shape, F32)
    wide = [
        d_mask[0:1, :],
        jnp.sum(dn1 * xhat, axis=0, keepdims=True),
        jnp.sum(dn1, axis=0, keepdims=True),
        jnp.sum(dqkv_ref[:, :width].astype(F32), axis=0, keepdims=True),
        jnp.sum(dqkv_ref[:, 2 * width :].astype(F32), axis=0, keepdims=True),
        sub_ref[1:2, :],
        sub_ref[0:1, :],
    ]
    lines = [v[:, j : j + LANES] for v in wide for j in range(0, v.shape[1], LANES)]
    each = -(-len(lines) // blocks)
    for i, line in enumerate(lines):
        small[i // each, i % each : i % each + 1, :] = line
    chips = blocks // 2
    for out_ref, owner in ((send_ref, core ^ 1), (keep_ref, core)):
        for index in range(chips):
            rel = relative(owner, place, chip_of(index, depth), depth, order)
            out_ref[rel, proj.tall : proj.tall + 16, :] = small[owner * chips + index].astype(BF16)


def gather_kernel(depth, order, layout, scale, small_at, sizes, *refs):
    count = len(layout)
    halves, outs = refs[:4], refs[4 : 4 + count]
    vectors = refs[4 + count : 4 + count + len(sizes)]
    held = refs[4 + count + len(sizes) : -2]
    small, sems = refs[-2:]
    core, place, _ = place_of()
    half = halves[0].shape[0]
    chips = 2 * half
    copies = []
    for side, owner in ((0, core), (1, core ^ 1)):
        for rel in range(chips):
            ref, at_block = halves[2 * side + rel // half], rel % half
            index = absolute(owner, place, rel, depth, order)
            slot = side * chips + rel
            for which, (pieces, base) in enumerate(layout):
                for j in range(pieces.width // LANES):
                    at = base + j * pieces.height
                    held[which][slot, :, j * LANES : (j + 1) * LANES] = (
                        ref[at_block, at : at + pieces.height, :].astype(F32) * scale
                    )
                top = pl.multiple_of((index // pieces.lane_blocks) * pieces.height, 16)
                lane = owner * pieces.half + (index % pieces.lane_blocks) * pieces.width
                copy = pltpu.make_async_copy(
                    held[which].at[slot],
                    outs[which].at[
                        pl.ds(top, pieces.height),
                        pl.ds(pl.multiple_of(lane, LANES), pieces.width),
                    ],
                    sems.at[which, slot],
                )
                copy.start()
                copies.append(copy)
            if sizes:
                small[owner * chips + index] = (
                    ref[at_block, small_at : small_at + 16, :].astype(F32) * scale
                )
    lines = sum(sizes) // LANES
    each = max(1, -(-lines // (2 * chips)))
    line = 0
    for out, size in zip(vectors, sizes):
        for j in range(size // LANES):
            out[j * LANES : (j + 1) * LANES] = small[
                line // each, line % each : line % each + 1, :
            ].reshape(LANES)
            line += 1
    for copy in copies:
        copy.wait()


def finish_kernel(flags, *refs):
    block_out, token_grad = refs[-2:]
    share = block_out.shape[1]
    blk = lax.axis_index("blk")
    for k, ref in enumerate(refs[:-2]):
        at = blk ^ k
        block_out[at] = ref[:share, :]
        token_grad[at] = jnp.where(flag_column(flags, at), 0.0, ref[share:, :].astype(F32))


WHOLE = pl.BlockSpec(memory_space=pltpu.VMEM)
FAR = pl.BlockSpec(memory_space=pltpu.HBM)


def call(kernel, outs, *args, scratch=(), far=0, far_outs=0, name=None):
    args = list(args)
    for i in range(far):
        args[i] = pltpu.with_memory_space_constraint(args[i], pltpu.HBM)
    return pl.pallas_call(
        kernel,
        out_shape=tuple(outs),
        in_specs=[FAR] * far + [WHOLE] * (len(args) - far),
        out_specs=tuple([FAR] * far_outs + [WHOLE] * (len(outs) - far_outs)),
        scratch_shapes=list(scratch),
        compiler_params=pltpu.CompilerParams(vmem_limit_bytes=VMEM_LIMIT),
        cost_estimate=pl.CostEstimate(
            flops=int(US.get(name, 0) * 1.15e9), bytes_accessed=0, transcendentals=0
        ),
        name=name,
    )(*args)


def like(array):
    return pltpu.VMEM(array.shape, array.dtype)


def after(value, *others):
    return lax.optimization_barrier((value, *others))[0]


def shape(dims, kind=BF16):
    return jax.ShapeDtypeStruct(tuple(dims), kind)


def add(*parts):
    total = parts[0].astype(F32)
    for part in parts[1:]:
        total = total + part.astype(F32)
    return total.astype(BF16)


def shards(
    dp_size,
    blk_size,
    tokens,
    mask_flags,
    buckets,
    cotangent,
    mask_token,
    norm1_gain,
    norm1_bias,
    w_qkv,
    b_query,
    b_value,
    w_out,
    b_out,
    norm2_gain,
    norm2_bias,
    w_up,
    b_up,
    w_down,
    b_down,
):
    micro_count, images, share, width = tokens.shape
    hidden = w_up.shape[1]
    count = micro_count * images
    rows = count * share
    deep = dp_size // 2
    depth = deep // 2
    chips = 4 * depth
    total_images = float(micro_count * images * dp_size)

    def send(value, change):
        table = []
        for d in range(dp_size):
            for b in range(blk_size):
                nz, ny, nx, nc = change(d // 2, d % 2, b // 2, b % 2)
                table.append((d * blk_size + b, (nz * 2 + ny) * blk_size + nx * 2 + nc))
        return lax.ppermute(value, ("dp", "blk"), table)

    def core_pair(z, y, x, c):
        return z, y, x, c ^ 1

    def depth_pair(k):
        return lambda z, y, x, c: (z ^ k, y, x, c)

    def image_pair(k):
        return lambda z, y, x, c: (z, y, x ^ (k >> 1), c ^ (k & 1))

    def halving(order):
        def flip(bits):
            def change(z, y, x, c):
                axis, bit = bits[c]
                at = {"z": z, "y": y, "x": x}
                at[axis] ^= bit
                return at["z"], at["y"], at["x"], c

            return change

        return [flip(bits) for bits in zip(*exchanges(order, depth))]

    class Sum:
        def __init__(self, keep, sent, order):
            self.order = order
            self.pairs = halving(order)
            self.keep, self.sent = keep, sent
            self.step = 0

        def cores(self, *behind):
            self.got = send(after(self.sent, *behind) if behind else self.sent, core_pair)
            return self

        def advance(self, *behind):
            count = len(self.pairs)
            if self.step < count:
                half = self.keep.shape[0] // 2
                away = add(self.keep[half:], self.got[half:])
                self.keep = add(self.keep[:half], self.got[:half])
                change = self.pairs[self.step]
            elif self.step == count:
                away = self.keep = add(self.keep, self.got)
                change = depth_pair(depth)
            else:
                if self.step == count + 1:
                    self.keep = add(self.keep, self.got)
                else:
                    self.keep = jnp.concatenate([self.keep, self.got])
                away = self.keep
                change = self.pairs[2 * count - self.step]
            self.got = send(after(away, *behind) if behind else away, change)
            self.step += 1

        @property
        def left(self):
            return 2 * len(self.pairs) + 1 - self.step

        def finish(self):
            mine = (self.keep, self.got)
            return mine + tuple(send(a, core_pair) for a in mine)

    down = Pieces(hidden, width, chips)
    up = Pieces(width, hidden, chips)
    out = Pieces(width, width, chips)
    proj = Pieces(width, 3 * width, chips)
    dma = pltpu.SemaphoreType.DMA

    tokens_in = tokens.reshape(count, share, width)
    flags = mask_flags.reshape(count, 1, share)
    cots_in = cotangent.reshape(count, share, width)
    filled = call(
        functools.partial(fill_kernel, count),
        [shape((share, width))] * count + [shape((share + 16, width))] * count,
        tokens_in,
        cots_in,
        flags,
        mask_token,
        far=4,
        scratch=[like(tokens_in), like(cots_in), like(flags), like(mask_token), dma((4,))],
        name="fill",
    )
    xs = list(filled[:1]) + [send(filled[k], image_pair(k)) for k in range(1, count)]
    cs = [filled[count]] + [
        send(after(filled[count + k], xs[1]), image_pair(k)) for k in range(1, count)
    ]
    vectors = [norm1_gain, norm1_bias, b_query, b_value, b_out, norm2_gain, norm2_bias, b_down, b_up]
    w_qkv, vecs = call(
        functools.partial(prefetch_kernel, images),
        [shape(w_qkv.shape), shape((16, width), F32)],
        after(w_qkv, xs[1]),
        buckets.T,
        *vectors,
        far=2 + len(vectors),
        scratch=[like(v) for v in vectors] + [like(buckets.T), dma((2 + len(vectors),))],
        name="prefetch",
    )
    weights = [w_out, w_up, w_down]
    w_out, w_up, w_down, qkv, p, rinv, o, x2, n2, h, gp = call(
        functools.partial(forward_kernel, count, share),
        [shape(w.shape) for w in weights]
        + [
            shape((rows, 3 * width)),
            shape((HEADS, rows, rows)),
            shape((rows, width), F32),
            shape((rows, width)),
            shape((rows, width), F32),
            shape((rows, width)),
            shape((rows, hidden)),
            shape((rows, hidden)),
        ],
        *weights,
        *xs,
        vecs,
        w_qkv,
        far=len(weights),
        scratch=[dma((len(weights),))],
        name="forward",
    )
    g, keep, sent = call(
        functools.partial(down_kernel, depth, ORDERS[0], down, count, share),
        [shape((rows, width))] + [shape((chips, down.tall, LANES))] * 2,
        *cs,
        vecs,
        h,
        name="down",
    )
    one = Sum(keep, sent, ORDERS[0]).cores()
    keep, sent, dx2, dx2r, block, sub = call(
        functools.partial(middle_kernel, depth, ORDERS[1], up, out),
        [shape((chips, up.tall + out.tall, LANES))] * 2
        + [
            shape((rows, width), F32),
            shape((rows, width)),
            shape((rows, width)),
            shape((8, hidden), F32),
        ],
        g,
        gp,
        h,
        n2,
        o,
        x2,
        vecs,
        w_up,
        w_down,
        scratch=[pltpu.VMEM((rows, hidden), BF16)],
        name="middle",
    )
    dx2r = after(dx2r, one.got)
    two = Sum(keep, sent, ORDERS[1]).cores()
    one.advance()
    *results, keep, sent = call(
        functools.partial(backward_kernel, depth, ORDERS[2], proj, count, share),
        [shape((2 * share, width))] * count + [shape((chips, proj.tall + 16, LANES))] * 2,
        *xs,
        *cs,
        qkv,
        p,
        rinv,
        o,
        dx2,
        dx2r,
        block,
        sub,
        vecs,
        w_qkv,
        w_out,
        scratch=[
            pltpu.VMEM((rows, 3 * width), BF16),
            pltpu.VMEM((2 * chips, 16, LANES), F32),
        ],
        name="backward",
    )
    three = Sum(keep, sent, ORDERS[2])
    three.cores(two.got)
    def whole(group, layout, small_at=0, sizes=(), name=None):
        outs = [shape((p.rows, 2 * p.half), F32) for p, _ in layout]
        outs += [shape((n,), F32) for n in sizes]
        return call(
            functools.partial(
                gather_kernel, depth, group.order, layout, 1.0 / total_images, small_at, sizes
            ),
            outs,
            *group.finish(),
            far_outs=len(layout),
            scratch=[pltpu.VMEM((2 * chips, p.height, p.width), F32) for p, _ in layout]
            + [pltpu.VMEM((2 * chips, 16, LANES), F32), dma((len(layout), 2 * chips))],
            name=name,
        )

    groups = (one, two, three)
    layouts = ([(down, 0)], [(up, 0), (out, up.tall)], [(proj, 0)])
    names = ("gather_down", "gather_up", "gather_proj")
    sizes = (width,) * 9 + (hidden,)
    done = {(3, 0): keep, (0, 0): one.got}
    grads = {}
    progress = True
    while progress:
        progress = False
        for which in (2, 1, 0):
            group = groups[which]
            if which in grads:
                continue
            waits = [b for a, b in TIES if a == (which, group.step)]
            waits += [(4, b) for a, b in WRITTEN if a == (which, group.step)]
            if any(w not in done for w in waits):
                continue
            progress = True
            behind = [done[w] for w in waits]
            if group.left:
                group.advance(*behind)
                done[which, group.step - 1] = group.got
            else:
                if behind:
                    group.got = after(group.got, *behind)
                grads[which] = whole(
                    group,
                    layouts[which],
                    proj.tall if which == 2 else 0,
                    sizes if which == 2 else (),
                    name=names[which],
                )
                done[4, which] = grads[which][0]
        if (5, 0) not in done and RESULTS in done:
            results = [results[0]] + [
                send(after(results[k], done[RESULTS]), image_pair(k)) for k in range(1, count)
            ]
            done[5, 0] = results[-1]
            progress = True
    (grad_down,), (grad_up, grad_out), (grad_proj, *small) = (grads[i] for i in range(3))
    mask_g, gain1_g, bias1_g, query_g, value_g, after_g, gain2_g, bias2_g, reduce_g, expand_g = small

    block_out, token_grad = call(
        finish_kernel,
        [shape((count, share, width)), shape((count, share, width), F32)],
        flags,
        *results,
        name="finish",
    )
    return (
        block_out.reshape(tokens.shape),
        token_grad.reshape(tokens.shape),
        mask_g,
        gain1_g,
        bias1_g,
        grad_proj,
        query_g,
        value_g,
        grad_out,
        after_g,
        gain2_g,
        bias2_g,
        grad_up,
        expand_g,
        grad_down,
        reduce_g,
    )


def solution(mesh):
    rows = P(None, "dp", "blk", None)
    placed = (rows, P(None, "dp", "blk"), P(None, "dp"), rows) + (P(),) * 14
    return jax.shard_map(
        functools.partial(shards, mesh.shape["dp"], mesh.shape["blk"]),
        mesh=mesh,
        in_specs=placed,
        out_specs=(rows, rows) + (P(),) * 14,
        check_vma=False,
    )
```

time: 170 us -> 110 us (0.65)
  starting transfers between devices: 75.6 us -> 43.8 us
  local copies, waits for them, and re-layouts: 13.2 us -> 0.01 us
  Pallas kernels: 31.5 us -> 24.3 us
  waiting for transfers between devices: 43.8 us -> 38 us
    ppermute x51 -> x39, starting transfers between devices: 75.6 us -> 43.8 us  [send(): return lax.ppermute(value, ('dp', 'blk'), table)]
    pallas_call x9 -> x10, Pallas kernels: 31.5 us -> 24.3 us  [call(): pl.pallas_call(kernel, out_shape=tuple(outs), in_specs=[FAR] * far + [WHO...]
    reshape x10 -> x0, local copies, waits for them, and re-layouts: 6.83 us -> none  [wide(): return v.reshape(1, -1)]
    unnamed x31 -> x2, local copies, waits for them, and re-layouts: 6.14 us -> 0.01 us
    ppermute x51 -> x39, waiting for transfers between devices: 43.8 us -> 38 us  [send(): return lax.ppermute(value, ('dp', 'blk'), table)]
  transfers between devices with their start and end apart: 51 -> 39, of which waited for: 18 -> 16; matrix products, arithmetic and copies ran while one was open for 5% -> 2% of each run, Pallas kernels for 5% -> 18%
where the time goes in v2:
time: 110 us; the launch traced here: 109 us
  starting transfers between devices  43.8 us (40%)
  waiting for transfers between devices  38 us (35%)
  Pallas kernels  24.3 us (22%)
  other arithmetic  1.91 us (2%)
  between operations  1.15 us (1%)
    ppermute x39, starting transfers between devices, send(): return lax.ppermute(value, ('dp', 'blk'), table)  43.8 us
    ppermute x39, waiting for transfers between devices, send(): return lax.ppermute(value, ('dp', 'blk'), table)  38 us
    pallas_call x10, Pallas kernels, call(): pl.pallas_call(kernel, out_shape=tuple(outs), in_specs=[FAR] * far + [WHO...  24.3 us
  transfers between devices with their start and end apart: 39, of which 16 were waited for; matrix products, arithmetic and copies ran while one was open for 2% of the time, Pallas kernels for 18%

profile of v2, /device:TPU:1, one launch (start us, length us, event | category | flops | bytes accessed | tf_op | source)
XLA Modules:
  0.0 109.1 jit_solution(8423636886629561746)
XLA Ops:
  1.9 2.7 %collective-permute-start.1 = (bf16[64,512]{1,0:T(8,128)(2,1)S(1)}, bf16[64,512]{1,0:T(8,128)(2,1)S(1)}, u32[]{:S(2)}, u32[]{:S(2)}) collective-permute-start(bf16[64,512]{1,0:T(8,128)(2,1)S(1)} %get-tuple-element.81), channel_id=1, source_target_pairs={{0,2},{1,3},{2,0},{3,1},{4,6},{5,7},{6,4},{7,5},{8,10},{9,11},{10,... | collective-permute-start | bytes 196616 | tf_op jit(solution)/shard_map/ppermute | solution.py:547
  4.7 1.7 %collective-permute-start.5 = (bf16[80,512]{1,0:T(8,128)(2,1)S(1)}, bf16[80,512]{1,0:T(8,128)(2,1)S(1)}, u32[]{:S(2)}, u32[]{:S(2)}) collective-permute-start(bf16[80,512]{1,0:T(8,128)(2,1)S(1)} %get-tuple-element.89), channel_id=1, source_target_pairs={{0,3},{1,2},{2,1},{3,0},{4,7},{5,6},{6,5},{7,4},{8,11},{9,10},{10,... | collective-permute-start | bytes 245768 | tf_op jit(solution)/shard_map/ppermute | solution.py:547
  6.8 1.5 %prefetch.1 = (bf16[512,1536]{1,0:T(8,128)(2,1)S(1)}, f32[16,512]{1,0:T(8,128)S(1)}) custom-call(bf16[512,1536]{1,0:T(8,128)(2,1)} %weight_hbm, s32[1,2]{1,0:T(1,128)} %bitcast.10, bf16[512]{0:T(512)(128)(2,1)} %refs_0_.2, bf16[512]{0:T(512)(128)(2,1)} %refs_1_.2, bf16[512]{0:T(512)(128)(2,1)} %refs_2_.2, bf16[512]{0:T(512)(128)(2,1)} %refs_3_.1, ...), custom_call_target="tpu_custom_call" | custom-call | tf_op jit(solution)/shard_map/prefetch/pallas_call | solution.py:477
  9.3 4.3 %forward.1 = (bf16[512,512]{1,0:T(8,128)(2,1)S(1)}, bf16[512,2048]{1,0:T(8,128)(2,1)S(1)}, bf16[2048,512]{1,0:T(8,128)(2,1)S(1)}, bf16[256,1536]{1,0:T(8,128)(2,...) custom-call(bf16[512,512]{1,0:T(8,128)(2,1)} %refs_0_.3, ...), custom_call_target="tpu_custom_call" | custom-call | flops 17250000896 | tf_op jit(solution)/shard_map/forward/pallas_call | solution.py:477
  14.6 3.0 %middle.1 = (bf16[8,640,128]{2,1,0:T(8,128)(2,1)S(1)}, bf16[8,640,128]{2,1,0:T(8,128)(2,1)S(1)}, f32[256,512]{1,0:T(8,128)S(1)}, bf16[256,512]{1,0:T(8,128)(2,1)...) custom-call(bf16[256,512]{1,0:T(8,128)(2,1)S(1)} %get-tuple-element.98.g_ref, ...), custom_call_target="tpu_custom_call" | custom-call | tf_op jit(solution)/shard_map/middle/pallas_call | solution.py:477
  19.9 5.2 %backward.1 = (bf16[128,512]{1,0:T(8,128)(2,1)S(1)}, bf16[128,512]{1,0:T(8,128)(2,1)S(1)}, bf16[128,512]{1,0:T(8,128)(2,1)S(1)}, bf16[128,512]{1,0:T(8,128)(2,1)...) custom-call(bf16[64,512]{1,0:T(8,128)(2,1)S(1)} %get-tuple-element.79.refs_3_.refs_0_, ...), custom_call_target="tpu_custom_call" | custom-call | tf_op jit(solution)/shard_map/backward/pallas_call | solution.py:477
  26.8 5.4 %collective-permute-done.30 = bf16[4,512,128]{2,1,0:T(8,128)(2,1)S(1)} collective-permute-done((bf16[4,512,128]{2,1,0:T(8,128)(2,1)S(1)}, bf16[4,512,128]{2,1,0:T(8,128)(2,1)S(1)}, u32[]{:S(2)}, u32[]{:S(2)}) %collective-permute-start.30) | collective-permute-done | bytes 524320 | tf_op jit(solution)/shard_map/ppermute | solution.py:547
  35.3 3.6 %collective-permute-done.31 = bf16[2,512,128]{2,1,0:T(8,128)(2,1)S(1)} collective-permute-done((bf16[2,512,128]{2,1,0:T(8,128)(2,1)S(1)}, bf16[2,512,128]{2,1,0:T(8,128)(2,1)S(1)}, u32[]{:S(2)}, u32[]{:S(2)}) %collective-permute-start.31) | collective-permute-done | bytes 262176 | tf_op jit(solution)/shard_map/ppermute | solution.py:547
  43.1 2.4 %collective-permute-start.33 = (bf16[1,512,128]{2,1,0:T(8,128)(2,1)S(1)}, bf16[1,512,128]{2,1,0:T(8,128)(2,1)S(1)}, u32[]{:S(2)}, u32[]{:S(2)}) collective-permute-start(bf16[1,512,128]{2,1,0:T(8,128)(2,1)S(1)} %add_convert_fusion.17), channel_id=1, source_target_pairs={{0,16},{1,17},{2,18},{3,19},{4,20},{5,21},{6,22},{7,23},{8,24},{9,... | collective-permute-start | bytes 393224 | tf_op jit(solution)/shard_map/ppermute | solution.py:547
  50.7 3.4 %collective-permute-done.23 = bf16[1,640,128]{2,1,0:T(8,128)(2,1)S(1)} collective-permute-done((bf16[1,640,128]{2,1,0:T(8,128)(2,1)S(1)}, bf16[1,640,128]{2,1,0:T(8,128)(2,1)S(1)}, u32[]{:S(2)}, u32[]{:S(2)}) %collective-permute-start.23) | collective-permute-done | bytes 163872 | tf_op jit(solution)/shard_map/ppermute | solution.py:547
  54.1 2.7 %collective-permute-start.24 = (bf16[1,640,128]{2,1,0:T(8,128)(2,1)S(1)}, bf16[1,640,128]{2,1,0:T(8,128)(2,1)S(1)}, u32[]{:S(2)}, u32[]{:S(2)}) collective-permute-start(bf16[1,640,128]{2,1,0:T(8,128)(2,1)S(1)} %add_convert_fusion.13), channel_id=1, source_target_pairs={{0,16},{1,17},{2,18},{3,19},{4,20},{5,21},{6,22},{7,23},{8,24},{9,... | collective-permute-start | bytes 491528 | tf_op jit(solution)/shard_map/ppermute | solution.py:547
  57.1 3.7 %collective-permute-done.24 = bf16[1,640,128]{2,1,0:T(8,128)(2,1)S(1)} collective-permute-done((bf16[1,640,128]{2,1,0:T(8,128)(2,1)S(1)}, bf16[1,640,128]{2,1,0:T(8,128)(2,1)S(1)}, u32[]{:S(2)}, u32[]{:S(2)}) %collective-permute-start.24) | collective-permute-done | bytes 163872 | tf_op jit(solution)/shard_map/ppermute | solution.py:547
  62.5 4.1 %collective-permute-done.25 = bf16[1,640,128]{2,1,0:T(8,128)(2,1)S(1)} collective-permute-done((bf16[1,640,128]{2,1,0:T(8,128)(2,1)S(1)}, bf16[1,640,128]{2,1,0:T(8,128)(2,1)S(1)}, u32[]{:S(2)}, u32[]{:S(2)}) %collective-permute-start.25) | collective-permute-done | bytes 163872 | tf_op jit(solution)/shard_map/ppermute | solution.py:547
  69.1 4.0 %collective-permute-done.15 = bf16[1,400,128]{2,1,0:T(8,128)(2,1)S(1)} collective-permute-done((bf16[1,400,128]{2,1,0:T(8,128)(2,1)S(1)}, bf16[1,400,128]{2,1,0:T(8,128)(2,1)S(1)}, u32[]{:S(2)}, u32[]{:S(2)}) %collective-permute-start.15) | collective-permute-done | bytes 102432 | tf_op jit(solution)/shard_map/ppermute | solution.py:547
  73.3 1.8 %collective-permute-start.27 = (bf16[4,640,128]{2,1,0:T(8,128)(2,1)S(1)}, bf16[4,640,128]{2,1,0:T(8,128)(2,1)S(1)}, u32[]{:S(2)}, u32[]{:S(2)}) collective-permute-start(bf16[4,640,128]{2,1,0:T(8,128)(2,1)S(1)} %pad_maximum_fusion.refs_0_), channel_id=1, source_target_pairs={{0,4},{1,3},{2,6},{3,1},{4,0},{5,7},{6,2},{7,5},{8,12},{9,11},{10,... | collective-permute-start | bytes 1966088 | tf_op jit(solution)/shard_map/ppermute | solution.py:547
  75.1 2.6 %collective-permute-done.16 = bf16[1,400,128]{2,1,0:T(8,128)(2,1)S(1)} collective-permute-done((bf16[1,400,128]{2,1,0:T(8,128)(2,1)S(1)}, bf16[1,400,128]{2,1,0:T(8,128)(2,1)S(1)}, u32[]{:S(2)}, u32[]{:S(2)}) %collective-permute-start.16) | collective-permute-done | bytes 102432 | tf_op jit(solution)/shard_map/ppermute | solution.py:547
  79.4 7.7 %collective-permute-start.37 = (bf16[4,512,128]{2,1,0:T(8,128)(2,1)S(1)}, bf16[4,512,128]{2,1,0:T(8,128)(2,1)S(1)}, u32[]{:S(2)}, u32[]{:S(2)}) collective-permute-start(bf16[4,512,128]{2,1,0:T(8,128)(2,1)S(1)} %pad_maximum_fusion.1.refs_0_), channel_id=1, source_target_pairs={{0,1},{1,0},{2,3},{3,2},{4,5},{5,4},{6,7},{7,6},{8,9},{9,8},{10,11... | collective-permute-start | bytes 1572872 | tf_op jit(solution)/shard_map/ppermute | solution.py:547
  87.1 2.8 %collective-permute-done.17 = bf16[2,400,128]{2,1,0:T(8,128)(2,1)S(1)} collective-permute-done((bf16[2,400,128]{2,1,0:T(8,128)(2,1)S(1)}, bf16[2,400,128]{2,1,0:T(8,128)(2,1)S(1)}, u32[]{:S(2)}, u32[]{:S(2)}) %collective-permute-start.17) | collective-permute-done | bytes 204832 | tf_op jit(solution)/shard_map/ppermute | solution.py:547
  89.9 1.9 %collective-permute-start.18 = (bf16[4,400,128]{2,1,0:T(8,128)(2,1)S(1)}, bf16[4,400,128]{2,1,0:T(8,128)(2,1)S(1)}, u32[]{:S(2)}, u32[]{:S(2)}) collective-permute-start(bf16[4,400,128]{2,1,0:T(8,128)(2,1)S(1)} %pad_maximum_fusion.2.refs_0_), channel_id=1, source_target_pairs={{0,2},{1,5},{2,0},{3,7},{4,6},{5,1},{6,4},{7,3},{8,10},{9,13},{10,... | collective-permute-start | bytes 1228808 | tf_op jit(solution)/shard_map/ppermute | solution.py:547
  95.9 1.5 %collective-permute-done.18.refs_1_ = bf16[4,400,128]{2,1,0:T(8,128)(2,1)S(1)} collective-permute-done((bf16[4,400,128]{2,1,0:T(8,128)(2,1)S(1)}, bf16[4,400,128]{2,1,0:T(8,128)(2,1)S(1)}, u32[]{:S(2)}, u32[]{:S(2)}) %collective-permute-start.18) | collective-permute-done | bytes 409632 | tf_op jit(solution)/shard_map/ppermute | solution.py:547
  97.4 3.2 %collective-permute-start.20 = (bf16[4,400,128]{2,1,0:T(8,128)(2,1)S(1)}, bf16[4,400,128]{2,1,0:T(8,128)(2,1)S(1)}, u32[]{:S(2)}, u32[]{:S(2)}) collective-permute-start(bf16[4,400,128]{2,1,0:T(8,128)(2,1)S(1)} %collective-permute-done.18.refs_1_), channel_id=1, source_target_pairs={{0,1},{1,0},{2,3},{3,2},{4,5},{5,4},{6,7},{7,6},{8,9},{9,8},{10,11... | collective-permute-start | bytes 1228808 | tf_op jit(solution)/shard_map/ppermute | solution.py:547
  101.6 2.2 %gather_down.1 = f32[2048,512]{1,0:T(8,128)} custom-call(bf16[4,512,128]{2,1,0:T(8,128)(2,1)S(1)} %pad_maximum_fusion.1.refs_0_, bf16[4,512,128]{2,1,0:T(8,128)(2,1)S(1)} %collective-permute-done.36.refs_1_, bf16[4,512,128]{2,1,0:T(8,128)(2,1)S(1)} %collective-permute-done.37.refs_2_, bf16[4,512,128]{2,1,0:T(8,128)(2,1)S(1)} %collective-permute-done.38.refs_3_), custom_call_target="tpu_custom_call" | custom-call | tf_op jit(solution)/shard_map/gather_down/pallas_call | solution.py:477
  103.8 2.5 %gather_proj.1 = (f32[512,1536]{1,0:T(8,128)}, f32[512]{0:T(512)}, f32[512]{0:T(512)}, f32[512]{0:T(512)}, f32[512]{0:T(512)}, /*index=5*/f32[512]{0:T(512)}, f3...) custom-call(bf16[4,400,128]{2,1,0:T(8,128)(2,1)S(1)} %pad_maximum_fusion.2.refs_0_, ...), custom_call_target="tpu_custom_call" | custom-call | tf_op jit(solution)/shard_map/gather_proj/pallas_call | solution.py:477
  106.3 2.6 %gather_up.1 = (f32[512,2048]{1,0:T(8,128)}, f32[512,512]{1,0:T(8,128)}) custom-call(bf16[4,640,128]{2,1,0:T(8,128)(2,1)S(1)} %pad_maximum_fusion.refs_0_, bf16[4,640,128]{2,1,0:T(8,128)(2,1)S(1)} %collective-permute-done.27.refs_1_, bf16[4,640,128]{2,1,0:T(8,128)(2,1)S(1)} %collective-permute-done.28.refs_2_, ...), custom_call_target="tpu_custom_call" | custom-call | tf_op jit(solution)/shard_map/gather_up/pallas_call | solution.py:477
  (87 shorter events, 31.6 us)
Async XLA Ops:
  4.7 9.0 %collective-permute-start.5 = (bf16[80,512]{1,0:T(8,128)(2,1)S(1)}, bf16[80,512]{1,0:T(8,128)(2,1)S(1)}, u32[]{:S(2)}, u32[]{:S(2)}) collective-permute-start(bf16[80,512]{1,0:T(8,128)(2,1)S(1)} %get-tuple-element.89), channel_id=1, source_target_pairs={{0,3},{1,2},{2,1},{3,0},{4,7},{5,6},{6,5},{7,4},{8,11},{9,10},{10,... | collective-permute-start | bytes 245768 | tf_op jit(solution)/shard_map/ppermute | solution.py:547
  6.4 7.3 %collective-permute-start.4 = (bf16[80,512]{1,0:T(8,128)(2,1)S(1)}, bf16[80,512]{1,0:T(8,128)(2,1)S(1)}, u32[]{:S(2)}, u32[]{:S(2)}) collective-permute-start(bf16[80,512]{1,0:T(8,128)(2,1)S(1)} %get-tuple-element.87), channel_id=1, source_target_pairs={{0,2},{1,3},{2,0},{3,1},{4,6},{5,7},{6,4},{7,5},{8,10},{9,11},{10,... | collective-permute-start | bytes 245768 | tf_op jit(solution)/shard_map/ppermute | solution.py:547
  6.4 7.2 %collective-permute-start.3 = (bf16[80,512]{1,0:T(8,128)(2,1)S(1)}, bf16[80,512]{1,0:T(8,128)(2,1)S(1)}, u32[]{:S(2)}, u32[]{:S(2)}) collective-permute-start(bf16[80,512]{1,0:T(8,128)(2,1)S(1)} %get-tuple-element.85), channel_id=1, source_target_pairs={{0,1},{1,0},{2,3},{3,2},{4,5},{5,4},{6,7},{7,6},{8,9},{9,8},{10,11... | collective-permute-start | bytes 245768 | tf_op jit(solution)/shard_map/ppermute | solution.py:547
  17.7 7.4 %collective-permute-start.10 = (bf16[8,640,128]{2,1,0:T(8,128)(2,1)S(1)}, bf16[8,640,128]{2,1,0:T(8,128)(2,1)S(1)}, u32[]{:S(2)}, u32[]{:S(2)}) collective-permute-start(bf16[8,640,128]{2,1,0:T(8,128)(2,1)S(1)} %get-tuple-element.122), channel_id=1, source_target_pairs={{0,1},{1,0},{2,3},{3,2},{4,5},{5,4},{6,7},{7,6},{8,9},{9,8},{10,11... | collective-permute-start | bytes 3932168 | tf_op jit(solution)/shard_map/ppermute | solution.py:547
  18.5 13.6 %collective-permute-start.30 = (bf16[4,512,128]{2,1,0:T(8,128)(2,1)S(1)}, bf16[4,512,128]{2,1,0:T(8,128)(2,1)S(1)}, u32[]{:S(2)}, u32[]{:S(2)}) collective-permute-start(bf16[4,512,128]{2,1,0:T(8,128)(2,1)S(1)} %get-tuple-element.145), channel_id=1, source_target_pairs={{0,8},{1,9},{2,10},{3,11},{4,12},{5,13},{6,14},{7,15},{8,0},{9,1},... | collective-permute-start | bytes 1572872 | tf_op jit(solution)/shard_map/ppermute | solution.py:547
  25.4 14.8 %collective-permute-start.21 = (bf16[4,640,128]{2,1,0:T(8,128)(2,1)S(1)}, bf16[4,640,128]{2,1,0:T(8,128)(2,1)S(1)}, u32[]{:S(2)}, u32[]{:S(2)}) collective-permute-start(bf16[4,640,128]{2,1,0:T(8,128)(2,1)S(1)} %get-tuple-element.131), channel_id=1, source_target_pairs={{0,4},{1,3},{2,6},{3,1},{4,0},{5,7},{6,2},{7,5},{8,12},{9,11},{10,... | collective-permute-start | bytes 1966088 | tf_op jit(solution)/shard_map/ppermute | solution.py:547
  33.5 12.0 %collective-permute-start.11 = (bf16[8,400,128]{2,1,0:T(8,128)(2,1)S(1)}, bf16[8,400,128]{2,1,0:T(8,128)(2,1)S(1)}, u32[]{:S(2)}, u32[]{:S(2)}) collective-permute-start(bf16[8,400,128]{2,1,0:T(8,128)(2,1)S(1)} %get-tuple-element.123), channel_id=1, source_target_pairs={{0,1},{1,0},{2,3},{3,2},{4,5},{5,4},{6,7},{7,6},{8,9},{9,8},{10,11... | collective-permute-start | bytes 2457608 | tf_op jit(solution)/shard_map/ppermute | solution.py:547
  34.7 26.1 %collective-permute-start.9 = (bf16[128,512]{1,0:T(8,128)(2,1)S(1)}, bf16[128,512]{1,0:T(8,128)(2,1)S(1)}, u32[]{:S(2)}, u32[]{:S(2)}) collective-permute-start(bf16[128,512]{1,0:T(8,128)(2,1)S(1)} %get-tuple-element.118), channel_id=1, source_target_pairs={{0,3},{1,2},{2,1},{3,0},{4,7},{5,6},{6,5},{7,4},{8,11},{9,10},{10,... | collective-permute-start | bytes 393224 | tf_op jit(solution)/shard_map/ppermute | solution.py:547
  40.4 7.7 %collective-permute-start.22 = (bf16[2,640,128]{2,1,0:T(8,128)(2,1)S(1)}, bf16[2,640,128]{2,1,0:T(8,128)(2,1)S(1)}, u32[]{:S(2)}, u32[]{:S(2)}) collective-permute-start(bf16[2,640,128]{2,1,0:T(8,128)(2,1)S(1)} %get-tuple-element.149), channel_id=1, source_target_pairs={{0,2},{1,5},{2,0},{3,7},{4,6},{5,1},{6,4},{7,3},{8,10},{9,13},{10,... | collective-permute-start | bytes 983048 | tf_op jit(solution)/shard_map/ppermute | solution.py:547
  45.7 11.2 %collective-permute-start.12 = (bf16[4,400,128]{2,1,0:T(8,128)(2,1)S(1)}, bf16[4,400,128]{2,1,0:T(8,128)(2,1)S(1)}, u32[]{:S(2)}, u32[]{:S(2)}) collective-permute-start(bf16[4,400,128]{2,1,0:T(8,128)(2,1)S(1)} %get-tuple-element.147), channel_id=1, source_target_pairs={{0,2},{1,5},{2,0},{3,7},{4,6},{5,1},{6,4},{7,3},{8,10},{9,13},{10,... | collective-permute-start | bytes 1228808 | tf_op jit(solution)/shard_map/ppermute | solution.py:547
  49.3 18.6 %collective-permute-start.34 = (bf16[1,512,128]{2,1,0:T(8,128)(2,1)S(1)}, bf16[1,512,128]{2,1,0:T(8,128)(2,1)S(1)}, u32[]{:S(2)}, u32[]{:S(2)}) collective-permute-start(bf16[1,512,128]{2,1,0:T(8,128)(2,1)S(1)} %add_convert_fusion.16), channel_id=1, source_target_pairs={{0,4},{1,3},{2,6},{3,1},{4,0},{5,7},{6,2},{7,5},{8,12},{9,11},{10,... | collective-permute-start | bytes 393224 | tf_op jit(solution)/shard_map/ppermute | solution.py:547
  54.1 6.6 %collective-permute-start.24 = (bf16[1,640,128]{2,1,0:T(8,128)(2,1)S(1)}, bf16[1,640,128]{2,1,0:T(8,128)(2,1)S(1)}, u32[]{:S(2)}, u32[]{:S(2)}) collective-permute-start(bf16[1,640,128]{2,1,0:T(8,128)(2,1)S(1)} %add_convert_fusion.13), channel_id=1, source_target_pairs={{0,16},{1,17},{2,18},{3,19},{4,20},{5,21},{6,22},{7,23},{8,24},{9,... | collective-permute-start | bytes 491528 | tf_op jit(solution)/shard_map/ppermute | solution.py:547
  66.6 6.5 %collective-permute-start.26 = (bf16[2,640,128]{2,1,0:T(8,128)(2,1)S(1)}, bf16[2,640,128]{2,1,0:T(8,128)(2,1)S(1)}, u32[]{:S(2)}, u32[]{:S(2)}) collective-permute-start(bf16[2,640,128]{2,1,0:T(8,128)(2,1)S(1)} %pad_maximum_fusion.3), channel_id=1, source_target_pairs={{0,2},{1,5},{2,0},{3,7},{4,6},{5,1},{6,4},{7,3},{8,10},{9,13},{10,... | collective-permute-start | bytes 983048 | tf_op jit(solution)/shard_map/ppermute | solution.py:547
  68.0 11.2 %collective-permute-start.35 = (bf16[2,512,128]{2,1,0:T(8,128)(2,1)S(1)}, bf16[2,512,128]{2,1,0:T(8,128)(2,1)S(1)}, u32[]{:S(2)}, u32[]{:S(2)}) collective-permute-start(bf16[2,512,128]{2,1,0:T(8,128)(2,1)S(1)} %pad_maximum_fusion.4), channel_id=1, source_target_pairs={{0,2},{1,5},{2,0},{3,7},{4,6},{5,1},{6,4},{7,3},{8,10},{9,13},{10,... | collective-permute-start | bytes 786440 | tf_op jit(solution)/shard_map/ppermute | solution.py:547
  73.3 21.2 %collective-permute-start.27 = (bf16[4,640,128]{2,1,0:T(8,128)(2,1)S(1)}, bf16[4,640,128]{2,1,0:T(8,128)(2,1)S(1)}, u32[]{:S(2)}, u32[]{:S(2)}) collective-permute-start(bf16[4,640,128]{2,1,0:T(8,128)(2,1)S(1)} %pad_maximum_fusion.refs_0_), channel_id=1, source_target_pairs={{0,4},{1,3},{2,6},{3,1},{4,0},{5,7},{6,2},{7,5},{8,12},{9,11},{10,... | collective-permute-start | bytes 1966088 | tf_op jit(solution)/shard_map/ppermute | solution.py:547
  77.7 12.2 %collective-permute-start.17 = (bf16[2,400,128]{2,1,0:T(8,128)(2,1)S(1)}, bf16[2,400,128]{2,1,0:T(8,128)(2,1)S(1)}, u32[]{:S(2)}, u32[]{:S(2)}) collective-permute-start(bf16[2,400,128]{2,1,0:T(8,128)(2,1)S(1)} %pad_maximum_fusion.5), channel_id=1, source_target_pairs={{0,4},{1,3},{2,6},{3,1},{4,0},{5,7},{6,2},{7,5},{8,12},{9,11},{10,... | collective-permute-start | bytes 614408 | tf_op jit(solution)/shard_map/ppermute | solution.py:547
  79.3 15.3 %collective-permute-start.36 = (bf16[4,512,128]{2,1,0:T(8,128)(2,1)S(1)}, bf16[4,512,128]{2,1,0:T(8,128)(2,1)S(1)}, u32[]{:S(2)}, u32[]{:S(2)}) collective-permute-start(bf16[4,512,128]{2,1,0:T(8,128)(2,1)S(1)} %pad_maximum_fusion.1.refs_0_), channel_id=1, source_target_pairs={{0,8},{1,9},{2,10},{3,11},{4,12},{5,13},{6,14},{7,15},{8,0},{9,1},... | collective-permute-start | bytes 1572872 | tf_op jit(solution)/shard_map/ppermute | solution.py:547
  79.4 13.2 %collective-permute-start.8 = (bf16[128,512]{1,0:T(8,128)(2,1)S(1)}, bf16[128,512]{1,0:T(8,128)(2,1)S(1)}, u32[]{:S(2)}, u32[]{:S(2)}) collective-permute-start(bf16[128,512]{1,0:T(8,128)(2,1)S(1)} %get-tuple-element.116), channel_id=1, source_target_pairs={{0,2},{1,3},{2,0},{3,1},{4,6},{5,7},{6,4},{7,5},{8,10},{9,11},{10,... | collective-permute-start | bytes 393224 | tf_op jit(solution)/shard_map/ppermute | solution.py:547
  79.4 16.5 %collective-permute-start.37 = (bf16[4,512,128]{2,1,0:T(8,128)(2,1)S(1)}, bf16[4,512,128]{2,1,0:T(8,128)(2,1)S(1)}, u32[]{:S(2)}, u32[]{:S(2)}) collective-permute-start(bf16[4,512,128]{2,1,0:T(8,128)(2,1)S(1)} %pad_maximum_fusion.1.refs_0_), channel_id=1, source_target_pairs={{0,1},{1,0},{2,3},{3,2},{4,5},{5,4},{6,7},{7,6},{8,9},{9,8},{10,11... | collective-permute-start | bytes 1572872 | tf_op jit(solution)/shard_map/ppermute | solution.py:547
  89.9 7.5 %collective-permute-start.18 = (bf16[4,400,128]{2,1,0:T(8,128)(2,1)S(1)}, bf16[4,400,128]{2,1,0:T(8,128)(2,1)S(1)}, u32[]{:S(2)}, u32[]{:S(2)}) collective-permute-start(bf16[4,400,128]{2,1,0:T(8,128)(2,1)S(1)} %pad_maximum_fusion.2.refs_0_), channel_id=1, source_target_pairs={{0,2},{1,5},{2,0},{3,7},{4,6},{5,1},{6,4},{7,3},{8,10},{9,13},{10,... | collective-permute-start | bytes 1228808 | tf_op jit(solution)/shard_map/ppermute | solution.py:547
  94.1 12.2 %collective-permute-start.28 = (bf16[4,640,128]{2,1,0:T(8,128)(2,1)S(1)}, bf16[4,640,128]{2,1,0:T(8,128)(2,1)S(1)}, u32[]{:S(2)}, u32[]{:S(2)}) collective-permute-start(bf16[4,640,128]{2,1,0:T(8,128)(2,1)S(1)} %pad_maximum_fusion.refs_0_), channel_id=1, source_target_pairs={{0,1},{1,0},{2,3},{3,2},{4,5},{5,4},{6,7},{7,6},{8,9},{9,8},{10,11... | collective-permute-start | bytes 1966088 | tf_op jit(solution)/shard_map/ppermute | solution.py:547
  94.4 11.9 %collective-permute-start.29 = (bf16[4,640,128]{2,1,0:T(8,128)(2,1)S(1)}, bf16[4,640,128]{2,1,0:T(8,128)(2,1)S(1)}, u32[]{:S(2)}, u32[]{:S(2)}) collective-permute-start(bf16[4,640,128]{2,1,0:T(8,128)(2,1)S(1)} %collective-permute-done.27.refs_1_), channel_id=1, source_target_pairs={{0,1},{1,0},{2,3},{3,2},{4,5},{5,4},{6,7},{7,6},{8,9},{9,8},{10,11... | collective-permute-start | bytes 1966088 | tf_op jit(solution)/shard_map/ppermute | solution.py:547
  94.6 7.1 %collective-permute-start.38 = (bf16[4,512,128]{2,1,0:T(8,128)(2,1)S(1)}, bf16[4,512,128]{2,1,0:T(8,128)(2,1)S(1)}, u32[]{:S(2)}, u32[]{:S(2)}) collective-permute-start(bf16[4,512,128]{2,1,0:T(8,128)(2,1)S(1)} %collective-permute-done.36.refs_1_), channel_id=1, source_target_pairs={{0,1},{1,0},{2,3},{3,2},{4,5},{5,4},{6,7},{7,6},{8,9},{9,8},{10,11... | collective-permute-start | bytes 1572872 | tf_op jit(solution)/shard_map/ppermute | solution.py:547
  95.9 7.9 %collective-permute-start.19 = (bf16[4,400,128]{2,1,0:T(8,128)(2,1)S(1)}, bf16[4,400,128]{2,1,0:T(8,128)(2,1)S(1)}, u32[]{:S(2)}, u32[]{:S(2)}) collective-permute-start(bf16[4,400,128]{2,1,0:T(8,128)(2,1)S(1)} %pad_maximum_fusion.2.refs_0_), channel_id=1, source_target_pairs={{0,1},{1,0},{2,3},{3,2},{4,5},{5,4},{6,7},{7,6},{8,9},{9,8},{10,11... | collective-permute-start | bytes 1228808 | tf_op jit(solution)/shard_map/ppermute | solution.py:547
  (16 other events, 102.2 us)

commit v3 on v2

--- a/solution.py
+++ b/solution.py
@@ -13,11 +13,13 @@
 LOG2E = 1.4426950408889634
 BF16 = jnp.bfloat16
 F32 = jnp.float32
-ORDERS = (('zxy', 'zyx'), ('yxz', 'xyz'), ('xyz', 'yxz'))
-TIES = (((0, 1), (3, 0)), ((1, 0), (3, 0)), ((1, 4), (5, 0)))
-RESULTS = (3, 0)
+ORDERS = (('zxy', 'yxz'), ('yzx', 'zxy'), ('yzx', 'xzy'))
+TIES = (((2, 2), (5, 0)), ((0, 2), (1, 0)), ((1, 3), (0, 1)), ((0, 1), (3, 0)), ((2, 4), (1, 4)), ((0, 6), (1, 5)), ((2, 5), (1, 2)), ((2, 1), (3, 0)), ((2, 2), (0, 1)), ((0, 2), (3, 0)), ((2, 3), (1, 2)), ((1, 0), (3, 0)))
+RESULTS = (1, 2)
 WRITTEN = ()
-US = {'forward': 15}
+BEFORE = 1
+THIRD = 1
+US = {'forward': 15, 'gather_up': 3}
 VMEM_LIMIT = 24 * 1024 * 1024
 
 
@@ -241,9 +243,13 @@
         )
         acc = jnp.zeros((rows, LANES), F32)
         racc = jnp.zeros((rows, LANES), F32)
+        stack = jnp.concatenate(
+            [keys * (lane_head == i).astype(F32).astype(BF16) for i in range(per)], axis=0
+        )
+        scores = dot_nt(stack, q)
         for i in range(per):
             here = lane_head == i
-            s = dot_nt(keys * here.astype(F32).astype(BF16), q) * scale + dead
+            s = scores[i * rows : (i + 1) * rows, :] * scale + dead
             top = jnp.max(s, axis=0, keepdims=True)
             p = jnp.exp2(s - top).astype(BF16)
             p_ref[group * per + i] = p
@@ -335,7 +341,7 @@
     cs = [refs.pop(0) for _ in range(count)]
     qkv_ref, p_ref, rinv_ref, o_ref, dx2_ref, dx2r_ref, block_ref, sub_ref, vecs, w_qkv, w_out = refs[:11]
     refs = refs[11:]
-    results = [refs.pop(0) for _ in range(count)]
+    results = [refs.pop(0) for _ in range(3)]
     keep_ref, send_ref, dqkv_ref, small = refs
     core, place, _ = place_of()
     rows = count * share
@@ -359,15 +365,29 @@
         dq = jnp.zeros((rows, LANES), F32)
         dk = jnp.zeros((rows, LANES), F32)
         dv = jnp.zeros((rows, LANES), F32)
+        stack = jnp.concatenate(
+            [
+                jnp.concatenate(
+                    [
+                        values * (lane_head == i).astype(F32).astype(BF16),
+                        minus * (lane_head == i).astype(F32).astype(BF16),
+                    ],
+                    axis=1,
+                )
+                for i in range(per)
+            ],
+            axis=0,
+        )
+        p = p_ref[group * per : (group + 1) * per].reshape(per * rows, rows)
+        ds = (p.astype(F32) * dot_nt(stack, rhs)).astype(BF16)
+        dks = dot(ds, q)
+        dvs = dot(p, ds_o)
         for i in range(per):
             here = lane_head == i
-            mask = here.astype(F32).astype(BF16)
-            lhs = jnp.concatenate([values * mask, minus * mask], axis=1)
-            p = p_ref[group * per + i]
-            ds = (p.astype(F32) * dot_nt(lhs, rhs)).astype(BF16)
-            dq = jnp.where(here, dot_tn(ds, keys), dq)
-            dk = jnp.where(here, dot(ds, q), dk)
-            dv = jnp.where(here, dot(p, ds_o), dv)
+            part = slice(i * rows, (i + 1) * rows)
+            dq = jnp.where(here, dot_tn(ds[part, :], keys), dq)
+            dk = jnp.where(here, dks[part, :], dk)
+            dv = jnp.where(here, dvs[part, :], dv)
         dqkv_ref[:, at : at + LANES] = (dq * scale).astype(BF16)
         dqkv_ref[:, width + at : width + at + LANES] = (dk * scale).astype(BF16)
         dqkv_ref[:, 2 * width + at : 2 * width + at + LANES] = dv.astype(BF16)
@@ -382,8 +402,9 @@
     for k in range(count):
         part = dx[k * share : (k + 1) * share, :]
         d_mask = d_mask + dot(cs[k][share : share + 16, :share], part)
-        results[k][:share, :] = block_ref[k * share : (k + 1) * share, :]
-        results[k][share:, :] = part
+        ref, at = results[min(k, 2)], 2 * share * max(k - 2, 0)
+        ref[at : at + share, :] = block_ref[k * share : (k + 1) * share, :]
+        ref[at + share : at + 2 * share, :] = part
     blocks = small.shape[0]
     small[...] = jnp.zeros(small.shape, F32)
     wide = [
@@ -463,7 +484,9 @@
     for k, ref in enumerate(refs[:-2]):
         at = blk ^ k
         block_out[at] = ref[:share, :]
-        token_grad[at] = jnp.where(flag_column(flags, at), 0.0, ref[share:, :].astype(F32))
+        token_grad[at] = jnp.where(
+            flag_column(flags, at), 0.0, ref[share : 2 * share, :].astype(F32)
+        )
 
 
 WHOLE = pl.BlockSpec(memory_space=pltpu.VMEM)
@@ -693,12 +716,16 @@
         scratch=[pltpu.VMEM((rows, hidden), BF16)],
         name="middle",
     )
-    dx2r = after(dx2r, one.got)
     two = Sum(keep, sent, ORDERS[1]).cores()
+    early = [one.got, two.got][:BEFORE]
+    if early:
+        dx2r = after(dx2r, *early)
     one.advance()
     *results, keep, sent = call(
         functools.partial(backward_kernel, depth, ORDERS[2], proj, count, share),
-        [shape((2 * share, width))] * count + [shape((chips, proj.tall + 16, LANES))] * 2,
+        [shape((2 * share, width))] * 2
+        + [shape((2 * share * (count - 2), width))]
+        + [shape((chips, proj.tall + 16, LANES))] * 2,
         *xs,
         *cs,
         qkv,
@@ -719,7 +746,7 @@
         name="backward",
     )
     three = Sum(keep, sent, ORDERS[2])
-    three.cores(two.got)
+    three.cores(*[two.got][:THIRD])
     def whole(group, layout, small_at=0, sizes=(), name=None):
         outs = [shape((p.rows, 2 * p.half), F32) for p, _ in layout]
         outs += [shape((n,), F32) for n in sizes]
@@ -769,9 +796,10 @@
                 )
                 done[4, which] = grads[which][0]
         if (5, 0) not in done and RESULTS in done:
-            results = [results[0]] + [
-                send(after(results[k], done[RESULTS]), image_pair(k)) for k in range(1, count)
-            ]
+            own, near, far = results
+            far = send(after(far, done[RESULTS]), image_pair(2))
+            near = send(after(near, done[RESULTS]), image_pair(1))
+            results = [own, near, far, send(far[2 * share :], image_pair(1))]
             done[5, 0] = results[-1]
             progress = True
     (grad_down,), (grad_up, grad_out), (grad_proj, *small) = (grads[i] for i in range(3))

time: 110 us -> 107 us (0.973)
  waiting for transfers between devices: 38 us -> 23.8 us
  starting transfers between devices: 43.8 us -> 56.5 us
    ppermute x39, waiting for transfers between devices: 38 us -> 23.8 us  [send(): return lax.ppermute(value, ('dp', 'blk'), table)]
    ppermute x39, starting transfers between devices: 43.8 us -> 56.5 us  [send(): return lax.ppermute(value, ('dp', 'blk'), table)]
  transfers between devices with their start and end apart: 39 -> 39, of which waited for: 16 -> 14; matrix products, arithmetic and copies ran while one was open for 2% -> 2% of each run, Pallas kernels for 18% -> 18%
where the time goes in v3:
time: 107 us
  starting transfers between devices  56.5 us (53%)
  waiting for transfers between devices  23.8 us (22%)
  Pallas kernels  23.4 us (22%)
  other arithmetic  1.91 us (2%)
  between operations  1.11 us (1%)
    ppermute x39, starting transfers between devices, send(): return lax.ppermute(value, ('dp', 'blk'), table)  56.5 us
    ppermute x39, waiting for transfers between devices, send(): return lax.ppermute(value, ('dp', 'blk'), table)  23.8 us
    pallas_call x10, Pallas kernels, call(): pl.pallas_call(kernel, out_shape=tuple(outs), in_specs=[FAR] * far + [WHO...  23.4 us
  transfers between devices with their start and end apart: 39, of which 14 were waited for; matrix products, arithmetic and copies ran while one was open for 2% of the time, Pallas kernels for 18%

profile of v3, /device:TPU:1, one launch (start us, length us, event | category | flops | bytes accessed | tf_op | source)
XLA Modules:
  0.0 106.7 jit_solution(15047650343229530515)
XLA Ops:
  1.9 2.7 %collective-permute-start.1 = (bf16[64,512]{1,0:T(8,128)(2,1)S(1)}, bf16[64,512]{1,0:T(8,128)(2,1)S(1)}, u32[]{:S(2)}, u32[]{:S(2)}) collective-permute-start(bf16[64,512]{1,0:T(8,128)(2,1)S(1)} %get-tuple-element.86), channel_id=1, source_target_pairs={{0,2},{1,3},{2,0},{3,1},{4,6},{5,7},{6,4},{7,5},{8,10},{9,11},{10,... | collective-permute-start | bytes 196616 | tf_op jit(solution)/shard_map/ppermute | solution.py:570
  4.7 1.7 %collective-permute-start.5 = (bf16[80,512]{1,0:T(8,128)(2,1)S(1)}, bf16[80,512]{1,0:T(8,128)(2,1)S(1)}, u32[]{:S(2)}, u32[]{:S(2)}) collective-permute-start(bf16[80,512]{1,0:T(8,128)(2,1)S(1)} %get-tuple-element.94), channel_id=1, source_target_pairs={{0,3},{1,2},{2,1},{3,0},{4,7},{5,6},{6,5},{7,4},{8,11},{9,10},{10,... | collective-permute-start | bytes 245768 | tf_op jit(solution)/shard_map/ppermute | solution.py:570
  6.8 1.5 %prefetch.1 = (bf16[512,1536]{1,0:T(8,128)(2,1)S(1)}, f32[16,512]{1,0:T(8,128)S(1)}) custom-call(bf16[512,1536]{1,0:T(8,128)(2,1)} %weight_hbm, s32[1,2]{1,0:T(1,128)} %bitcast.10, bf16[512]{0:T(512)(128)(2,1)} %refs_0_.2, bf16[512]{0:T(512)(128)(2,1)} %refs_1_.2, bf16[512]{0:T(512)(128)(2,1)} %refs_2_.2, bf16[512]{0:T(512)(128)(2,1)} %refs_3_.1, ...), custom_call_target="tpu_custom_call" | custom-call | tf_op jit(solution)/shard_map/prefetch/pallas_call | solution.py:500
  9.3 4.3 %forward.1 = (bf16[512,512]{1,0:T(8,128)(2,1)S(1)}, bf16[512,2048]{1,0:T(8,128)(2,1)S(1)}, bf16[2048,512]{1,0:T(8,128)(2,1)S(1)}, bf16[256,1536]{1,0:T(8,128)(2,...) custom-call(bf16[512,512]{1,0:T(8,128)(2,1)} %refs_0_.3, ...), custom_call_target="tpu_custom_call" | custom-call | flops 17250000896 | tf_op jit(solution)/shard_map/forward/pallas_call | solution.py:500
  14.6 3.0 %middle.1 = (bf16[8,640,128]{2,1,0:T(8,128)(2,1)S(1)}, bf16[8,640,128]{2,1,0:T(8,128)(2,1)S(1)}, f32[256,512]{1,0:T(8,128)S(1)}, bf16[256,512]{1,0:T(8,128)(2,1)...) custom-call(bf16[256,512]{1,0:T(8,128)(2,1)S(1)} %get-tuple-element.103.g_ref, ...), custom_call_target="tpu_custom_call" | custom-call | tf_op jit(solution)/shard_map/middle/pallas_call | solution.py:500
  19.8 4.3 %backward.1 = (bf16[128,512]{1,0:T(8,128)(2,1)S(1)}, bf16[128,512]{1,0:T(8,128)(2,1)S(1)}, bf16[256,512]{1,0:T(8,128)(2,1)S(1)}, bf16[8,400,128]{2,1,0:T(8,128)(2,1)S(1)}, bf16[8,400,128]{2,1,0:T(8,128)(2,1)S(1)}) custom-call(bf16[64,512]{1,0:T(8,128)(2,1)S(1)} %get-tuple-element.84.refs_3_.refs_0_, ...), custom_call_target="tpu_custom_call" | custom-call | tf_op jit(solution)/shard_map/backward/pallas_call | solution.py:500
  29.6 4.3 %collective-permute-done.18 = bf16[2,512,128]{2,1,0:T(8,128)(2,1)S(1)} collective-permute-done((bf16[2,512,128]{2,1,0:T(8,128)(2,1)S(1)}, bf16[2,512,128]{2,1,0:T(8,128)(2,1)S(1)}, u32[]{:S(2)}, u32[]{:S(2)}) %collective-permute-start.18) | collective-permute-done | bytes 262176 | tf_op jit(solution)/shard_map/ppermute | solution.py:570
  38.3 2.4 %collective-permute-start.33 = (bf16[1,512,128]{2,1,0:T(8,128)(2,1)S(1)}, bf16[1,512,128]{2,1,0:T(8,128)(2,1)S(1)}, u32[]{:S(2)}, u32[]{:S(2)}) collective-permute-start(bf16[1,512,128]{2,1,0:T(8,128)(2,1)S(1)} %add_convert_fusion.17), channel_id=1, source_target_pairs={{0,16},{1,17},{2,18},{3,19},{4,20},{5,21},{6,22},{7,23},{8,24},{9,... | collective-permute-start | bytes 393224 | tf_op jit(solution)/shard_map/ppermute | solution.py:570
  44.0 1.8 %collective-permute-start.34 = (bf16[1,512,128]{2,1,0:T(8,128)(2,1)S(1)}, bf16[1,512,128]{2,1,0:T(8,128)(2,1)S(1)}, u32[]{:S(2)}, u32[]{:S(2)}) collective-permute-start(bf16[1,512,128]{2,1,0:T(8,128)(2,1)S(1)} %add_convert_fusion.16), channel_id=1, source_target_pairs={{0,4},{1,9},{2,6},{3,11},{4,0},{5,13},{6,2},{7,15},{8,12},{9,1},{1... | collective-permute-start | bytes 393224 | tf_op jit(solution)/shard_map/ppermute | solution.py:570
  46.8 4.1 %collective-permute-start.21 = (bf16[1,640,128]{2,1,0:T(8,128)(2,1)S(1)}, bf16[1,640,128]{2,1,0:T(8,128)(2,1)S(1)}, u32[]{:S(2)}, u32[]{:S(2)}) collective-permute-start(bf16[1,640,128]{2,1,0:T(8,128)(2,1)S(1)} %add_convert_fusion.13), channel_id=1, source_target_pairs={{0,16},{1,17},{2,18},{3,19},{4,20},{5,21},{6,22},{7,23},{8,24},{9,... | collective-permute-start | bytes 491528 | tf_op jit(solution)/shard_map/ppermute | solution.py:570
  52.4 2.1 %collective-permute-done.21 = bf16[1,640,128]{2,1,0:T(8,128)(2,1)S(1)} collective-permute-done((bf16[1,640,128]{2,1,0:T(8,128)(2,1)S(1)}, bf16[1,640,128]{2,1,0:T(8,128)(2,1)S(1)}, u32[]{:S(2)}, u32[]{:S(2)}) %collective-permute-start.21) | collective-permute-done | bytes 163872 | tf_op jit(solution)/shard_map/ppermute | solution.py:570
  54.5 2.0 %collective-permute-start.22 = (bf16[1,640,128]{2,1,0:T(8,128)(2,1)S(1)}, bf16[1,640,128]{2,1,0:T(8,128)(2,1)S(1)}, u32[]{:S(2)}, u32[]{:S(2)}) collective-permute-start(bf16[1,640,128]{2,1,0:T(8,128)(2,1)S(1)} %add_convert_fusion.12), channel_id=1, source_target_pairs={{0,2},{1,5},{2,0},{3,7},{4,6},{5,1},{6,4},{7,3},{8,10},{9,13},{10,... | collective-permute-start | bytes 491528 | tf_op jit(solution)/shard_map/ppermute | solution.py:570
  56.6 6.4 %collective-permute-start.13 = (bf16[128,512]{1,0:T(8,128)(2,1)S(1)}, bf16[128,512]{1,0:T(8,128)(2,1)S(1)}, u32[]{:S(2)}, u32[]{:S(2)}) collective-permute-start(bf16[128,512]{1,0:T(8,128)(2,1)S(1)} %slice.156), channel_id=1, source_target_pairs={{0,1},{1,0},{2,3},{3,2},{4,5},{5,4},{6,7},{7,6},{8,9},{9,8},{10,11... | collective-permute-start | bytes 393224 | tf_op jit(solution)/shard_map/ppermute | solution.py:570
  64.2 3.6 %collective-permute-done.19 = bf16[1,400,128]{2,1,0:T(8,128)(2,1)S(1)} collective-permute-done((bf16[1,400,128]{2,1,0:T(8,128)(2,1)S(1)}, bf16[1,400,128]{2,1,0:T(8,128)(2,1)S(1)}, u32[]{:S(2)}, u32[]{:S(2)}) %collective-permute-start.19) | collective-permute-done | bytes 102432 | tf_op jit(solution)/shard_map/ppermute | solution.py:570
  68.5 3.9 %collective-permute-done.20 = bf16[1,400,128]{2,1,0:T(8,128)(2,1)S(1)} collective-permute-done((bf16[1,400,128]{2,1,0:T(8,128)(2,1)S(1)}, bf16[1,400,128]{2,1,0:T(8,128)(2,1)S(1)}, u32[]{:S(2)}, u32[]{:S(2)}) %collective-permute-start.20) | collective-permute-done | bytes 102432 | tf_op jit(solution)/shard_map/ppermute | solution.py:570
  72.6 2.5 %collective-permute-start.29 = (bf16[4,640,128]{2,1,0:T(8,128)(2,1)S(1)}, bf16[4,640,128]{2,1,0:T(8,128)(2,1)S(1)}, u32[]{:S(2)}, u32[]{:S(2)}) collective-permute-start(bf16[4,640,128]{2,1,0:T(8,128)(2,1)S(1)} %pad_maximum_fusion.refs_0_), channel_id=1, source_target_pairs={{0,4},{1,9},{2,6},{3,11},{4,0},{5,13},{6,2},{7,15},{8,12},{9,1},{1... | collective-permute-start | bytes 1966088 | tf_op jit(solution)/shard_map/ppermute | solution.py:570
  76.3 2.5 %collective-permute-start.24 = (bf16[2,400,128]{2,1,0:T(8,128)(2,1)S(1)}, bf16[2,400,128]{2,1,0:T(8,128)(2,1)S(1)}, u32[]{:S(2)}, u32[]{:S(2)}) collective-permute-start(bf16[2,400,128]{2,1,0:T(8,128)(2,1)S(1)} %pad_maximum_fusion.5), channel_id=1, source_target_pairs={{0,8},{1,9},{2,10},{3,11},{4,12},{5,13},{6,14},{7,15},{8,0},{9,1},... | collective-permute-start | bytes 614408 | tf_op jit(solution)/shard_map/ppermute | solution.py:570
  79.0 5.3 %collective-permute-start.37 = (bf16[4,512,128]{2,1,0:T(8,128)(2,1)S(1)}, bf16[4,512,128]{2,1,0:T(8,128)(2,1)S(1)}, u32[]{:S(2)}, u32[]{:S(2)}) collective-permute-start(bf16[4,512,128]{2,1,0:T(8,128)(2,1)S(1)} %pad_maximum_fusion.1.refs_0_), channel_id=1, source_target_pairs={{0,1},{1,0},{2,3},{3,2},{4,5},{5,4},{6,7},{7,6},{8,9},{9,8},{10,11... | collective-permute-start | bytes 1572872 | tf_op jit(solution)/shard_map/ppermute | solution.py:570
  84.2 2.0 %collective-permute-done.24 = bf16[2,400,128]{2,1,0:T(8,128)(2,1)S(1)} collective-permute-done((bf16[2,400,128]{2,1,0:T(8,128)(2,1)S(1)}, bf16[2,400,128]{2,1,0:T(8,128)(2,1)S(1)}, u32[]{:S(2)}, u32[]{:S(2)}) %collective-permute-start.24) | collective-permute-done | bytes 204832 | tf_op jit(solution)/shard_map/ppermute | solution.py:570
  90.0 3.9 %collective-permute-start.31 = (bf16[4,640,128]{2,1,0:T(8,128)(2,1)S(1)}, bf16[4,640,128]{2,1,0:T(8,128)(2,1)S(1)}, u32[]{:S(2)}, u32[]{:S(2)}) collective-permute-start(bf16[4,640,128]{2,1,0:T(8,128)(2,1)S(1)} %collective-permute-done.29.refs_1_), channel_id=1, source_target_pairs={{0,1},{1,0},{2,3},{3,2},{4,5},{5,4},{6,7},{7,6},{8,9},{9,8},{10,11... | collective-permute-start | bytes 1966088 | tf_op jit(solution)/shard_map/ppermute | solution.py:570
  94.4 3.9 %collective-permute-start.27 = (bf16[4,400,128]{2,1,0:T(8,128)(2,1)S(1)}, bf16[4,400,128]{2,1,0:T(8,128)(2,1)S(1)}, u32[]{:S(2)}, u32[]{:S(2)}) collective-permute-start(bf16[4,400,128]{2,1,0:T(8,128)(2,1)S(1)} %collective-permute-done.25.refs_1_), channel_id=1, source_target_pairs={{0,1},{1,0},{2,3},{3,2},{4,5},{5,4},{6,7},{7,6},{8,9},{9,8},{10,11... | collective-permute-start | bytes 1228808 | tf_op jit(solution)/shard_map/ppermute | solution.py:570
  99.2 2.2 %gather_down.1 = f32[2048,512]{1,0:T(8,128)} custom-call(bf16[4,512,128]{2,1,0:T(8,128)(2,1)S(1)} %pad_maximum_fusion.1.refs_0_, bf16[4,512,128]{2,1,0:T(8,128)(2,1)S(1)} %collective-permute-done.36.refs_1_, bf16[4,512,128]{2,1,0:T(8,128)(2,1)S(1)} %collective-permute-done.37.refs_2_, bf16[4,512,128]{2,1,0:T(8,128)(2,1)S(1)} %collective-permute-done.38.refs_3_), custom_call_target="tpu_custom_call" | custom-call | tf_op jit(solution)/shard_map/gather_down/pallas_call | solution.py:500
  101.4 2.5 %gather_proj.1 = (f32[512,1536]{1,0:T(8,128)}, f32[512]{0:T(512)}, f32[512]{0:T(512)}, f32[512]{0:T(512)}, f32[512]{0:T(512)}, /*index=5*/f32[512]{0:T(512)}, f3...) custom-call(bf16[4,400,128]{2,1,0:T(8,128)(2,1)S(1)} %pad_maximum_fusion.2.refs_0_, ...), custom_call_target="tpu_custom_call" | custom-call | tf_op jit(solution)/shard_map/gather_proj/pallas_call | solution.py:500
  103.9 2.6 %gather_up.1 = (f32[512,2048]{1,0:T(8,128)}, f32[512,512]{1,0:T(8,128)}) custom-call(bf16[4,640,128]{2,1,0:T(8,128)(2,1)S(1)} %pad_maximum_fusion.refs_0_, bf16[4,640,128]{2,1,0:T(8,128)(2,1)S(1)} %collective-permute-done.29.refs_1_, bf16[4,640,128]{2,1,0:T(8,128)(2,1)S(1)} %collective-permute-done.30.refs_2_, ...), custom_call_target="tpu_custom_call" | custom-call | flops 3449999872 | tf_op jit(solution)/shard_map/gather_up/pallas_call | solution.py:500
  (88 shorter events, 30.2 us)
Async XLA Ops:
  4.7 8.9 %collective-permute-start.5 = (bf16[80,512]{1,0:T(8,128)(2,1)S(1)}, bf16[80,512]{1,0:T(8,128)(2,1)S(1)}, u32[]{:S(2)}, u32[]{:S(2)}) collective-permute-start(bf16[80,512]{1,0:T(8,128)(2,1)S(1)} %get-tuple-element.94), channel_id=1, source_target_pairs={{0,3},{1,2},{2,1},{3,0},{4,7},{5,6},{6,5},{7,4},{8,11},{9,10},{10,... | collective-permute-start | bytes 245768 | tf_op jit(solution)/shard_map/ppermute | solution.py:570
  6.4 7.2 %collective-permute-start.4 = (bf16[80,512]{1,0:T(8,128)(2,1)S(1)}, bf16[80,512]{1,0:T(8,128)(2,1)S(1)}, u32[]{:S(2)}, u32[]{:S(2)}) collective-permute-start(bf16[80,512]{1,0:T(8,128)(2,1)S(1)} %get-tuple-element.92), channel_id=1, source_target_pairs={{0,2},{1,3},{2,0},{3,1},{4,6},{5,7},{6,4},{7,5},{8,10},{9,11},{10,... | collective-permute-start | bytes 245768 | tf_op jit(solution)/shard_map/ppermute | solution.py:570
  6.4 7.2 %collective-permute-start.3 = (bf16[80,512]{1,0:T(8,128)(2,1)S(1)}, bf16[80,512]{1,0:T(8,128)(2,1)S(1)}, u32[]{:S(2)}, u32[]{:S(2)}) collective-permute-start(bf16[80,512]{1,0:T(8,128)(2,1)S(1)} %get-tuple-element.90), channel_id=1, source_target_pairs={{0,1},{1,0},{2,3},{3,2},{4,5},{5,4},{6,7},{7,6},{8,9},{9,8},{10,11... | collective-permute-start | bytes 245768 | tf_op jit(solution)/shard_map/ppermute | solution.py:570
  18.5 8.4 %collective-permute-start.17 = (bf16[4,512,128]{2,1,0:T(8,128)(2,1)S(1)}, bf16[4,512,128]{2,1,0:T(8,128)(2,1)S(1)}, u32[]{:S(2)}, u32[]{:S(2)}) collective-permute-start(bf16[4,512,128]{2,1,0:T(8,128)(2,1)S(1)} %get-tuple-element.155), channel_id=1, source_target_pairs={{0,8},{1,5},{2,10},{3,7},{4,12},{5,1},{6,14},{7,3},{8,0},{9,13},{1... | collective-permute-start | bytes 1572872 | tf_op jit(solution)/shard_map/ppermute | solution.py:570
  24.4 9.9 %collective-permute-start.8 = (bf16[4,640,128]{2,1,0:T(8,128)(2,1)S(1)}, bf16[4,640,128]{2,1,0:T(8,128)(2,1)S(1)}, u32[]{:S(2)}, u32[]{:S(2)}) collective-permute-start(bf16[4,640,128]{2,1,0:T(8,128)(2,1)S(1)} %get-tuple-element.121), channel_id=1, source_target_pairs={{0,4},{1,9},{2,6},{3,11},{4,0},{5,13},{6,2},{7,15},{8,12},{9,1},{1... | collective-permute-start | bytes 1966088 | tf_op jit(solution)/shard_map/ppermute | solution.py:570
  27.0 6.9 %collective-permute-start.18 = (bf16[2,512,128]{2,1,0:T(8,128)(2,1)S(1)}, bf16[2,512,128]{2,1,0:T(8,128)(2,1)S(1)}, u32[]{:S(2)}, u32[]{:S(2)}) collective-permute-start(bf16[2,512,128]{2,1,0:T(8,128)(2,1)S(1)} %get-tuple-element.131), channel_id=1, source_target_pairs={{0,2},{1,3},{2,0},{3,1},{4,6},{5,7},{6,4},{7,5},{8,10},{9,11},{10,... | collective-permute-start | bytes 786440 | tf_op jit(solution)/shard_map/ppermute | solution.py:570
  28.4 12.3 %collective-permute-start.14 = (bf16[8,400,128]{2,1,0:T(8,128)(2,1)S(1)}, bf16[8,400,128]{2,1,0:T(8,128)(2,1)S(1)}, u32[]{:S(2)}, u32[]{:S(2)}) collective-permute-start(bf16[8,400,128]{2,1,0:T(8,128)(2,1)S(1)} %get-tuple-element.128), channel_id=1, source_target_pairs={{0,1},{1,0},{2,3},{3,2},{4,5},{5,4},{6,7},{7,6},{8,9},{9,8},{10,11... | collective-permute-start | bytes 2457608 | tf_op jit(solution)/shard_map/ppermute | solution.py:570
  40.9 11.3 %collective-permute-start.15 = (bf16[4,400,128]{2,1,0:T(8,128)(2,1)S(1)}, bf16[4,400,128]{2,1,0:T(8,128)(2,1)S(1)}, u32[]{:S(2)}, u32[]{:S(2)}) collective-permute-start(bf16[4,400,128]{2,1,0:T(8,128)(2,1)S(1)} %get-tuple-element.157), channel_id=1, source_target_pairs={{0,4},{1,3},{2,6},{3,1},{4,0},{5,7},{6,2},{7,5},{8,12},{9,11},{10,... | collective-permute-start | bytes 1228808 | tf_op jit(solution)/shard_map/ppermute | solution.py:570
  44.0 23.9 %collective-permute-start.34 = (bf16[1,512,128]{2,1,0:T(8,128)(2,1)S(1)}, bf16[1,512,128]{2,1,0:T(8,128)(2,1)S(1)}, u32[]{:S(2)}, u32[]{:S(2)}) collective-permute-start(bf16[1,512,128]{2,1,0:T(8,128)(2,1)S(1)} %add_convert_fusion.16), channel_id=1, source_target_pairs={{0,4},{1,9},{2,6},{3,11},{4,0},{5,13},{6,2},{7,15},{8,12},{9,1},{1... | collective-permute-start | bytes 393224 | tf_op jit(solution)/shard_map/ppermute | solution.py:570
  46.8 7.6 %collective-permute-start.21 = (bf16[1,640,128]{2,1,0:T(8,128)(2,1)S(1)}, bf16[1,640,128]{2,1,0:T(8,128)(2,1)S(1)}, u32[]{:S(2)}, u32[]{:S(2)}) collective-permute-start(bf16[1,640,128]{2,1,0:T(8,128)(2,1)S(1)} %add_convert_fusion.13), channel_id=1, source_target_pairs={{0,16},{1,17},{2,18},{3,19},{4,20},{5,21},{6,22},{7,23},{8,24},{9,... | collective-permute-start | bytes 491528 | tf_op jit(solution)/shard_map/ppermute | solution.py:570
  52.3 10.6 %collective-permute-start.16 = (bf16[2,400,128]{2,1,0:T(8,128)(2,1)S(1)}, bf16[2,400,128]{2,1,0:T(8,128)(2,1)S(1)}, u32[]{:S(2)}, u32[]{:S(2)}) collective-permute-start(bf16[2,400,128]{2,1,0:T(8,128)(2,1)S(1)} %get-tuple-element.129), channel_id=1, source_target_pairs={{0,8},{1,9},{2,10},{3,11},{4,12},{5,13},{6,14},{7,15},{8,0},{9,1},... | collective-permute-start | bytes 614408 | tf_op jit(solution)/shard_map/ppermute | solution.py:570
  54.5 9.4 %collective-permute-start.22 = (bf16[1,640,128]{2,1,0:T(8,128)(2,1)S(1)}, bf16[1,640,128]{2,1,0:T(8,128)(2,1)S(1)}, u32[]{:S(2)}, u32[]{:S(2)}) collective-permute-start(bf16[1,640,128]{2,1,0:T(8,128)(2,1)S(1)} %add_convert_fusion.12), channel_id=1, source_target_pairs={{0,2},{1,5},{2,0},{3,7},{4,6},{5,1},{6,4},{7,3},{8,10},{9,13},{10,... | collective-permute-start | bytes 491528 | tf_op jit(solution)/shard_map/ppermute | solution.py:570
  56.6 7.4 %collective-permute-start.13 = (bf16[128,512]{1,0:T(8,128)(2,1)S(1)}, bf16[128,512]{1,0:T(8,128)(2,1)S(1)}, u32[]{:S(2)}, u32[]{:S(2)}) collective-permute-start(bf16[128,512]{1,0:T(8,128)(2,1)S(1)} %slice.156), channel_id=1, source_target_pairs={{0,1},{1,0},{2,3},{3,2},{4,5},{5,4},{6,7},{7,6},{8,9},{9,8},{10,11... | collective-permute-start | bytes 393224 | tf_op jit(solution)/shard_map/ppermute | solution.py:570
  64.0 8.5 %collective-permute-start.28 = (bf16[2,640,128]{2,1,0:T(8,128)(2,1)S(1)}, bf16[2,640,128]{2,1,0:T(8,128)(2,1)S(1)}, u32[]{:S(2)}, u32[]{:S(2)}) collective-permute-start(bf16[2,640,128]{2,1,0:T(8,128)(2,1)S(1)} %pad_maximum_fusion.3), channel_id=1, source_target_pairs={{0,8},{1,3},{2,10},{3,1},{4,12},{5,7},{6,14},{7,5},{8,0},{9,11},{1... | collective-permute-start | bytes 983048 | tf_op jit(solution)/shard_map/ppermute | solution.py:570
  67.9 10.9 %collective-permute-start.35 = (bf16[2,512,128]{2,1,0:T(8,128)(2,1)S(1)}, bf16[2,512,128]{2,1,0:T(8,128)(2,1)S(1)}, u32[]{:S(2)}, u32[]{:S(2)}) collective-permute-start(bf16[2,512,128]{2,1,0:T(8,128)(2,1)S(1)} %pad_maximum_fusion.4), channel_id=1, source_target_pairs={{0,2},{1,3},{2,0},{3,1},{4,6},{5,7},{6,4},{7,5},{8,10},{9,11},{10,... | collective-permute-start | bytes 786440 | tf_op jit(solution)/shard_map/ppermute | solution.py:570
  72.6 17.4 %collective-permute-start.29 = (bf16[4,640,128]{2,1,0:T(8,128)(2,1)S(1)}, bf16[4,640,128]{2,1,0:T(8,128)(2,1)S(1)}, u32[]{:S(2)}, u32[]{:S(2)}) collective-permute-start(bf16[4,640,128]{2,1,0:T(8,128)(2,1)S(1)} %pad_maximum_fusion.refs_0_), channel_id=1, source_target_pairs={{0,4},{1,9},{2,6},{3,11},{4,0},{5,13},{6,2},{7,15},{8,12},{9,1},{1... | collective-permute-start | bytes 1966088 | tf_op jit(solution)/shard_map/ppermute | solution.py:570
  76.3 9.9 %collective-permute-start.24 = (bf16[2,400,128]{2,1,0:T(8,128)(2,1)S(1)}, bf16[2,400,128]{2,1,0:T(8,128)(2,1)S(1)}, u32[]{:S(2)}, u32[]{:S(2)}) collective-permute-start(bf16[2,400,128]{2,1,0:T(8,128)(2,1)S(1)} %pad_maximum_fusion.5), channel_id=1, source_target_pairs={{0,8},{1,9},{2,10},{3,11},{4,12},{5,13},{6,14},{7,15},{8,0},{9,1},... | collective-permute-start | bytes 614408 | tf_op jit(solution)/shard_map/ppermute | solution.py:570
  78.9 14.9 %collective-permute-start.36 = (bf16[4,512,128]{2,1,0:T(8,128)(2,1)S(1)}, bf16[4,512,128]{2,1,0:T(8,128)(2,1)S(1)}, u32[]{:S(2)}, u32[]{:S(2)}) collective-permute-start(bf16[4,512,128]{2,1,0:T(8,128)(2,1)S(1)} %pad_maximum_fusion.1.refs_0_), channel_id=1, source_target_pairs={{0,8},{1,5},{2,10},{3,7},{4,12},{5,1},{6,14},{7,3},{8,0},{9,13},{1... | collective-permute-start | bytes 1572872 | tf_op jit(solution)/shard_map/ppermute | solution.py:570
  79.0 15.0 %collective-permute-start.37 = (bf16[4,512,128]{2,1,0:T(8,128)(2,1)S(1)}, bf16[4,512,128]{2,1,0:T(8,128)(2,1)S(1)}, u32[]{:S(2)}, u32[]{:S(2)}) collective-permute-start(bf16[4,512,128]{2,1,0:T(8,128)(2,1)S(1)} %pad_maximum_fusion.1.refs_0_), channel_id=1, source_target_pairs={{0,1},{1,0},{2,3},{3,2},{4,5},{5,4},{6,7},{7,6},{8,9},{9,8},{10,11... | collective-permute-start | bytes 1572872 | tf_op jit(solution)/shard_map/ppermute | solution.py:570
  86.3 8.0 %collective-permute-start.25 = (bf16[4,400,128]{2,1,0:T(8,128)(2,1)S(1)}, bf16[4,400,128]{2,1,0:T(8,128)(2,1)S(1)}, u32[]{:S(2)}, u32[]{:S(2)}) collective-permute-start(bf16[4,400,128]{2,1,0:T(8,128)(2,1)S(1)} %pad_maximum_fusion.2.refs_0_), channel_id=1, source_target_pairs={{0,4},{1,3},{2,6},{3,1},{4,0},{5,7},{6,2},{7,5},{8,12},{9,11},{10,... | collective-permute-start | bytes 1228808 | tf_op jit(solution)/shard_map/ppermute | solution.py:570
  89.6 14.3 %collective-permute-start.30 = (bf16[4,640,128]{2,1,0:T(8,128)(2,1)S(1)}, bf16[4,640,128]{2,1,0:T(8,128)(2,1)S(1)}, u32[]{:S(2)}, u32[]{:S(2)}) collective-permute-start(bf16[4,640,128]{2,1,0:T(8,128)(2,1)S(1)} %pad_maximum_fusion.refs_0_), channel_id=1, source_target_pairs={{0,1},{1,0},{2,3},{3,2},{4,5},{5,4},{6,7},{7,6},{8,9},{9,8},{10,11... | collective-permute-start | bytes 1966088 | tf_op jit(solution)/shard_map/ppermute | solution.py:570
  90.0 13.9 %collective-permute-start.31 = (bf16[4,640,128]{2,1,0:T(8,128)(2,1)S(1)}, bf16[4,640,128]{2,1,0:T(8,128)(2,1)S(1)}, u32[]{:S(2)}, u32[]{:S(2)}) collective-permute-start(bf16[4,640,128]{2,1,0:T(8,128)(2,1)S(1)} %collective-permute-done.29.refs_1_), channel_id=1, source_target_pairs={{0,1},{1,0},{2,3},{3,2},{4,5},{5,4},{6,7},{7,6},{8,9},{9,8},{10,11... | collective-permute-start | bytes 1966088 | tf_op jit(solution)/shard_map/ppermute | solution.py:570
  94.0 7.4 %collective-permute-start.26 = (bf16[4,400,128]{2,1,0:T(8,128)(2,1)S(1)}, bf16[4,400,128]{2,1,0:T(8,128)(2,1)S(1)}, u32[]{:S(2)}, u32[]{:S(2)}) collective-permute-start(bf16[4,400,128]{2,1,0:T(8,128)(2,1)S(1)} %pad_maximum_fusion.2.refs_0_), channel_id=1, source_target_pairs={{0,1},{1,0},{2,3},{3,2},{4,5},{5,4},{6,7},{7,6},{8,9},{9,8},{10,11... | collective-permute-start | bytes 1228808 | tf_op jit(solution)/shard_map/ppermute | solution.py:570
  94.4 7.0 %collective-permute-start.27 = (bf16[4,400,128]{2,1,0:T(8,128)(2,1)S(1)}, bf16[4,400,128]{2,1,0:T(8,128)(2,1)S(1)}, u32[]{:S(2)}, u32[]{:S(2)}) collective-permute-start(bf16[4,400,128]{2,1,0:T(8,128)(2,1)S(1)} %collective-permute-done.25.refs_1_), channel_id=1, source_target_pairs={{0,1},{1,0},{2,3},{3,2},{4,5},{5,4},{6,7},{7,6},{8,9},{9,8},{10,11... | collective-permute-start | bytes 1228808 | tf_op jit(solution)/shard_map/ppermute | solution.py:570
  (16 other events, 95.2 us)

commit v4 on v3

--- a/solution.py
+++ b/solution.py
@@ -14,12 +14,12 @@
 BF16 = jnp.bfloat16
 F32 = jnp.float32
 ORDERS = (('zxy', 'yxz'), ('yzx', 'zxy'), ('yzx', 'xzy'))
-TIES = (((2, 2), (5, 0)), ((0, 2), (1, 0)), ((1, 3), (0, 1)), ((0, 1), (3, 0)), ((2, 4), (1, 4)), ((0, 6), (1, 5)), ((2, 5), (1, 2)), ((2, 1), (3, 0)), ((2, 2), (0, 1)), ((0, 2), (3, 0)), ((2, 3), (1, 2)), ((1, 0), (3, 0)))
+TIES = (((2, 2), (5, 0)), ((0, 2), (1, 0)), ((1, 3), (0, 1)), ((0, 1), (3, 0)), ((2, 4), (1, 4)), ((0, 6), (1, 5)), ((2, 5), (1, 2)), ((2, 1), (3, 0)), ((2, 2), (0, 1)), ((0, 2), (3, 0)), ((2, 3), (1, 2)), ((1, 0), (3, 0)), ((2, 5), (7, 0)))
 RESULTS = (1, 2)
 WRITTEN = ()
 BEFORE = 1
 THIRD = 1
-US = {'forward': 15, 'gather_up': 3}
+US = {'forward': 15, 'gather_up': 8}
 VMEM_LIMIT = 24 * 1024 * 1024
 
 
@@ -801,17 +801,18 @@
             near = send(after(near, done[RESULTS]), image_pair(1))
             results = [own, near, far, send(far[2 * share :], image_pair(1))]
             done[5, 0] = results[-1]
+            block_out, token_grad = call(
+                finish_kernel,
+                [shape((count, share, width)), shape((count, share, width), F32)],
+                flags,
+                *results,
+                name="finish",
+            )
+            done[7, 0] = block_out
             progress = True
     (grad_down,), (grad_up, grad_out), (grad_proj, *small) = (grads[i] for i in range(3))
     mask_g, gain1_g, bias1_g, query_g, value_g, after_g, gain2_g, bias2_g, reduce_g, expand_g = small
 
-    block_out, token_grad = call(
-        finish_kernel,
-        [shape((count, share, width)), shape((count, share, width), F32)],
-        flags,
-        *results,
-        name="finish",
-    )
     return (
         block_out.reshape(tokens.shape),
         token_grad.reshape(tokens.shape),

time: 107 us -> 106 us (level)
  waiting for transfers between devices: 23.8 us -> 18 us
  starting transfers between devices: 56.5 us -> 61.2 us
    ppermute x39, waiting for transfers between devices: 23.8 us -> 18 us  [send(): return lax.ppermute(value, ('dp', 'blk'), table)]
    ppermute x39, starting transfers between devices: 56.5 us -> 61.2 us  [send(): return lax.ppermute(value, ('dp', 'blk'), table)]
  transfers between devices with their start and end apart: 39 -> 39, of which waited for: 14 -> 13; matrix products, arithmetic and copies ran while one was open for 2% -> 2% of each run, Pallas kernels for 18% -> 18%
where the time goes in v4:
time: 106 us
  starting transfers between devices  61.2 us (58%)
  Pallas kernels  23.4 us (22%)
  waiting for transfers between devices  18 us (17%)
  other arithmetic  1.92 us (2%)
  between operations  1.13 us (1%)
    ppermute x39, starting transfers between devices, send(): return lax.ppermute(value, ('dp', 'blk'), table)  61.2 us
    pallas_call x10, Pallas kernels, call(): pl.pallas_call(kernel, out_shape=tuple(outs), in_specs=[FAR] * far + [WHO...  23.4 us
    ppermute x39, waiting for transfers between devices, send(): return lax.ppermute(value, ('dp', 'blk'), table)  18 us
  transfers between devices with their start and end apart: 39, of which 13 were waited for; matrix products, arithmetic and copies ran while one was open for 2% of the time, Pallas kernels for 18%

profile of v4, /device:TPU:1, one launch (start us, length us, event | category | flops | bytes accessed | tf_op | source)
XLA Modules:
  0.0 105.7 jit_solution(2650733025744878465)
XLA Ops:
  1.9 2.7 %collective-permute-start.1 = (bf16[64,512]{1,0:T(8,128)(2,1)S(1)}, bf16[64,512]{1,0:T(8,128)(2,1)S(1)}, u32[]{:S(2)}, u32[]{:S(2)}) collective-permute-start(bf16[64,512]{1,0:T(8,128)(2,1)S(1)} %get-tuple-element.86), channel_id=1, source_target_pairs={{0,2},{1,3},{2,0},{3,1},{4,6},{5,7},{6,4},{7,5},{8,10},{9,11},{10,... | collective-permute-start | bytes 196616 | tf_op jit(solution)/shard_map/ppermute | solution.py:570
  4.7 1.7 %collective-permute-start.5 = (bf16[80,512]{1,0:T(8,128)(2,1)S(1)}, bf16[80,512]{1,0:T(8,128)(2,1)S(1)}, u32[]{:S(2)}, u32[]{:S(2)}) collective-permute-start(bf16[80,512]{1,0:T(8,128)(2,1)S(1)} %get-tuple-element.94), channel_id=1, source_target_pairs={{0,3},{1,2},{2,1},{3,0},{4,7},{5,6},{6,5},{7,4},{8,11},{9,10},{10,... | collective-permute-start | bytes 245768 | tf_op jit(solution)/shard_map/ppermute | solution.py:570
  9.3 4.3 %forward.1 = (bf16[512,512]{1,0:T(8,128)(2,1)S(1)}, bf16[512,2048]{1,0:T(8,128)(2,1)S(1)}, bf16[2048,512]{1,0:T(8,128)(2,1)S(1)}, bf16[256,1536]{1,0:T(8,128)(2,...) custom-call(bf16[512,512]{1,0:T(8,128)(2,1)} %refs_0_.3, ...), custom_call_target="tpu_custom_call" | custom-call | flops 17250000896 | tf_op jit(solution)/shard_map/forward/pallas_call | solution.py:500
  14.6 3.0 %middle.1 = (bf16[8,640,128]{2,1,0:T(8,128)(2,1)S(1)}, bf16[8,640,128]{2,1,0:T(8,128)(2,1)S(1)}, f32[256,512]{1,0:T(8,128)S(1)}, bf16[256,512]{1,0:T(8,128)(2,1)...) custom-call(bf16[256,512]{1,0:T(8,128)(2,1)S(1)} %get-tuple-element.103.g_ref, ...), custom_call_target="tpu_custom_call" | custom-call | tf_op jit(solution)/shard_map/middle/pallas_call | solution.py:500
  19.8 4.3 %backward.1 = (bf16[128,512]{1,0:T(8,128)(2,1)S(1)}, bf16[128,512]{1,0:T(8,128)(2,1)S(1)}, bf16[256,512]{1,0:T(8,128)(2,1)S(1)}, bf16[8,400,128]{2,1,0:T(8,128)(2,1)S(1)}, bf16[8,400,128]{2,1,0:T(8,128)(2,1)S(1)}) custom-call(bf16[64,512]{1,0:T(8,128)(2,1)S(1)} %get-tuple-element.84.refs_3_.refs_0_, ...), custom_call_target="tpu_custom_call" | custom-call | tf_op jit(solution)/shard_map/backward/pallas_call | solution.py:500
  29.6 4.3 %collective-permute-done.18 = bf16[2,512,128]{2,1,0:T(8,128)(2,1)S(1)} collective-permute-done((bf16[2,512,128]{2,1,0:T(8,128)(2,1)S(1)}, bf16[2,512,128]{2,1,0:T(8,128)(2,1)S(1)}, u32[]{:S(2)}, u32[]{:S(2)}) %collective-permute-start.18) | collective-permute-done | bytes 262176 | tf_op jit(solution)/shard_map/ppermute | solution.py:570
  38.3 2.4 %collective-permute-start.33 = (bf16[1,512,128]{2,1,0:T(8,128)(2,1)S(1)}, bf16[1,512,128]{2,1,0:T(8,128)(2,1)S(1)}, u32[]{:S(2)}, u32[]{:S(2)}) collective-permute-start(bf16[1,512,128]{2,1,0:T(8,128)(2,1)S(1)} %add_convert_fusion.17), channel_id=1, source_target_pairs={{0,16},{1,17},{2,18},{3,19},{4,20},{5,21},{6,22},{7,23},{8,24},{9,... | collective-permute-start | bytes 393224 | tf_op jit(solution)/shard_map/ppermute | solution.py:570
  44.0 1.8 %collective-permute-start.34 = (bf16[1,512,128]{2,1,0:T(8,128)(2,1)S(1)}, bf16[1,512,128]{2,1,0:T(8,128)(2,1)S(1)}, u32[]{:S(2)}, u32[]{:S(2)}) collective-permute-start(bf16[1,512,128]{2,1,0:T(8,128)(2,1)S(1)} %add_convert_fusion.16), channel_id=1, source_target_pairs={{0,4},{1,9},{2,6},{3,11},{4,0},{5,13},{6,2},{7,15},{8,12},{9,1},{1... | collective-permute-start | bytes 393224 | tf_op jit(solution)/shard_map/ppermute | solution.py:570
  46.8 4.1 %collective-permute-start.21 = (bf16[1,640,128]{2,1,0:T(8,128)(2,1)S(1)}, bf16[1,640,128]{2,1,0:T(8,128)(2,1)S(1)}, u32[]{:S(2)}, u32[]{:S(2)}) collective-permute-start(bf16[1,640,128]{2,1,0:T(8,128)(2,1)S(1)} %add_convert_fusion.13), channel_id=1, source_target_pairs={{0,16},{1,17},{2,18},{3,19},{4,20},{5,21},{6,22},{7,23},{8,24},{9,... | collective-permute-start | bytes 491528 | tf_op jit(solution)/shard_map/ppermute | solution.py:570
  52.4 2.1 %collective-permute-done.21 = bf16[1,640,128]{2,1,0:T(8,128)(2,1)S(1)} collective-permute-done((bf16[1,640,128]{2,1,0:T(8,128)(2,1)S(1)}, bf16[1,640,128]{2,1,0:T(8,128)(2,1)S(1)}, u32[]{:S(2)}, u32[]{:S(2)}) %collective-permute-start.21) | collective-permute-done | bytes 163872 | tf_op jit(solution)/shard_map/ppermute | solution.py:570
  54.5 2.0 %collective-permute-start.22 = (bf16[1,640,128]{2,1,0:T(8,128)(2,1)S(1)}, bf16[1,640,128]{2,1,0:T(8,128)(2,1)S(1)}, u32[]{:S(2)}, u32[]{:S(2)}) collective-permute-start(bf16[1,640,128]{2,1,0:T(8,128)(2,1)S(1)} %add_convert_fusion.12), channel_id=1, source_target_pairs={{0,2},{1,5},{2,0},{3,7},{4,6},{5,1},{6,4},{7,3},{8,10},{9,13},{10,... | collective-permute-start | bytes 491528 | tf_op jit(solution)/shard_map/ppermute | solution.py:570
  56.6 6.4 %collective-permute-start.13 = (bf16[128,512]{1,0:T(8,128)(2,1)S(1)}, bf16[128,512]{1,0:T(8,128)(2,1)S(1)}, u32[]{:S(2)}, u32[]{:S(2)}) collective-permute-start(bf16[128,512]{1,0:T(8,128)(2,1)S(1)} %slice.156), channel_id=1, source_target_pairs={{0,1},{1,0},{2,3},{3,2},{4,5},{5,4},{6,7},{7,6},{8,9},{9,8},{10,11... | collective-permute-start | bytes 393224 | tf_op jit(solution)/shard_map/ppermute | solution.py:570
  64.2 3.6 %collective-permute-done.19 = bf16[1,400,128]{2,1,0:T(8,128)(2,1)S(1)} collective-permute-done((bf16[1,400,128]{2,1,0:T(8,128)(2,1)S(1)}, bf16[1,400,128]{2,1,0:T(8,128)(2,1)S(1)}, u32[]{:S(2)}, u32[]{:S(2)}) %collective-permute-start.19) | collective-permute-done | bytes 102432 | tf_op jit(solution)/shard_map/ppermute | solution.py:570
  68.5 3.8 %collective-permute-start.11 = (bf16[128,512]{1,0:T(8,128)(2,1)S(1)}, bf16[128,512]{1,0:T(8,128)(2,1)S(1)}, u32[]{:S(2)}, u32[]{:S(2)}) collective-permute-start(bf16[128,512]{1,0:T(8,128)(2,1)S(1)} %get-tuple-element.122), channel_id=1, source_target_pairs={{0,1},{1,0},{2,3},{3,2},{4,5},{5,4},{6,7},{7,6},{8,9},{9,8},{10,11... | collective-permute-start | bytes 393224 | tf_op jit(solution)/shard_map/ppermute | solution.py:570
  72.6 2.5 %collective-permute-start.29 = (bf16[4,640,128]{2,1,0:T(8,128)(2,1)S(1)}, bf16[4,640,128]{2,1,0:T(8,128)(2,1)S(1)}, u32[]{:S(2)}, u32[]{:S(2)}) collective-permute-start(bf16[4,640,128]{2,1,0:T(8,128)(2,1)S(1)} %pad_maximum_fusion.refs_0_), channel_id=1, source_target_pairs={{0,4},{1,9},{2,6},{3,11},{4,0},{5,13},{6,2},{7,15},{8,12},{9,1},{1... | collective-permute-start | bytes 1966088 | tf_op jit(solution)/shard_map/ppermute | solution.py:570
  76.3 2.5 %collective-permute-start.24 = (bf16[2,400,128]{2,1,0:T(8,128)(2,1)S(1)}, bf16[2,400,128]{2,1,0:T(8,128)(2,1)S(1)}, u32[]{:S(2)}, u32[]{:S(2)}) collective-permute-start(bf16[2,400,128]{2,1,0:T(8,128)(2,1)S(1)} %pad_maximum_fusion.5), channel_id=1, source_target_pairs={{0,8},{1,9},{2,10},{3,11},{4,12},{5,13},{6,14},{7,15},{8,0},{9,1},... | collective-permute-start | bytes 614408 | tf_op jit(solution)/shard_map/ppermute | solution.py:570
  79.0 5.3 %collective-permute-start.37 = (bf16[4,512,128]{2,1,0:T(8,128)(2,1)S(1)}, bf16[4,512,128]{2,1,0:T(8,128)(2,1)S(1)}, u32[]{:S(2)}, u32[]{:S(2)}) collective-permute-start(bf16[4,512,128]{2,1,0:T(8,128)(2,1)S(1)} %pad_maximum_fusion.1.refs_0_), channel_id=1, source_target_pairs={{0,1},{1,0},{2,3},{3,2},{4,5},{5,4},{6,7},{7,6},{8,9},{9,8},{10,11... | collective-permute-start | bytes 1572872 | tf_op jit(solution)/shard_map/ppermute | solution.py:570
  84.2 2.0 %collective-permute-done.24 = bf16[2,400,128]{2,1,0:T(8,128)(2,1)S(1)} collective-permute-done((bf16[2,400,128]{2,1,0:T(8,128)(2,1)S(1)}, bf16[2,400,128]{2,1,0:T(8,128)(2,1)S(1)}, u32[]{:S(2)}, u32[]{:S(2)}) %collective-permute-start.24) | collective-permute-done | bytes 204832 | tf_op jit(solution)/shard_map/ppermute | solution.py:570
  86.3 1.6 %collective-permute-start.25 = (bf16[4,400,128]{2,1,0:T(8,128)(2,1)S(1)}, bf16[4,400,128]{2,1,0:T(8,128)(2,1)S(1)}, u32[]{:S(2)}, u32[]{:S(2)}) collective-permute-start(bf16[4,400,128]{2,1,0:T(8,128)(2,1)S(1)} %pad_maximum_fusion.2.refs_0_), channel_id=1, source_target_pairs={{0,4},{1,3},{2,6},{3,1},{4,0},{5,7},{6,2},{7,5},{8,12},{9,11},{10,... | collective-permute-start | bytes 1228808 | tf_op jit(solution)/shard_map/ppermute | solution.py:570
  89.5 4.4 %collective-permute-start.31 = (bf16[4,640,128]{2,1,0:T(8,128)(2,1)S(1)}, bf16[4,640,128]{2,1,0:T(8,128)(2,1)S(1)}, u32[]{:S(2)}, u32[]{:S(2)}) collective-permute-start(bf16[4,640,128]{2,1,0:T(8,128)(2,1)S(1)} %collective-permute-done.29.refs_1_), channel_id=1, source_target_pairs={{0,1},{1,0},{2,3},{3,2},{4,5},{5,4},{6,7},{7,6},{8,9},{9,8},{10,11... | collective-permute-start | bytes 1966088 | tf_op jit(solution)/shard_map/ppermute | solution.py:570
  94.3 3.9 %collective-permute-start.27 = (bf16[4,400,128]{2,1,0:T(8,128)(2,1)S(1)}, bf16[4,400,128]{2,1,0:T(8,128)(2,1)S(1)}, u32[]{:S(2)}, u32[]{:S(2)}) collective-permute-start(bf16[4,400,128]{2,1,0:T(8,128)(2,1)S(1)} %collective-permute-done.25.refs_1_), channel_id=1, source_target_pairs={{0,1},{1,0},{2,3},{3,2},{4,5},{5,4},{6,7},{7,6},{8,9},{9,8},{10,11... | collective-permute-start | bytes 1228808 | tf_op jit(solution)/shard_map/ppermute | solution.py:570
  98.2 2.2 %gather_down.1 = f32[2048,512]{1,0:T(8,128)} custom-call(bf16[4,512,128]{2,1,0:T(8,128)(2,1)S(1)} %pad_maximum_fusion.1.refs_0_, bf16[4,512,128]{2,1,0:T(8,128)(2,1)S(1)} %collective-permute-done.36.refs_1_, bf16[4,512,128]{2,1,0:T(8,128)(2,1)S(1)} %collective-permute-done.37.refs_2_, bf16[4,512,128]{2,1,0:T(8,128)(2,1)S(1)} %collective-permute-done.38.refs_3_), custom_call_target="tpu_custom_call" | custom-call | tf_op jit(solution)/shard_map/gather_down/pallas_call | solution.py:500
  100.4 2.5 %gather_proj.1 = (f32[512,1536]{1,0:T(8,128)}, f32[512]{0:T(512)}, f32[512]{0:T(512)}, f32[512]{0:T(512)}, f32[512]{0:T(512)}, /*index=5*/f32[512]{0:T(512)}, f3...) custom-call(bf16[4,400,128]{2,1,0:T(8,128)(2,1)S(1)} %pad_maximum_fusion.2.refs_0_, ...), custom_call_target="tpu_custom_call" | custom-call | tf_op jit(solution)/shard_map/gather_proj/pallas_call | solution.py:500
  102.9 2.6 %gather_up.1 = (f32[512,2048]{1,0:T(8,128)}, f32[512,512]{1,0:T(8,128)}) custom-call(bf16[4,640,128]{2,1,0:T(8,128)(2,1)S(1)} %pad_maximum_fusion.refs_0_, bf16[4,640,128]{2,1,0:T(8,128)(2,1)S(1)} %collective-permute-done.29.refs_1_, bf16[4,640,128]{2,1,0:T(8,128)(2,1)S(1)} %collective-permute-done.30.refs_2_, ...), custom_call_target="tpu_custom_call" | custom-call | flops 9200000000 | tf_op jit(solution)/shard_map/gather_up/pallas_call | solution.py:500
  (88 shorter events, 28.8 us)
Async XLA Ops:
  4.7 8.9 %collective-permute-start.5 = (bf16[80,512]{1,0:T(8,128)(2,1)S(1)}, bf16[80,512]{1,0:T(8,128)(2,1)S(1)}, u32[]{:S(2)}, u32[]{:S(2)}) collective-permute-start(bf16[80,512]{1,0:T(8,128)(2,1)S(1)} %get-tuple-element.94), channel_id=1, source_target_pairs={{0,3},{1,2},{2,1},{3,0},{4,7},{5,6},{6,5},{7,4},{8,11},{9,10},{10,... | collective-permute-start | bytes 245768 | tf_op jit(solution)/shard_map/ppermute | solution.py:570
  6.4 7.2 %collective-permute-start.4 = (bf16[80,512]{1,0:T(8,128)(2,1)S(1)}, bf16[80,512]{1,0:T(8,128)(2,1)S(1)}, u32[]{:S(2)}, u32[]{:S(2)}) collective-permute-start(bf16[80,512]{1,0:T(8,128)(2,1)S(1)} %get-tuple-element.92), channel_id=1, source_target_pairs={{0,2},{1,3},{2,0},{3,1},{4,6},{5,7},{6,4},{7,5},{8,10},{9,11},{10,... | collective-permute-start | bytes 245768 | tf_op jit(solution)/shard_map/ppermute | solution.py:570
  6.4 7.2 %collective-permute-start.3 = (bf16[80,512]{1,0:T(8,128)(2,1)S(1)}, bf16[80,512]{1,0:T(8,128)(2,1)S(1)}, u32[]{:S(2)}, u32[]{:S(2)}) collective-permute-start(bf16[80,512]{1,0:T(8,128)(2,1)S(1)} %get-tuple-element.90), channel_id=1, source_target_pairs={{0,1},{1,0},{2,3},{3,2},{4,5},{5,4},{6,7},{7,6},{8,9},{9,8},{10,11... | collective-permute-start | bytes 245768 | tf_op jit(solution)/shard_map/ppermute | solution.py:570
  17.6 6.4 %collective-permute-start.7 = (bf16[8,640,128]{2,1,0:T(8,128)(2,1)S(1)}, bf16[8,640,128]{2,1,0:T(8,128)(2,1)S(1)}, u32[]{:S(2)}, u32[]{:S(2)}) collective-permute-start(bf16[8,640,128]{2,1,0:T(8,128)(2,1)S(1)} %get-tuple-element.119), channel_id=1, source_target_pairs={{0,1},{1,0},{2,3},{3,2},{4,5},{5,4},{6,7},{7,6},{8,9},{9,8},{10,11... | collective-permute-start | bytes 3932168 | tf_op jit(solution)/shard_map/ppermute | solution.py:570
  18.5 8.4 %collective-permute-start.17 = (bf16[4,512,128]{2,1,0:T(8,128)(2,1)S(1)}, bf16[4,512,128]{2,1,0:T(8,128)(2,1)S(1)}, u32[]{:S(2)}, u32[]{:S(2)}) collective-permute-start(bf16[4,512,128]{2,1,0:T(8,128)(2,1)S(1)} %get-tuple-element.155), channel_id=1, source_target_pairs={{0,8},{1,5},{2,10},{3,7},{4,12},{5,1},{6,14},{7,3},{8,0},{9,13},{1... | collective-permute-start | bytes 1572872 | tf_op jit(solution)/shard_map/ppermute | solution.py:570
  24.4 9.9 %collective-permute-start.8 = (bf16[4,640,128]{2,1,0:T(8,128)(2,1)S(1)}, bf16[4,640,128]{2,1,0:T(8,128)(2,1)S(1)}, u32[]{:S(2)}, u32[]{:S(2)}) collective-permute-start(bf16[4,640,128]{2,1,0:T(8,128)(2,1)S(1)} %get-tuple-element.121), channel_id=1, source_target_pairs={{0,4},{1,9},{2,6},{3,11},{4,0},{5,13},{6,2},{7,15},{8,12},{9,1},{1... | collective-permute-start | bytes 1966088 | tf_op jit(solution)/shard_map/ppermute | solution.py:570
  27.0 6.9 %collective-permute-start.18 = (bf16[2,512,128]{2,1,0:T(8,128)(2,1)S(1)}, bf16[2,512,128]{2,1,0:T(8,128)(2,1)S(1)}, u32[]{:S(2)}, u32[]{:S(2)}) collective-permute-start(bf16[2,512,128]{2,1,0:T(8,128)(2,1)S(1)} %get-tuple-element.131), channel_id=1, source_target_pairs={{0,2},{1,3},{2,0},{3,1},{4,6},{5,7},{6,4},{7,5},{8,10},{9,11},{10,... | collective-permute-start | bytes 786440 | tf_op jit(solution)/shard_map/ppermute | solution.py:570
  28.4 12.3 %collective-permute-start.14 = (bf16[8,400,128]{2,1,0:T(8,128)(2,1)S(1)}, bf16[8,400,128]{2,1,0:T(8,128)(2,1)S(1)}, u32[]{:S(2)}, u32[]{:S(2)}) collective-permute-start(bf16[8,400,128]{2,1,0:T(8,128)(2,1)S(1)} %get-tuple-element.128), channel_id=1, source_target_pairs={{0,1},{1,0},{2,3},{3,2},{4,5},{5,4},{6,7},{7,6},{8,9},{9,8},{10,11... | collective-permute-start | bytes 2457608 | tf_op jit(solution)/shard_map/ppermute | solution.py:570
  40.9 11.3 %collective-permute-start.15 = (bf16[4,400,128]{2,1,0:T(8,128)(2,1)S(1)}, bf16[4,400,128]{2,1,0:T(8,128)(2,1)S(1)}, u32[]{:S(2)}, u32[]{:S(2)}) collective-permute-start(bf16[4,400,128]{2,1,0:T(8,128)(2,1)S(1)} %get-tuple-element.157), channel_id=1, source_target_pairs={{0,4},{1,3},{2,6},{3,1},{4,0},{5,7},{6,2},{7,5},{8,12},{9,11},{10,... | collective-permute-start | bytes 1228808 | tf_op jit(solution)/shard_map/ppermute | solution.py:570
  44.0 23.9 %collective-permute-start.34 = (bf16[1,512,128]{2,1,0:T(8,128)(2,1)S(1)}, bf16[1,512,128]{2,1,0:T(8,128)(2,1)S(1)}, u32[]{:S(2)}, u32[]{:S(2)}) collective-permute-start(bf16[1,512,128]{2,1,0:T(8,128)(2,1)S(1)} %add_convert_fusion.16), channel_id=1, source_target_pairs={{0,4},{1,9},{2,6},{3,11},{4,0},{5,13},{6,2},{7,15},{8,12},{9,1},{1... | collective-permute-start | bytes 393224 | tf_op jit(solution)/shard_map/ppermute | solution.py:570
  46.8 7.6 %collective-permute-start.21 = (bf16[1,640,128]{2,1,0:T(8,128)(2,1)S(1)}, bf16[1,640,128]{2,1,0:T(8,128)(2,1)S(1)}, u32[]{:S(2)}, u32[]{:S(2)}) collective-permute-start(bf16[1,640,128]{2,1,0:T(8,128)(2,1)S(1)} %add_convert_fusion.13), channel_id=1, source_target_pairs={{0,16},{1,17},{2,18},{3,19},{4,20},{5,21},{6,22},{7,23},{8,24},{9,... | collective-permute-start | bytes 491528 | tf_op jit(solution)/shard_map/ppermute | solution.py:570
  52.3 10.6 %collective-permute-start.16 = (bf16[2,400,128]{2,1,0:T(8,128)(2,1)S(1)}, bf16[2,400,128]{2,1,0:T(8,128)(2,1)S(1)}, u32[]{:S(2)}, u32[]{:S(2)}) collective-permute-start(bf16[2,400,128]{2,1,0:T(8,128)(2,1)S(1)} %get-tuple-element.129), channel_id=1, source_target_pairs={{0,8},{1,9},{2,10},{3,11},{4,12},{5,13},{6,14},{7,15},{8,0},{9,1},... | collective-permute-start | bytes 614408 | tf_op jit(solution)/shard_map/ppermute | solution.py:570
  54.5 9.4 %collective-permute-start.22 = (bf16[1,640,128]{2,1,0:T(8,128)(2,1)S(1)}, bf16[1,640,128]{2,1,0:T(8,128)(2,1)S(1)}, u32[]{:S(2)}, u32[]{:S(2)}) collective-permute-start(bf16[1,640,128]{2,1,0:T(8,128)(2,1)S(1)} %add_convert_fusion.12), channel_id=1, source_target_pairs={{0,2},{1,5},{2,0},{3,7},{4,6},{5,1},{6,4},{7,3},{8,10},{9,13},{10,... | collective-permute-start | bytes 491528 | tf_op jit(solution)/shard_map/ppermute | solution.py:570
  56.6 7.4 %collective-permute-start.13 = (bf16[128,512]{1,0:T(8,128)(2,1)S(1)}, bf16[128,512]{1,0:T(8,128)(2,1)S(1)}, u32[]{:S(2)}, u32[]{:S(2)}) collective-permute-start(bf16[128,512]{1,0:T(8,128)(2,1)S(1)} %slice.156), channel_id=1, source_target_pairs={{0,1},{1,0},{2,3},{3,2},{4,5},{5,4},{6,7},{7,6},{8,9},{9,8},{10,11... | collective-permute-start | bytes 393224 | tf_op jit(solution)/shard_map/ppermute | solution.py:570
  64.0 8.5 %collective-permute-start.28 = (bf16[2,640,128]{2,1,0:T(8,128)(2,1)S(1)}, bf16[2,640,128]{2,1,0:T(8,128)(2,1)S(1)}, u32[]{:S(2)}, u32[]{:S(2)}) collective-permute-start(bf16[2,640,128]{2,1,0:T(8,128)(2,1)S(1)} %pad_maximum_fusion.3), channel_id=1, source_target_pairs={{0,8},{1,3},{2,10},{3,1},{4,12},{5,7},{6,14},{7,5},{8,0},{9,11},{1... | collective-permute-start | bytes 983048 | tf_op jit(solution)/shard_map/ppermute | solution.py:570
  67.9 10.9 %collective-permute-start.35 = (bf16[2,512,128]{2,1,0:T(8,128)(2,1)S(1)}, bf16[2,512,128]{2,1,0:T(8,128)(2,1)S(1)}, u32[]{:S(2)}, u32[]{:S(2)}) collective-permute-start(bf16[2,512,128]{2,1,0:T(8,128)(2,1)S(1)} %pad_maximum_fusion.4), channel_id=1, source_target_pairs={{0,2},{1,3},{2,0},{3,1},{4,6},{5,7},{6,4},{7,5},{8,10},{9,11},{10,... | collective-permute-start | bytes 786440 | tf_op jit(solution)/shard_map/ppermute | solution.py:570
  68.5 6.6 %collective-permute-start.11 = (bf16[128,512]{1,0:T(8,128)(2,1)S(1)}, bf16[128,512]{1,0:T(8,128)(2,1)S(1)}, u32[]{:S(2)}, u32[]{:S(2)}) collective-permute-start(bf16[128,512]{1,0:T(8,128)(2,1)S(1)} %get-tuple-element.122), channel_id=1, source_target_pairs={{0,1},{1,0},{2,3},{3,2},{4,5},{5,4},{6,7},{7,6},{8,9},{9,8},{10,11... | collective-permute-start | bytes 393224 | tf_op jit(solution)/shard_map/ppermute | solution.py:570
  72.6 16.9 %collective-permute-start.29 = (bf16[4,640,128]{2,1,0:T(8,128)(2,1)S(1)}, bf16[4,640,128]{2,1,0:T(8,128)(2,1)S(1)}, u32[]{:S(2)}, u32[]{:S(2)}) collective-permute-start(bf16[4,640,128]{2,1,0:T(8,128)(2,1)S(1)} %pad_maximum_fusion.refs_0_), channel_id=1, source_target_pairs={{0,4},{1,9},{2,6},{3,11},{4,0},{5,13},{6,2},{7,15},{8,12},{9,1},{1... | collective-permute-start | bytes 1966088 | tf_op jit(solution)/shard_map/ppermute | solution.py:570
  76.3 9.9 %collective-permute-start.24 = (bf16[2,400,128]{2,1,0:T(8,128)(2,1)S(1)}, bf16[2,400,128]{2,1,0:T(8,128)(2,1)S(1)}, u32[]{:S(2)}, u32[]{:S(2)}) collective-permute-start(bf16[2,400,128]{2,1,0:T(8,128)(2,1)S(1)} %pad_maximum_fusion.5), channel_id=1, source_target_pairs={{0,8},{1,9},{2,10},{3,11},{4,12},{5,13},{6,14},{7,15},{8,0},{9,1},... | collective-permute-start | bytes 614408 | tf_op jit(solution)/shard_map/ppermute | solution.py:570
  78.9 14.9 %collective-permute-start.36 = (bf16[4,512,128]{2,1,0:T(8,128)(2,1)S(1)}, bf16[4,512,128]{2,1,0:T(8,128)(2,1)S(1)}, u32[]{:S(2)}, u32[]{:S(2)}) collective-permute-start(bf16[4,512,128]{2,1,0:T(8,128)(2,1)S(1)} %pad_maximum_fusion.1.refs_0_), channel_id=1, source_target_pairs={{0,8},{1,5},{2,10},{3,7},{4,12},{5,1},{6,14},{7,3},{8,0},{9,13},{1... | collective-permute-start | bytes 1572872 | tf_op jit(solution)/shard_map/ppermute | solution.py:570
  79.0 15.0 %collective-permute-start.37 = (bf16[4,512,128]{2,1,0:T(8,128)(2,1)S(1)}, bf16[4,512,128]{2,1,0:T(8,128)(2,1)S(1)}, u32[]{:S(2)}, u32[]{:S(2)}) collective-permute-start(bf16[4,512,128]{2,1,0:T(8,128)(2,1)S(1)} %pad_maximum_fusion.1.refs_0_), channel_id=1, source_target_pairs={{0,1},{1,0},{2,3},{3,2},{4,5},{5,4},{6,7},{7,6},{8,9},{9,8},{10,11... | collective-permute-start | bytes 1572872 | tf_op jit(solution)/shard_map/ppermute | solution.py:570
  86.3 8.0 %collective-permute-start.25 = (bf16[4,400,128]{2,1,0:T(8,128)(2,1)S(1)}, bf16[4,400,128]{2,1,0:T(8,128)(2,1)S(1)}, u32[]{:S(2)}, u32[]{:S(2)}) collective-permute-start(bf16[4,400,128]{2,1,0:T(8,128)(2,1)S(1)} %pad_maximum_fusion.2.refs_0_), channel_id=1, source_target_pairs={{0,4},{1,3},{2,6},{3,1},{4,0},{5,7},{6,2},{7,5},{8,12},{9,11},{10,... | collective-permute-start | bytes 1228808 | tf_op jit(solution)/shard_map/ppermute | solution.py:570
  87.9 15.0 %collective-permute-start.30 = (bf16[4,640,128]{2,1,0:T(8,128)(2,1)S(1)}, bf16[4,640,128]{2,1,0:T(8,128)(2,1)S(1)}, u32[]{:S(2)}, u32[]{:S(2)}) collective-permute-start(bf16[4,640,128]{2,1,0:T(8,128)(2,1)S(1)} %pad_maximum_fusion.refs_0_), channel_id=1, source_target_pairs={{0,1},{1,0},{2,3},{3,2},{4,5},{5,4},{6,7},{7,6},{8,9},{9,8},{10,11... | collective-permute-start | bytes 1966088 | tf_op jit(solution)/shard_map/ppermute | solution.py:570
  89.5 13.4 %collective-permute-start.31 = (bf16[4,640,128]{2,1,0:T(8,128)(2,1)S(1)}, bf16[4,640,128]{2,1,0:T(8,128)(2,1)S(1)}, u32[]{:S(2)}, u32[]{:S(2)}) collective-permute-start(bf16[4,640,128]{2,1,0:T(8,128)(2,1)S(1)} %collective-permute-done.29.refs_1_), channel_id=1, source_target_pairs={{0,1},{1,0},{2,3},{3,2},{4,5},{5,4},{6,7},{7,6},{8,9},{9,8},{10,11... | collective-permute-start | bytes 1966088 | tf_op jit(solution)/shard_map/ppermute | solution.py:570
  (16 other events, 83.9 us)

commit v5 on v4

--- a/solution.py
+++ b/solution.py
@@ -114,12 +114,20 @@
 
 
 def weight_grad(keep_ref, send_ref, core, place, depth, order, pieces, base, lhs, rhs_ref):
-    stripe = max(pieces.height, min(512, pieces.rows))
-    for out_ref, owner in ((send_ref, core ^ 1), (keep_ref, core)):
-        rhs = rhs_ref[:, pl.ds(pl.multiple_of(owner * pieces.half, LANES), pieces.half)]
-        for start in range(0, pieces.rows, stripe):
-            value = dot_tn(lhs[:, start : start + stripe], rhs)
-            store_pieces(out_ref, owner, place, depth, order, pieces, base, value, start)
+    stripe = max(pieces.height, min(256, pieces.rows))
+    sides = ((send_ref, core ^ 1), (keep_ref, core))
+    rhs = jnp.concatenate(
+        [
+            rhs_ref[:, pl.ds(pl.multiple_of(owner * pieces.half, LANES), pieces.half)]
+            for _, owner in sides
+        ],
+        axis=1,
+    )
+    for start in range(0, pieces.rows, stripe):
+        value = dot_tn(lhs[:, start : start + stripe], rhs)
+        for side, (out_ref, owner) in enumerate(sides):
+            part = value[:, side * pieces.half : (side + 1) * pieces.half]
+            store_pieces(out_ref, owner, place, depth, order, pieces, base, part, start)
 
 
 def place_of():

time: 106 us -> 106 us (level)
  no operation moved by 1% of the time
where the time goes in v5:
time: 106 us
  starting transfers between devices  61.2 us (58%)
  Pallas kernels  23.4 us (22%)
  waiting for transfers between devices  18 us (17%)
  other arithmetic  1.92 us (2%)
  between operations  1.13 us (1%)
    ppermute x39, starting transfers between devices, send(): return lax.ppermute(value, ('dp', 'blk'), table)  61.2 us
    pallas_call x10, Pallas kernels, call(): pl.pallas_call(kernel, out_shape=tuple(outs), in_specs=[FAR] * far + [WHO...  23.4 us
    ppermute x39, waiting for transfers between devices, send(): return lax.ppermute(value, ('dp', 'blk'), table)  18 us
  transfers between devices with their start and end apart: 39, of which 13 were waited for; matrix products, arithmetic and copies ran while one was open for 2% of the time, Pallas kernels for 18%

profile of v5, /device:TPU:1, one launch (start us, length us, event | category | flops | bytes accessed | tf_op | source)
XLA Modules:
  0.0 105.6 jit_solution(14655894048057720328)
XLA Ops:
  1.9 2.7 %collective-permute-start.1 = (bf16[64,512]{1,0:T(8,128)(2,1)S(1)}, bf16[64,512]{1,0:T(8,128)(2,1)S(1)}, u32[]{:S(2)}, u32[]{:S(2)}) collective-permute-start(bf16[64,512]{1,0:T(8,128)(2,1)S(1)} %get-tuple-element.86), channel_id=1, source_target_pairs={{0,2},{1,3},{2,0},{3,1},{4,6},{5,7},{6,4},{7,5},{8,10},{9,11},{10,... | collective-permute-start | bytes 196616 | tf_op jit(solution)/shard_map/ppermute | solution.py:578
  4.7 1.7 %collective-permute-start.5 = (bf16[80,512]{1,0:T(8,128)(2,1)S(1)}, bf16[80,512]{1,0:T(8,128)(2,1)S(1)}, u32[]{:S(2)}, u32[]{:S(2)}) collective-permute-start(bf16[80,512]{1,0:T(8,128)(2,1)S(1)} %get-tuple-element.94), channel_id=1, source_target_pairs={{0,3},{1,2},{2,1},{3,0},{4,7},{5,6},{6,5},{7,4},{8,11},{9,10},{10,... | collective-permute-start | bytes 245768 | tf_op jit(solution)/shard_map/ppermute | solution.py:578
  9.3 4.3 %forward.1 = (bf16[512,512]{1,0:T(8,128)(2,1)S(1)}, bf16[512,2048]{1,0:T(8,128)(2,1)S(1)}, bf16[2048,512]{1,0:T(8,128)(2,1)S(1)}, bf16[256,1536]{1,0:T(8,128)(2,...) custom-call(bf16[512,512]{1,0:T(8,128)(2,1)} %refs_0_.3, ...), custom_call_target="tpu_custom_call" | custom-call | flops 17250000896 | tf_op jit(solution)/shard_map/forward/pallas_call | solution.py:508
  14.6 3.1 %middle.1 = (bf16[8,640,128]{2,1,0:T(8,128)(2,1)S(1)}, bf16[8,640,128]{2,1,0:T(8,128)(2,1)S(1)}, f32[256,512]{1,0:T(8,128)S(1)}, bf16[256,512]{1,0:T(8,128)(2,1)...) custom-call(bf16[256,512]{1,0:T(8,128)(2,1)S(1)} %get-tuple-element.103.g_ref, ...), custom_call_target="tpu_custom_call" | custom-call | tf_op jit(solution)/shard_map/middle/pallas_call | solution.py:508
  19.8 4.3 %backward.1 = (bf16[128,512]{1,0:T(8,128)(2,1)S(1)}, bf16[128,512]{1,0:T(8,128)(2,1)S(1)}, bf16[256,512]{1,0:T(8,128)(2,1)S(1)}, bf16[8,400,128]{2,1,0:T(8,128)(2,1)S(1)}, bf16[8,400,128]{2,1,0:T(8,128)(2,1)S(1)}) custom-call(bf16[64,512]{1,0:T(8,128)(2,1)S(1)} %get-tuple-element.84.refs_3_.refs_0_, ...), custom_call_target="tpu_custom_call" | custom-call | tf_op jit(solution)/shard_map/backward/pallas_call | solution.py:508
  29.6 4.2 %collective-permute-done.18 = bf16[2,512,128]{2,1,0:T(8,128)(2,1)S(1)} collective-permute-done((bf16[2,512,128]{2,1,0:T(8,128)(2,1)S(1)}, bf16[2,512,128]{2,1,0:T(8,128)(2,1)S(1)}, u32[]{:S(2)}, u32[]{:S(2)}) %collective-permute-start.18) | collective-permute-done | bytes 262176 | tf_op jit(solution)/shard_map/ppermute | solution.py:578
  38.3 2.4 %collective-permute-start.33 = (bf16[1,512,128]{2,1,0:T(8,128)(2,1)S(1)}, bf16[1,512,128]{2,1,0:T(8,128)(2,1)S(1)}, u32[]{:S(2)}, u32[]{:S(2)}) collective-permute-start(bf16[1,512,128]{2,1,0:T(8,128)(2,1)S(1)} %add_convert_fusion.17), channel_id=1, source_target_pairs={{0,16},{1,17},{2,18},{3,19},{4,20},{5,21},{6,22},{7,23},{8,24},{9,... | collective-permute-start | bytes 393224 | tf_op jit(solution)/shard_map/ppermute | solution.py:578
  44.0 1.8 %collective-permute-start.34 = (bf16[1,512,128]{2,1,0:T(8,128)(2,1)S(1)}, bf16[1,512,128]{2,1,0:T(8,128)(2,1)S(1)}, u32[]{:S(2)}, u32[]{:S(2)}) collective-permute-start(bf16[1,512,128]{2,1,0:T(8,128)(2,1)S(1)} %add_convert_fusion.16), channel_id=1, source_target_pairs={{0,4},{1,9},{2,6},{3,11},{4,0},{5,13},{6,2},{7,15},{8,12},{9,1},{1... | collective-permute-start | bytes 393224 | tf_op jit(solution)/shard_map/ppermute | solution.py:578
  46.8 4.1 %collective-permute-start.21 = (bf16[1,640,128]{2,1,0:T(8,128)(2,1)S(1)}, bf16[1,640,128]{2,1,0:T(8,128)(2,1)S(1)}, u32[]{:S(2)}, u32[]{:S(2)}) collective-permute-start(bf16[1,640,128]{2,1,0:T(8,128)(2,1)S(1)} %add_convert_fusion.13), channel_id=1, source_target_pairs={{0,16},{1,17},{2,18},{3,19},{4,20},{5,21},{6,22},{7,23},{8,24},{9,... | collective-permute-start | bytes 491528 | tf_op jit(solution)/shard_map/ppermute | solution.py:578
  52.4 2.1 %collective-permute-done.21 = bf16[1,640,128]{2,1,0:T(8,128)(2,1)S(1)} collective-permute-done((bf16[1,640,128]{2,1,0:T(8,128)(2,1)S(1)}, bf16[1,640,128]{2,1,0:T(8,128)(2,1)S(1)}, u32[]{:S(2)}, u32[]{:S(2)}) %collective-permute-start.21) | collective-permute-done | bytes 163872 | tf_op jit(solution)/shard_map/ppermute | solution.py:578
  54.5 2.1 %collective-permute-start.22 = (bf16[1,640,128]{2,1,0:T(8,128)(2,1)S(1)}, bf16[1,640,128]{2,1,0:T(8,128)(2,1)S(1)}, u32[]{:S(2)}, u32[]{:S(2)}) collective-permute-start(bf16[1,640,128]{2,1,0:T(8,128)(2,1)S(1)} %add_convert_fusion.12), channel_id=1, source_target_pairs={{0,2},{1,5},{2,0},{3,7},{4,6},{5,1},{6,4},{7,3},{8,10},{9,13},{10,... | collective-permute-start | bytes 491528 | tf_op jit(solution)/shard_map/ppermute | solution.py:578
  56.6 6.4 %collective-permute-start.13 = (bf16[128,512]{1,0:T(8,128)(2,1)S(1)}, bf16[128,512]{1,0:T(8,128)(2,1)S(1)}, u32[]{:S(2)}, u32[]{:S(2)}) collective-permute-start(bf16[128,512]{1,0:T(8,128)(2,1)S(1)} %slice.156), channel_id=1, source_target_pairs={{0,1},{1,0},{2,3},{3,2},{4,5},{5,4},{6,7},{7,6},{8,9},{9,8},{10,11... | collective-permute-start | bytes 393224 | tf_op jit(solution)/shard_map/ppermute | solution.py:578
  64.2 3.6 %collective-permute-done.19 = bf16[1,400,128]{2,1,0:T(8,128)(2,1)S(1)} collective-permute-done((bf16[1,400,128]{2,1,0:T(8,128)(2,1)S(1)}, bf16[1,400,128]{2,1,0:T(8,128)(2,1)S(1)}, u32[]{:S(2)}, u32[]{:S(2)}) %collective-permute-start.19) | collective-permute-done | bytes 102432 | tf_op jit(solution)/shard_map/ppermute | solution.py:578
  68.5 3.8 %collective-permute-start.11 = (bf16[128,512]{1,0:T(8,128)(2,1)S(1)}, bf16[128,512]{1,0:T(8,128)(2,1)S(1)}, u32[]{:S(2)}, u32[]{:S(2)}) collective-permute-start(bf16[128,512]{1,0:T(8,128)(2,1)S(1)} %get-tuple-element.122), channel_id=1, source_target_pairs={{0,1},{1,0},{2,3},{3,2},{4,5},{5,4},{6,7},{7,6},{8,9},{9,8},{10,11... | collective-permute-start | bytes 393224 | tf_op jit(solution)/shard_map/ppermute | solution.py:578
  72.6 2.5 %collective-permute-start.29 = (bf16[4,640,128]{2,1,0:T(8,128)(2,1)S(1)}, bf16[4,640,128]{2,1,0:T(8,128)(2,1)S(1)}, u32[]{:S(2)}, u32[]{:S(2)}) collective-permute-start(bf16[4,640,128]{2,1,0:T(8,128)(2,1)S(1)} %pad_maximum_fusion.refs_0_), channel_id=1, source_target_pairs={{0,4},{1,9},{2,6},{3,11},{4,0},{5,13},{6,2},{7,15},{8,12},{9,1},{1... | collective-permute-start | bytes 1966088 | tf_op jit(solution)/shard_map/ppermute | solution.py:578
  76.3 2.5 %collective-permute-start.24 = (bf16[2,400,128]{2,1,0:T(8,128)(2,1)S(1)}, bf16[2,400,128]{2,1,0:T(8,128)(2,1)S(1)}, u32[]{:S(2)}, u32[]{:S(2)}) collective-permute-start(bf16[2,400,128]{2,1,0:T(8,128)(2,1)S(1)} %pad_maximum_fusion.5), channel_id=1, source_target_pairs={{0,8},{1,9},{2,10},{3,11},{4,12},{5,13},{6,14},{7,15},{8,0},{9,1},... | collective-permute-start | bytes 614408 | tf_op jit(solution)/shard_map/ppermute | solution.py:578
  78.9 5.3 %collective-permute-start.37 = (bf16[4,512,128]{2,1,0:T(8,128)(2,1)S(1)}, bf16[4,512,128]{2,1,0:T(8,128)(2,1)S(1)}, u32[]{:S(2)}, u32[]{:S(2)}) collective-permute-start(bf16[4,512,128]{2,1,0:T(8,128)(2,1)S(1)} %pad_maximum_fusion.1.refs_0_), channel_id=1, source_target_pairs={{0,1},{1,0},{2,3},{3,2},{4,5},{5,4},{6,7},{7,6},{8,9},{9,8},{10,11... | collective-permute-start | bytes 1572872 | tf_op jit(solution)/shard_map/ppermute | solution.py:578
  84.2 2.0 %collective-permute-done.24 = bf16[2,400,128]{2,1,0:T(8,128)(2,1)S(1)} collective-permute-done((bf16[2,400,128]{2,1,0:T(8,128)(2,1)S(1)}, bf16[2,400,128]{2,1,0:T(8,128)(2,1)S(1)}, u32[]{:S(2)}, u32[]{:S(2)}) %collective-permute-start.24) | collective-permute-done | bytes 204832 | tf_op jit(solution)/shard_map/ppermute | solution.py:578
  86.2 1.6 %collective-permute-start.25 = (bf16[4,400,128]{2,1,0:T(8,128)(2,1)S(1)}, bf16[4,400,128]{2,1,0:T(8,128)(2,1)S(1)}, u32[]{:S(2)}, u32[]{:S(2)}) collective-permute-start(bf16[4,400,128]{2,1,0:T(8,128)(2,1)S(1)} %pad_maximum_fusion.2.refs_0_), channel_id=1, source_target_pairs={{0,4},{1,3},{2,6},{3,1},{4,0},{5,7},{6,2},{7,5},{8,12},{9,11},{10,... | collective-permute-start | bytes 1228808 | tf_op jit(solution)/shard_map/ppermute | solution.py:578
  89.4 4.4 %collective-permute-start.31 = (bf16[4,640,128]{2,1,0:T(8,128)(2,1)S(1)}, bf16[4,640,128]{2,1,0:T(8,128)(2,1)S(1)}, u32[]{:S(2)}, u32[]{:S(2)}) collective-permute-start(bf16[4,640,128]{2,1,0:T(8,128)(2,1)S(1)} %collective-permute-done.29.refs_1_), channel_id=1, source_target_pairs={{0,1},{1,0},{2,3},{3,2},{4,5},{5,4},{6,7},{7,6},{8,9},{9,8},{10,11... | collective-permute-start | bytes 1966088 | tf_op jit(solution)/shard_map/ppermute | solution.py:578
  94.3 3.9 %collective-permute-start.27 = (bf16[4,400,128]{2,1,0:T(8,128)(2,1)S(1)}, bf16[4,400,128]{2,1,0:T(8,128)(2,1)S(1)}, u32[]{:S(2)}, u32[]{:S(2)}) collective-permute-start(bf16[4,400,128]{2,1,0:T(8,128)(2,1)S(1)} %collective-permute-done.25.refs_1_), channel_id=1, source_target_pairs={{0,1},{1,0},{2,3},{3,2},{4,5},{5,4},{6,7},{7,6},{8,9},{9,8},{10,11... | collective-permute-start | bytes 1228808 | tf_op jit(solution)/shard_map/ppermute | solution.py:578
  98.2 2.2 %gather_down.1 = f32[2048,512]{1,0:T(8,128)} custom-call(bf16[4,512,128]{2,1,0:T(8,128)(2,1)S(1)} %pad_maximum_fusion.1.refs_0_, bf16[4,512,128]{2,1,0:T(8,128)(2,1)S(1)} %collective-permute-done.36.refs_1_, bf16[4,512,128]{2,1,0:T(8,128)(2,1)S(1)} %collective-permute-done.37.refs_2_, bf16[4,512,128]{2,1,0:T(8,128)(2,1)S(1)} %collective-permute-done.38.refs_3_), custom_call_target="tpu_custom_call" | custom-call | tf_op jit(solution)/shard_map/gather_down/pallas_call | solution.py:508
  100.4 2.5 %gather_proj.1 = (f32[512,1536]{1,0:T(8,128)}, f32[512]{0:T(512)}, f32[512]{0:T(512)}, f32[512]{0:T(512)}, f32[512]{0:T(512)}, /*index=5*/f32[512]{0:T(512)}, f3...) custom-call(bf16[4,400,128]{2,1,0:T(8,128)(2,1)S(1)} %pad_maximum_fusion.2.refs_0_, ...), custom_call_target="tpu_custom_call" | custom-call | tf_op jit(solution)/shard_map/gather_proj/pallas_call | solution.py:508
  102.9 2.6 %gather_up.1 = (f32[512,2048]{1,0:T(8,128)}, f32[512,512]{1,0:T(8,128)}) custom-call(bf16[4,640,128]{2,1,0:T(8,128)(2,1)S(1)} %pad_maximum_fusion.refs_0_, bf16[4,640,128]{2,1,0:T(8,128)(2,1)S(1)} %collective-permute-done.29.refs_1_, bf16[4,640,128]{2,1,0:T(8,128)(2,1)S(1)} %collective-permute-done.30.refs_2_, ...), custom_call_target="tpu_custom_call" | custom-call | flops 9200000000 | tf_op jit(solution)/shard_map/gather_up/pallas_call | solution.py:508
  (88 shorter events, 28.9 us)
Async XLA Ops:
  1.9 6.4 %collective-permute-start.1 = (bf16[64,512]{1,0:T(8,128)(2,1)S(1)}, bf16[64,512]{1,0:T(8,128)(2,1)S(1)}, u32[]{:S(2)}, u32[]{:S(2)}) collective-permute-start(bf16[64,512]{1,0:T(8,128)(2,1)S(1)} %get-tuple-element.86), channel_id=1, source_target_pairs={{0,2},{1,3},{2,0},{3,1},{4,6},{5,7},{6,4},{7,5},{8,10},{9,11},{10,... | collective-permute-start | bytes 196616 | tf_op jit(solution)/shard_map/ppermute | solution.py:578
  4.7 8.9 %collective-permute-start.5 = (bf16[80,512]{1,0:T(8,128)(2,1)S(1)}, bf16[80,512]{1,0:T(8,128)(2,1)S(1)}, u32[]{:S(2)}, u32[]{:S(2)}) collective-permute-start(bf16[80,512]{1,0:T(8,128)(2,1)S(1)} %get-tuple-element.94), channel_id=1, source_target_pairs={{0,3},{1,2},{2,1},{3,0},{4,7},{5,6},{6,5},{7,4},{8,11},{9,10},{10,... | collective-permute-start | bytes 245768 | tf_op jit(solution)/shard_map/ppermute | solution.py:578
  6.4 7.2 %collective-permute-start.4 = (bf16[80,512]{1,0:T(8,128)(2,1)S(1)}, bf16[80,512]{1,0:T(8,128)(2,1)S(1)}, u32[]{:S(2)}, u32[]{:S(2)}) collective-permute-start(bf16[80,512]{1,0:T(8,128)(2,1)S(1)} %get-tuple-element.92), channel_id=1, source_target_pairs={{0,2},{1,3},{2,0},{3,1},{4,6},{5,7},{6,4},{7,5},{8,10},{9,11},{10,... | collective-permute-start | bytes 245768 | tf_op jit(solution)/shard_map/ppermute | solution.py:578
  6.4 7.2 %collective-permute-start.3 = (bf16[80,512]{1,0:T(8,128)(2,1)S(1)}, bf16[80,512]{1,0:T(8,128)(2,1)S(1)}, u32[]{:S(2)}, u32[]{:S(2)}) collective-permute-start(bf16[80,512]{1,0:T(8,128)(2,1)S(1)} %get-tuple-element.90), channel_id=1, source_target_pairs={{0,1},{1,0},{2,3},{3,2},{4,5},{5,4},{6,7},{7,6},{8,9},{9,8},{10,11... | collective-permute-start | bytes 245768 | tf_op jit(solution)/shard_map/ppermute | solution.py:578
  18.4 8.4 %collective-permute-start.17 = (bf16[4,512,128]{2,1,0:T(8,128)(2,1)S(1)}, bf16[4,512,128]{2,1,0:T(8,128)(2,1)S(1)}, u32[]{:S(2)}, u32[]{:S(2)}) collective-permute-start(bf16[4,512,128]{2,1,0:T(8,128)(2,1)S(1)} %get-tuple-element.155), channel_id=1, source_target_pairs={{0,8},{1,5},{2,10},{3,7},{4,12},{5,1},{6,14},{7,3},{8,0},{9,13},{1... | collective-permute-start | bytes 1572872 | tf_op jit(solution)/shard_map/ppermute | solution.py:578
  24.4 10.0 %collective-permute-start.8 = (bf16[4,640,128]{2,1,0:T(8,128)(2,1)S(1)}, bf16[4,640,128]{2,1,0:T(8,128)(2,1)S(1)}, u32[]{:S(2)}, u32[]{:S(2)}) collective-permute-start(bf16[4,640,128]{2,1,0:T(8,128)(2,1)S(1)} %get-tuple-element.121), channel_id=1, source_target_pairs={{0,4},{1,9},{2,6},{3,11},{4,0},{5,13},{6,2},{7,15},{8,12},{9,1},{1... | collective-permute-start | bytes 1966088 | tf_op jit(solution)/shard_map/ppermute | solution.py:578
  27.0 6.8 %collective-permute-start.18 = (bf16[2,512,128]{2,1,0:T(8,128)(2,1)S(1)}, bf16[2,512,128]{2,1,0:T(8,128)(2,1)S(1)}, u32[]{:S(2)}, u32[]{:S(2)}) collective-permute-start(bf16[2,512,128]{2,1,0:T(8,128)(2,1)S(1)} %get-tuple-element.131), channel_id=1, source_target_pairs={{0,2},{1,3},{2,0},{3,1},{4,6},{5,7},{6,4},{7,5},{8,10},{9,11},{10,... | collective-permute-start | bytes 786440 | tf_op jit(solution)/shard_map/ppermute | solution.py:578
  28.3 12.3 %collective-permute-start.14 = (bf16[8,400,128]{2,1,0:T(8,128)(2,1)S(1)}, bf16[8,400,128]{2,1,0:T(8,128)(2,1)S(1)}, u32[]{:S(2)}, u32[]{:S(2)}) collective-permute-start(bf16[8,400,128]{2,1,0:T(8,128)(2,1)S(1)} %get-tuple-element.128), channel_id=1, source_target_pairs={{0,1},{1,0},{2,3},{3,2},{4,5},{5,4},{6,7},{7,6},{8,9},{9,8},{10,11... | collective-permute-start | bytes 2457608 | tf_op jit(solution)/shard_map/ppermute | solution.py:578
  40.8 11.3 %collective-permute-start.15 = (bf16[4,400,128]{2,1,0:T(8,128)(2,1)S(1)}, bf16[4,400,128]{2,1,0:T(8,128)(2,1)S(1)}, u32[]{:S(2)}, u32[]{:S(2)}) collective-permute-start(bf16[4,400,128]{2,1,0:T(8,128)(2,1)S(1)} %get-tuple-element.157), channel_id=1, source_target_pairs={{0,4},{1,3},{2,6},{3,1},{4,0},{5,7},{6,2},{7,5},{8,12},{9,11},{10,... | collective-permute-start | bytes 1228808 | tf_op jit(solution)/shard_map/ppermute | solution.py:578
  44.0 23.9 %collective-permute-start.34 = (bf16[1,512,128]{2,1,0:T(8,128)(2,1)S(1)}, bf16[1,512,128]{2,1,0:T(8,128)(2,1)S(1)}, u32[]{:S(2)}, u32[]{:S(2)}) collective-permute-start(bf16[1,512,128]{2,1,0:T(8,128)(2,1)S(1)} %add_convert_fusion.16), channel_id=1, source_target_pairs={{0,4},{1,9},{2,6},{3,11},{4,0},{5,13},{6,2},{7,15},{8,12},{9,1},{1... | collective-permute-start | bytes 393224 | tf_op jit(solution)/shard_map/ppermute | solution.py:578
  46.8 7.6 %collective-permute-start.21 = (bf16[1,640,128]{2,1,0:T(8,128)(2,1)S(1)}, bf16[1,640,128]{2,1,0:T(8,128)(2,1)S(1)}, u32[]{:S(2)}, u32[]{:S(2)}) collective-permute-start(bf16[1,640,128]{2,1,0:T(8,128)(2,1)S(1)} %add_convert_fusion.13), channel_id=1, source_target_pairs={{0,16},{1,17},{2,18},{3,19},{4,20},{5,21},{6,22},{7,23},{8,24},{9,... | collective-permute-start | bytes 491528 | tf_op jit(solution)/shard_map/ppermute | solution.py:578
  52.3 10.6 %collective-permute-start.16 = (bf16[2,400,128]{2,1,0:T(8,128)(2,1)S(1)}, bf16[2,400,128]{2,1,0:T(8,128)(2,1)S(1)}, u32[]{:S(2)}, u32[]{:S(2)}) collective-permute-start(bf16[2,400,128]{2,1,0:T(8,128)(2,1)S(1)} %get-tuple-element.129), channel_id=1, source_target_pairs={{0,8},{1,9},{2,10},{3,11},{4,12},{5,13},{6,14},{7,15},{8,0},{9,1},... | collective-permute-start | bytes 614408 | tf_op jit(solution)/shard_map/ppermute | solution.py:578
  54.5 9.4 %collective-permute-start.22 = (bf16[1,640,128]{2,1,0:T(8,128)(2,1)S(1)}, bf16[1,640,128]{2,1,0:T(8,128)(2,1)S(1)}, u32[]{:S(2)}, u32[]{:S(2)}) collective-permute-start(bf16[1,640,128]{2,1,0:T(8,128)(2,1)S(1)} %add_convert_fusion.12), channel_id=1, source_target_pairs={{0,2},{1,5},{2,0},{3,7},{4,6},{5,1},{6,4},{7,3},{8,10},{9,13},{10,... | collective-permute-start | bytes 491528 | tf_op jit(solution)/shard_map/ppermute | solution.py:578
  56.6 7.4 %collective-permute-start.13 = (bf16[128,512]{1,0:T(8,128)(2,1)S(1)}, bf16[128,512]{1,0:T(8,128)(2,1)S(1)}, u32[]{:S(2)}, u32[]{:S(2)}) collective-permute-start(bf16[128,512]{1,0:T(8,128)(2,1)S(1)} %slice.156), channel_id=1, source_target_pairs={{0,1},{1,0},{2,3},{3,2},{4,5},{5,4},{6,7},{7,6},{8,9},{9,8},{10,11... | collective-permute-start | bytes 393224 | tf_op jit(solution)/shard_map/ppermute | solution.py:578
  64.0 8.5 %collective-permute-start.28 = (bf16[2,640,128]{2,1,0:T(8,128)(2,1)S(1)}, bf16[2,640,128]{2,1,0:T(8,128)(2,1)S(1)}, u32[]{:S(2)}, u32[]{:S(2)}) collective-permute-start(bf16[2,640,128]{2,1,0:T(8,128)(2,1)S(1)} %pad_maximum_fusion.3), channel_id=1, source_target_pairs={{0,8},{1,3},{2,10},{3,1},{4,12},{5,7},{6,14},{7,5},{8,0},{9,11},{1... | collective-permute-start | bytes 983048 | tf_op jit(solution)/shard_map/ppermute | solution.py:578
  67.9 10.9 %collective-permute-start.35 = (bf16[2,512,128]{2,1,0:T(8,128)(2,1)S(1)}, bf16[2,512,128]{2,1,0:T(8,128)(2,1)S(1)}, u32[]{:S(2)}, u32[]{:S(2)}) collective-permute-start(bf16[2,512,128]{2,1,0:T(8,128)(2,1)S(1)} %pad_maximum_fusion.4), channel_id=1, source_target_pairs={{0,2},{1,3},{2,0},{3,1},{4,6},{5,7},{6,4},{7,5},{8,10},{9,11},{10,... | collective-permute-start | bytes 786440 | tf_op jit(solution)/shard_map/ppermute | solution.py:578
  68.5 6.6 %collective-permute-start.11 = (bf16[128,512]{1,0:T(8,128)(2,1)S(1)}, bf16[128,512]{1,0:T(8,128)(2,1)S(1)}, u32[]{:S(2)}, u32[]{:S(2)}) collective-permute-start(bf16[128,512]{1,0:T(8,128)(2,1)S(1)} %get-tuple-element.122), channel_id=1, source_target_pairs={{0,1},{1,0},{2,3},{3,2},{4,5},{5,4},{6,7},{7,6},{8,9},{9,8},{10,11... | collective-permute-start | bytes 393224 | tf_op jit(solution)/shard_map/ppermute | solution.py:578
  72.6 16.8 %collective-permute-start.29 = (bf16[4,640,128]{2,1,0:T(8,128)(2,1)S(1)}, bf16[4,640,128]{2,1,0:T(8,128)(2,1)S(1)}, u32[]{:S(2)}, u32[]{:S(2)}) collective-permute-start(bf16[4,640,128]{2,1,0:T(8,128)(2,1)S(1)} %pad_maximum_fusion.refs_0_), channel_id=1, source_target_pairs={{0,4},{1,9},{2,6},{3,11},{4,0},{5,13},{6,2},{7,15},{8,12},{9,1},{1... | collective-permute-start | bytes 1966088 | tf_op jit(solution)/shard_map/ppermute | solution.py:578
  76.3 9.9 %collective-permute-start.24 = (bf16[2,400,128]{2,1,0:T(8,128)(2,1)S(1)}, bf16[2,400,128]{2,1,0:T(8,128)(2,1)S(1)}, u32[]{:S(2)}, u32[]{:S(2)}) collective-permute-start(bf16[2,400,128]{2,1,0:T(8,128)(2,1)S(1)} %pad_maximum_fusion.5), channel_id=1, source_target_pairs={{0,8},{1,9},{2,10},{3,11},{4,12},{5,13},{6,14},{7,15},{8,0},{9,1},... | collective-permute-start | bytes 614408 | tf_op jit(solution)/shard_map/ppermute | solution.py:578
  78.9 14.9 %collective-permute-start.36 = (bf16[4,512,128]{2,1,0:T(8,128)(2,1)S(1)}, bf16[4,512,128]{2,1,0:T(8,128)(2,1)S(1)}, u32[]{:S(2)}, u32[]{:S(2)}) collective-permute-start(bf16[4,512,128]{2,1,0:T(8,128)(2,1)S(1)} %pad_maximum_fusion.1.refs_0_), channel_id=1, source_target_pairs={{0,8},{1,5},{2,10},{3,7},{4,12},{5,1},{6,14},{7,3},{8,0},{9,13},{1... | collective-permute-start | bytes 1572872 | tf_op jit(solution)/shard_map/ppermute | solution.py:578
  78.9 15.0 %collective-permute-start.37 = (bf16[4,512,128]{2,1,0:T(8,128)(2,1)S(1)}, bf16[4,512,128]{2,1,0:T(8,128)(2,1)S(1)}, u32[]{:S(2)}, u32[]{:S(2)}) collective-permute-start(bf16[4,512,128]{2,1,0:T(8,128)(2,1)S(1)} %pad_maximum_fusion.1.refs_0_), channel_id=1, source_target_pairs={{0,1},{1,0},{2,3},{3,2},{4,5},{5,4},{6,7},{7,6},{8,9},{9,8},{10,11... | collective-permute-start | bytes 1572872 | tf_op jit(solution)/shard_map/ppermute | solution.py:578
  86.2 8.1 %collective-permute-start.25 = (bf16[4,400,128]{2,1,0:T(8,128)(2,1)S(1)}, bf16[4,400,128]{2,1,0:T(8,128)(2,1)S(1)}, u32[]{:S(2)}, u32[]{:S(2)}) collective-permute-start(bf16[4,400,128]{2,1,0:T(8,128)(2,1)S(1)} %pad_maximum_fusion.2.refs_0_), channel_id=1, source_target_pairs={{0,4},{1,3},{2,6},{3,1},{4,0},{5,7},{6,2},{7,5},{8,12},{9,11},{10,... | collective-permute-start | bytes 1228808 | tf_op jit(solution)/shard_map/ppermute | solution.py:578
  87.9 15.0 %collective-permute-start.30 = (bf16[4,640,128]{2,1,0:T(8,128)(2,1)S(1)}, bf16[4,640,128]{2,1,0:T(8,128)(2,1)S(1)}, u32[]{:S(2)}, u32[]{:S(2)}) collective-permute-start(bf16[4,640,128]{2,1,0:T(8,128)(2,1)S(1)} %pad_maximum_fusion.refs_0_), channel_id=1, source_target_pairs={{0,1},{1,0},{2,3},{3,2},{4,5},{5,4},{6,7},{7,6},{8,9},{9,8},{10,11... | collective-permute-start | bytes 1966088 | tf_op jit(solution)/shard_map/ppermute | solution.py:578
  89.4 13.5 %collective-permute-start.31 = (bf16[4,640,128]{2,1,0:T(8,128)(2,1)S(1)}, bf16[4,640,128]{2,1,0:T(8,128)(2,1)S(1)}, u32[]{:S(2)}, u32[]{:S(2)}) collective-permute-start(bf16[4,640,128]{2,1,0:T(8,128)(2,1)S(1)} %collective-permute-done.29.refs_1_), channel_id=1, source_target_pairs={{0,1},{1,0},{2,3},{3,2},{4,5},{5,4},{6,7},{7,6},{8,9},{9,8},{10,11... | collective-permute-start | bytes 1966088 | tf_op jit(solution)/shard_map/ppermute | solution.py:578
  (16 other events, 83.9 us)
